TPU v7x, 32 devices: a whole 2x2x4 slice. The times are simulated.
32 devices in a mesh: dp: 8 (over y, x, core), feat: 4 (over z).
Axes of the slice: x: 2, y: 2, z: 4, core: 2. Of those that a mesh axis runs over, the one named last changes fastest.
Arguments:
- tokens: bfloat16 [8192, 1024], P('dp'), may hold values from -6 to 6
- cotangent: bfloat16 [8192, 1024], P('dp'), may hold values from -6 to 6
- doc_starts: int32 [8, 8], P('dp'), may hold values from 0 to 1023, as said below
- queries_keys: float32 [1024, 512], P(None, 'feat'), may hold values from -0.1875 to 0.1875
- value_weight: float32 [1024, 1024], P(None, 'feat'), may hold values from -0.1875 to 0.1875
- out_weight: float32 [1024, 1024], P('feat'), may hold values from -1 to 1
- gate_up: float32 [2, 1024, 2752], P(None, None, 'feat'), may hold values from -0.1875 to 0.1875
- down_weight: float32 [2752, 1024], P('feat'), may hold values from -0.109375 to 0.109375
- norm_gains: float32 [2, 1024], replicated, may hold values from 0.5 to 1.5
- queries_moment: float32 [1024, 512], P(None, 'feat'), may hold values from -224 to 224
- value_moment: float32 [1024, 1024], P(None, 'feat'), may hold values from -224 to 224
- out_moment: float32 [1024, 1024], P('feat'), may hold values from -224 to 224
- gate_moment: float32 [2, 1024, 2752], P(None, None, 'feat'), may hold values from -224 to 224
- down_moment: float32 [2752, 1024], P('feat'), may hold values from -224 to 224
- gains_moment: float32 [2, 1024], replicated, may hold values from -512 to 512
- queries_average: float32 [1024, 512], P(None, 'feat'), may hold values from -0.1875 to 0.1875
- value_average: float32 [1024, 1024], P(None, 'feat'), may hold values from -0.1875 to 0.1875
- out_average: float32 [1024, 1024], P('feat'), may hold values from -1 to 1
- gate_average: float32 [2, 1024, 2752], P(None, None, 'feat'), may hold values from -0.1875 to 0.1875
- down_average: float32 [2752, 1024], P('feat'), may hold values from -0.109375 to 0.109375
- gains_average: float32 [2, 1024], replicated, may hold values from 0.5 to 1.5
Outputs:
- mixed: bfloat16 [8192, 1024], P('dp')
- input_gradient: float32 [8192, 1024], P('dp')
- queries_momentum: float32 [1024, 512], P(None, 'feat')
- queries_new: float32 [1024, 512], P(None, 'feat')
- queries_mean: float32 [1024, 512], P(None, 'feat')
- value_momentum: float32 [1024, 1024], P(None, 'feat')
- value_new: float32 [1024, 1024], P(None, 'feat')
- value_mean: float32 [1024, 1024], P(None, 'feat')
- out_momentum: float32 [1024, 1024], P('feat')
- out_new: float32 [1024, 1024], P('feat')
- out_mean: float32 [1024, 1024], P('feat')
- gate_momentum: float32 [2, 1024, 2752], P(None, None, 'feat')
- gate_new: float32 [2, 1024, 2752], P(None, None, 'feat')
- gate_mean: float32 [2, 1024, 2752], P(None, None, 'feat')
- down_momentum: float32 [2752, 1024], P('feat')
- down_new: float32 [2752, 1024], P('feat')
- down_mean: float32 [2752, 1024], P('feat')
- gains_momentum: float32 [2, 1024], replicated
- gains_new: float32 [2, 1024], replicated
- gains_mean: float32 [2, 1024], replicated
Inputs may be any that keep to these rules, and one draw needn't show every extreme that they name: `doc_starts`: each row's first start is 0, its last is 1023, and its 8 starts strictly increase.
All inputs are finite; a program needn't handle non-finite values.
Results may differ from a plain program's by a relative error of at most 0.015.
Values may be sent and summed in bfloat16 or wider, within the bound.
A program may use at most 256 MiB of HBM per device.

v0:
```python
import jax
import jax.numpy as jnp
from jax import lax
from jax.sharding import PartitionSpec as P

D = 1024
HEADS = 16
QK = 16
HV = 64
FF = 2752
STEP = 4


EPS = 1e-06
MOMENTUM = 0.9


def feature_map(pairs, features):
    lead = pairs.shape[:-1]
    outer = (pairs[..., :, None] * pairs[..., None, :]).reshape(lead + (QK * QK,)) * 0.5**0.5
    ones = jnp.ones(lead + (1,), jnp.float32)
    zeros = jnp.zeros(lead + (features - 1 - QK - QK * QK,), jnp.float32)
    return jnp.concatenate([ones, pairs, outer, zeros], axis=-1)


def doc_mask(starts_row, count):
    position = jnp.arange(count, dtype=jnp.int32)
    document = jnp.sum((starts_row[None, :] <= position[:, None]).astype(jnp.int32), axis=1)
    same = document[:, None] == document[None, :]
    causal = position[None, :] <= position[:, None]
    return jnp.logical_and(same, causal)


def update(weight, grad_total, moment, average, rate):
    moment_next = MOMENTUM * moment + grad_total
    weight_next = weight - rate * (grad_total + MOMENTUM * moment_next)
    average_next = average + (weight_next - average) / STEP
    return (moment_next, weight_next, average_next)


def on_device(
    tokens,
    cotangent,
    doc_starts,
    queries_keys,
    value_weight,
    out_weight,
    gate_up,
    down_weight,
    norm_gains,
    queries_moment,
    value_moment,
    out_moment,
    gate_moment,
    down_moment,
    gains_moment,
    queries_average,
    value_average,
    out_average,
    gate_average,
    down_average,
    gains_average,
):
    groups = lax.axis_size("feat")
    length = tokens.shape[0]
    total_tokens = float(length * lax.axis_size("dp"))
    features = (1 + QK + QK * QK + groups - 1) // groups * groups
    group_size = features // groups
    half = HEADS * QK
    own_heads = HEADS // groups
    keep = doc_mask(doc_starts[0], length)
    keep_float = keep.astype(jnp.float32)
    keep_low = keep.astype(jnp.bfloat16)
    pairs_low = queries_keys.astype(jnp.bfloat16)
    value_low = value_weight.astype(jnp.bfloat16)
    out_low = out_weight.astype(jnp.bfloat16)
    gate_low = gate_up.astype(jnp.bfloat16)
    down_low = down_weight.astype(jnp.bfloat16)
    inputs = tokens.astype(jnp.float32)
    scale_one = lax.rsqrt(jnp.mean(inputs * inputs, axis=1, keepdims=True) + EPS)
    unit_one = inputs * scale_one
    normed_one = (unit_one * norm_gains[0]).astype(jnp.bfloat16)
    pairs_part = jnp.dot(normed_one, pairs_low, preferred_element_type=jnp.float32).astype(
        jnp.bfloat16
    )
    value_part = jnp.dot(normed_one, value_low, preferred_element_type=jnp.float32).astype(
        jnp.bfloat16
    )
    pair_cols = pairs_part.shape[1]
    pairs_all = lax.all_gather(pairs_part, "feat", axis=1, tiled=True)
    head_start = lax.axis_index("feat") * own_heads * QK
    query_cols = lax.dynamic_slice_in_dim(pairs_all, head_start, own_heads * QK, 1)
    key_cols = lax.dynamic_slice_in_dim(pairs_all, half + head_start, own_heads * QK, 1)
    value_heads = value_part.reshape(length, own_heads, HV)

    def whole_features(pairs):
        return feature_map(pairs.reshape(length, own_heads, QK) * 0.5, features)

    query_feats, query_pull = jax.vjp(whole_features, query_cols.astype(jnp.float32))
    key_feats, key_pull = jax.vjp(whole_features, key_cols.astype(jnp.float32))
    query_low = query_feats.astype(jnp.bfloat16)
    key_low = key_feats.astype(jnp.bfloat16)
    numer_sum = jnp.zeros((length, own_heads, HV), jnp.float32)
    denom_own = jnp.zeros((length, own_heads), jnp.float32)
    group_scores = []
    for group in range(groups):
        lower = group * group_size
        scores = (
            jnp.einsum(
                "thf,shf->hts",
                query_low[:, :, lower : lower + group_size],
                key_low[:, :, lower : lower + group_size],
                preferred_element_type=jnp.float32,
            )
            * keep_float[None]
        )
        scores_low = scores.astype(jnp.bfloat16)
        group_scores.append(scores_low)
        numer_sum = numer_sum + jnp.einsum(
            "hts,shc->thc", scores_low, value_heads, preferred_element_type=jnp.float32
        )
        denom_own = denom_own + jnp.sum(scores, axis=2).T
    numer_own = numer_sum.reshape(length, own_heads * HV)
    attn_heads = numer_own.reshape(length, own_heads, HV) / denom_own[:, :, None]
    attn_low = attn_heads.reshape(length, own_heads * HV).astype(jnp.bfloat16)
    attended = lax.psum(jnp.dot(attn_low, out_low, preferred_element_type=jnp.float32), "feat")
    hidden_one = inputs + attended
    scale_two = lax.rsqrt(jnp.mean(hidden_one * hidden_one, axis=1, keepdims=True) + EPS)
    unit_two = hidden_one * scale_two
    normed_two = (unit_two * norm_gains[1]).astype(jnp.bfloat16)
    gate_value = jnp.dot(normed_two, gate_low[0], preferred_element_type=jnp.float32)
    up_value = jnp.dot(normed_two, gate_low[1], preferred_element_type=jnp.float32)
    activated = jax.nn.silu(gate_value)
    hidden_low = (activated * up_value).astype(jnp.bfloat16)
    ffn_out = lax.psum(
        jnp.dot(hidden_low, down_low, preferred_element_type=jnp.float32).astype(jnp.bfloat16),
        "feat",
    ).astype(jnp.float32)
    mixed = (hidden_one + ffn_out).astype(jnp.bfloat16)
    grad_down = jnp.einsum("tf,td->fd", hidden_low, cotangent, preferred_element_type=jnp.float32)
    grad_hidden_units = jnp.einsum(
        "td,fd->tf", cotangent, down_low, preferred_element_type=jnp.float32
    )
    sigmoid_gate = jax.nn.sigmoid(gate_value)
    slope = sigmoid_gate * (1.0 + gate_value * (1.0 - sigmoid_gate))
    grad_gate = (grad_hidden_units * up_value * slope).astype(jnp.bfloat16)
    grad_up = (grad_hidden_units * activated).astype(jnp.bfloat16)
    grad_gate_up = jnp.stack(
        [
            jnp.einsum("td,tf->df", normed_two, grad_gate, preferred_element_type=jnp.float32),
            jnp.einsum("td,tf->df", normed_two, grad_up, preferred_element_type=jnp.float32),
        ]
    )
    normed_two_part = jnp.einsum(
        "tf,df->td", grad_gate, gate_low[0], preferred_element_type=jnp.float32
    ) + jnp.einsum("tf,df->td", grad_up, gate_low[1], preferred_element_type=jnp.float32)
    grad_normed_two = lax.psum(normed_two_part.astype(jnp.bfloat16), "feat").astype(jnp.float32)
    gain_two = jnp.sum(grad_normed_two * unit_two, axis=0)
    grad_unit_two = grad_normed_two * norm_gains[1]
    grad_hidden = cotangent.astype(jnp.float32) + scale_two * (
        grad_unit_two - unit_two * jnp.mean(grad_unit_two * unit_two, axis=1, keepdims=True)
    )
    grad_attended = grad_hidden.astype(jnp.bfloat16)
    grad_out = jnp.einsum("tv,td->vd", attn_low, grad_attended, preferred_element_type=jnp.float32)
    grad_attn = jnp.einsum(
        "td,vd->tv", grad_attended, out_low, preferred_element_type=jnp.float32
    ).reshape(length, own_heads, HV)
    grad_numer = (
        (grad_attn / denom_own[:, :, None]).reshape(length, own_heads * HV).astype(jnp.bfloat16)
    )
    grad_denom = (-jnp.sum(grad_attn * attn_heads, axis=2) / denom_own).astype(jnp.bfloat16)
    numer_back = grad_numer.reshape(length, own_heads, HV)
    grad_scores = (
        jnp.einsum("thc,shc->hts", numer_back, value_heads, preferred_element_type=jnp.float32)
        + grad_denom.T.astype(jnp.float32)[:, :, None]
    )
    grad_scores_low = grad_scores.astype(jnp.bfloat16) * keep_low[None]
    grad_query_feats = jnp.einsum(
        "hts,shf->thf", grad_scores_low, key_low, preferred_element_type=jnp.float32
    )
    grad_key_feats = jnp.einsum(
        "hts,thf->shf", grad_scores_low, query_low, preferred_element_type=jnp.float32
    )
    value_grad_sum = jnp.zeros((length, own_heads, HV), jnp.float32)
    for group in range(groups):
        value_grad_sum = value_grad_sum + jnp.einsum(
            "hts,thc->shc", group_scores[group], numer_back, preferred_element_type=jnp.float32
        )
    grad_query = query_pull(grad_query_feats)[0]
    grad_key = key_pull(grad_key_feats)[0]
    own_back = jnp.concatenate([grad_query, grad_key], axis=1).astype(jnp.bfloat16)
    gathered = lax.all_gather(own_back, "feat", axis=1, tiled=True)
    reordered = (
        gathered.reshape(length, groups, 2, own_heads * QK)
        .transpose(0, 2, 1, 3)
        .reshape(length, 2 * half)
    )
    pairs_back_low = lax.dynamic_slice_in_dim(
        reordered, lax.axis_index("feat") * pair_cols, pair_cols, 1
    )
    value_back_low = value_grad_sum.reshape(length, own_heads * HV).astype(jnp.bfloat16)
    grad_pairs = jnp.einsum(
        "td,tq->dq", normed_one, pairs_back_low, preferred_element_type=jnp.float32
    )
    grad_value = jnp.einsum(
        "td,tv->dv", normed_one, value_back_low, preferred_element_type=jnp.float32
    )
    normed_one_part = jnp.einsum(
        "tq,dq->td", pairs_back_low, pairs_low, preferred_element_type=jnp.float32
    ) + jnp.einsum("tv,dv->td", value_back_low, value_low, preferred_element_type=jnp.float32)
    grad_normed_one = lax.psum(normed_one_part.astype(jnp.bfloat16), "feat").astype(jnp.float32)
    gain_one = jnp.sum(grad_normed_one * unit_one, axis=0)
    grad_unit_one = grad_normed_one * norm_gains[0]
    input_gradient = grad_hidden + scale_one * (
        grad_unit_one - unit_one * jnp.mean(grad_unit_one * unit_one, axis=1, keepdims=True)
    )
    grad_pairs, grad_value, grad_out, grad_gate_up, grad_down, gain_one, gain_two = lax.psum(
        (grad_pairs, grad_value, grad_out, grad_gate_up, grad_down, gain_one, gain_two), "dp"
    )
    grad_gains = jnp.stack([gain_one, gain_two])
    first = update(
        queries_keys, grad_pairs, queries_moment, queries_average, (D * total_tokens) ** (-0.5)
    )
    second = update(
        value_weight, grad_value, value_moment, value_average, (D * total_tokens) ** (-0.5)
    )
    third = update(
        out_weight, grad_out, out_moment, out_average, (HEADS * HV * total_tokens) ** (-0.5)
    )
    fourth = update(gate_up, grad_gate_up, gate_moment, gate_average, (D * total_tokens) ** (-0.5))
    fifth = update(down_weight, grad_down, down_moment, down_average, (FF * total_tokens) ** (-0.5))
    sixth = update(
        norm_gains, grad_gains, gains_moment, gains_average, 0.2 * total_tokens ** (-0.5)
    )
    return (
        mixed,
        input_gradient,
        first[0],
        first[1],
        first[2],
        second[0],
        second[1],
        second[2],
        third[0],
        third[1],
        third[2],
        fourth[0],
        fourth[1],
        fourth[2],
        fifth[0],
        fifth[1],
        fifth[2],
        sixth[0],
        sixth[1],
        sixth[2],
    )


def solution(mesh):
    in_specs = (
        P("dp", None),
        P("dp", None),
        P("dp", None),
        P(None, "feat"),
        P(None, "feat"),
        P("feat", None),
        P(None, None, "feat"),
        P("feat", None),
        P(),
        P(None, "feat"),
        P(None, "feat"),
        P("feat", None),
        P(None, None, "feat"),
        P("feat", None),
        P(),
        P(None, "feat"),
        P(None, "feat"),
        P("feat", None),
        P(None, None, "feat"),
        P("feat", None),
        P(),
    )
    out_specs = (
        P("dp", None),
        P("dp", None),
        P(None, "feat"),
        P(None, "feat"),
        P(None, "feat"),
        P(None, "feat"),
        P(None, "feat"),
        P(None, "feat"),
        P("feat", None),
        P("feat", None),
        P("feat", None),
        P(None, None, "feat"),
        P(None, None, "feat"),
        P(None, None, "feat"),
        P("feat", None),
        P("feat", None),
        P("feat", None),
        P(),
        P(),
        P(),
    )
    return jax.shard_map(
        on_device, mesh=mesh, in_specs=in_specs, out_specs=out_specs, check_vma=False
    )
```

profile of v0, /device:TPU:0, one launch (start us, length us, event | category | flops | bytes accessed | tf_op | source)
XLA Modules:
  0.0 848.6 jit_solution(9565755110201909743)
XLA Ops:
  19.5 25.2 %all-gather.3.cloned.1.call-done = bf16[1024,512]{0,1:T(8,128)(2,1)} async-done(((bf16[1024,128]{0,1:T(8,128)(2,1)}), bf16[1024,512]{0,1:T(8,128)(2,1)}) %all-gather.3.cloned.1.call-update) | async-done | bytes 1048592 | tf_op jit(solution)/shard_map/all_gather | solution.py:90
  47.0 8.1 fusion.70
  55.1 8.1 fusion.71
  63.3 8.1 fusion.66
  71.4 8.4 fusion.56
  79.9 24.5 %multiply_reduce_fusion.2 = (f32[4,1024]{1,0:T(4,128)S(1)}, f32[4,1024]{1,0:T(4,128)S(1)}, f32[4,1024]{1,0:T(4,128)S(1)}, f32[4,1024]{1,0:T(4,128)S(1)}, f32[4,1024,1024]{1,2,0:T(8,128)}) fusion(f32[1024,1024]{0,1:T(8,128)S(1)} %copy-done, f32[4,1024,1024]{1,2,0:T(8,128)} %fusion.70, f32[4,1024,1024]{1,2,0:T(8,128)} %fusion.71, ...), kind=kOutput, calls=%fused_computation.5 | convolution fusion | flops 612352000 | bytes 72548352 | tf_op jit(solution)/shard_map/thf,shf->hts/dot_general | solution.py:109
  104.4 8.5 convolution_add_fusion.5
  112.9 8.5 convolution_add_fusion.4
  121.4 9.5 %fusion.107 = (bf16[1024,4,64]{0,2,1:T(8,128)(2,1)S(1)}, f32[1024,4,64]{0,2,1:T(8,128)}) fusion(f32[1024,4]{0,1:T(4,128)S(1)} %bitcast.127, f32[4,64,1024]{2,1,0:T(8,128)S(1)} %convolution_add_fusion.4, bf16[1024,4,64]{0,2,1:T(8,128)(2,1)S(1)} %bitcast.103, f32[4,1024,1024]{1,2,0:T(8,128)} %fusion.70, f32[1024,1024]{0,1:T(8,128)S(1)} %copy-done), kind=kOutput, calls=%fused_computation.184 | convolution fusion | flops 546045952 | bytes 24133632 | tf_op jit(solution)/shard_map/hts,shc->thc/dot_general | solution.py:119
  139.3 149.8 %all-reduce.10.cloned.1.call-done = f32[1024,1024]{1,0:T(8,128)} async-done(((f32[1024,1024]{1,0:T(8,128)}), f32[1024,1024]{1,0:T(8,128)}) %all-reduce.10.cloned.1.call-update) | async-done | bytes 4194320 | tf_op jit(solution)/shard_map/psum | solution.py:126
  312.5 5.6 convolution_convert_fusion
  318.0 76.0 %all-reduce.12.cloned.1.call-done = bf16[1024,1024]{1,0:T(8,128)(2,1)} async-done(((bf16[1024,1024]{1,0:T(8,128)(2,1)}), bf16[1024,1024]{1,0:T(8,128)(2,1)}) %all-reduce.12.cloned.1.call-update) | async-done | bytes 2097168 | tf_op jit(solution)/shard_map/psum | solution.py:157
  405.6 9.0 %fusion.55 = f32[4,64,1024]{2,1,0:T(8,128)S(1)} fusion(bf16[1024,4,64]{0,2,1:T(8,128)(2,1)S(1)} %bitcast.105, f32[4,1024,1024]{1,2,0:T(8,128)} %fusion.66, f32[1024,1024]{0,1:T(8,128)S(1)} %copy-done.1), kind=kOutput, calls=%fused_computation.102 | convolution fusion | flops 545259520 | bytes 22544384 | tf_op jit(solution)/shard_map/hts,thc->shc/dot_general | solution.py:186
  419.8 9.6 %fusion.37 = f32[1024,4,276]{0,2,1:T(8,128)} fusion(bf16[4,1024,1024]{2,1,0:T(8,128)(2,1)} %add_convert_fusion, bf16[1024,1024]{1,0:T(8,128)(2,1)} %copy.96, bf16[1024,4,1]{0,2,1:T(2,128)(2,1)S(1)} %broadcast.172, bf16[1024,4,256]{0,2,1:T(8,128)(2,1)} %bitcast.99, bf16[1024,4,16]{0,2,1:T(8,128)(2,1)S(1)} %get-tuple-element.65, bf16[276]{0:T(512)(128)(2,1)S(1)} %pad.15.clone), kind=kOutput, calls=%fused_computation.77 | convolution fusion | flops 2328494080 | bytes 17244712 | tf_op jit(solution)/shard_map/hts,shf->thf/dot_general | solution.py:178
  429.5 8.8 %fusion.42 = f32[1024,4,276]{0,2,1:T(8,128)} fusion(bf16[4,1024,1024]{2,1,0:T(8,128)(2,1)} %add_convert_fusion, bf16[1024,1024]{1,0:T(8,128)(2,1)} %copy.96, bf16[1024,4,1]{0,2,1:T(2,128)(2,1)S(1)} %broadcast.172, bf16[1024,4,256]{0,2,1:T(8,128)(2,1)S(1)} %bitcast.94, bf16[1024,4,16]{0,2,1:T(8,128)(2,1)S(1)} %get-tuple-element.64, ...), kind=kOutput, calls=%fused_computation.78 | convolution fusion | flops 2328494080 | bytes 17244712 | tf_op jit(solution)/shard_map/hts,thf->shf/dot_general | solution.py:181
  438.3 10.0 %convolution_add_fusion.2 = f32[4,64,1024]{2,1,0:T(8,128)} fusion(f32[4,64,1024]{2,1,0:T(8,128)S(1)} %fusion.55, bf16[1024,4,64]{0,2,1:T(8,128)(2,1)S(1)} %bitcast.107, f32[4,1024,1024]{1,2,0:T(8,128)} %get-tuple-element.72, f32[1024,1024]{0,1:T(8,128)S(1)} %copy-done.1), kind=kOutput, calls=%fused_computation.88 | convolution fusion | flops 545521664 | bytes 23592960 | tf_op jit(solution)/shard_map/hts,thc->shc/dot_general | solution.py:186
  462.0 10.3 %convolution_add_fusion.1 = f32[4,64,1024]{2,1,0:T(8,128)S(1)} fusion(f32[4,64,1024]{2,1,0:T(8,128)} %convolution_add_fusion.2, bf16[1024,4,64]{0,2,1:T(8,128)(2,1)S(1)} %bitcast.108, f32[4,1024,1024]{1,2,0:T(8,128)} %fusion.71, f32[1024,1024]{0,1:T(8,128)} %get-tuple-element.71), kind=kOutput, calls=%fused_computation.87 | convolution fusion | flops 545521664 | bytes 23592960 | tf_op jit(solution)/shard_map/hts,thc->shc/dot_general | solution.py:186
  472.4 9.9 %fusion.49 = bf16[4,64,1024]{2,1,0:T(8,128)(2,1)} fusion(f32[4,64,1024]{2,1,0:T(8,128)S(1)} %convolution_add_fusion.1, bf16[1024,4,64]{0,2,1:T(8,128)(2,1)S(1)} %bitcast.109, f32[4,1024,1024]{1,2,0:T(8,128)} %fusion.70, f32[1024,1024]{0,1:T(8,128)S(1)} %copy-done.2), kind=kOutput, calls=%fused_computation.95 | convolution fusion | flops 545783808 | bytes 23068672 | tf_op jit(solution)/shard_map/hts,thc->shc/dot_general | solution.py:186
  482.2 6.8 all-gather.5.cloned.1.call-done
  514.5 135.8 %all-reduce.16.cloned.1.call-done = (bf16[1024,1024]{1,0:T(8,128)(2,1)}, bf16[1024,1024]{1,0:T(8,128)(2,1)}) async-done(((bf16[1024,1024]{1,0:T(8,128)(2,1)}, bf16[1024,1024]{1,0:T(8,128)(2,1)}), (bf16[1024,1024]{1,0:T(8,128)(2,1)}, bf16[1024,1024]{1,0:T(8,128)(2,1)})) %all-reduce.16.cloned.1.call-update) | async-done | bytes 4194320 | tf_op jit(solution)/shard_map/psum | solution.py:135
  653.3 14.4 %all-reduce.2 = (f32[1,1024]{1,0:T(1,128)S(1)}, f32[1,1024]{1,0:T(1,128)S(1)}) all-reduce(f32[1,1024]{1,0:T(1,128)S(1)} %bitcast.135, f32[1,1024]{1,0:T(1,128)S(1)} %bitcast.136), channel_id=1, replica_groups=mesh['dp'=8,'feat'=4] {'dp'}, use_global_device_ids=true, to_apply=%region_26.27 | all-reduce | flops 2048 | bytes 16384 | tf_op jit(solution)/shard_map/psum | solution.py:217
  668.5 5.2 add_convert_fusion.3
  676.4 136.8 %all-reduce.14.cloned.1.call-done = (f32[1024,128]{1,0:T(8,128)}, f32[1024,256]{1,0:T(8,128)}, f32[256,1024]{1,0:T(8,128)}, f32[2,1024,688]{1,2,0:T(8,128)}, f32[688,1024]{1,0:T(8,128)}) async-done(((f32[1024,128]{1,0:T(8,128)}, f32[1024,256]{1,0:T(8,128)}, f32[256,1024]{1,0:T(8,128)}, f32[2,1024,688]{1,2,0:T(8,128)}, f32[688,1024]{1,0:T(8,128)}), (f32[1024,128]{1,0:T(8,128)}, f32[1024,256]{1,0:T(8,128)}, ...) | async-done | bytes 11075600 | tf_op jit(solution)/shard_map/psum | solution.py:217
  813.3 14.7 %multiply_add_fusion = (f32[2,1024,688]{1,2,0:T(8,128)}, f32[2,1024,688]{1,2,0:T(8,128)}, f32[2,1024,688]{1,2,0:T(8,128)}) fusion(f32[2,1024,688]{1,2,0:T(8,128)} %param.39, f32[2,1024,688]{1,2,0:T(8,128)} %param.27, f32[2,1024,688]{1,2,0:T(8,128)} %get-tuple-element.37, f32[2,1024,688]{1,2,0:T(8,128)} %param.33), kind=kLoop, calls=%fused_computation.21 | loop fusion | flops 12681216 | bytes 39452672 | tf_op jit(solution)/shard_map/add | solution.py:37
  (199 shorter events, 121.6 us)
Async XLA Ops:
  7.2 37.5 %all-gather.3.cloned.1.call-start = ((), (), s32[]{:S(2)}) async-start(), calls=%async_computation | async-start | bytes 1310720 | tf_op jit(solution)/shard_map/all_gather | solution.py:90
  13.9 275.2 %all-reduce.10.cloned.1.call-start = ((), (), s32[]{:S(2)}) async-start(), calls=%async_computation.1 | async-start | bytes 8388608 | tf_op jit(solution)/shard_map/psum | solution.py:126
  45.7 9.4 %copy-start.20 = (f32[1024,64]{0,1:T(8,128)}, f32[1024,64]{0,1:T(8,128)S(1)}, u32[]{:S(2)}) copy-start(f32[1024,64]{0,1:T(8,128)S(1)} %get-tuple-element.66) | copy-start | bytes 786436
  46.3 33.6 %copy-start.11 = (bf16[1024,4,16,16]{0,3,2,1:T(8,128)(2,1)}, bf16[1024,4,16,16]{0,3,2,1:T(8,128)(2,1)S(1)}, u32[]{:S(2)}) copy-start(bf16[1024,4,16,16]{0,3,2,1:T(8,128)(2,1)S(1)} %multiply_convert_fusion.6) | copy-start | bytes 6291460
  47.0 32.9 %copy-start.13 = (bf16[1024,4,16,16]{0,3,2,1:T(8,128)(2,1)}, bf16[1024,4,16,16]{0,3,2,1:T(8,128)(2,1)S(1)}, u32[]{:S(2)}) copy-start(bf16[1024,4,16,16]{0,3,2,1:T(8,128)(2,1)S(1)} %multiply_convert_fusion.5) | copy-start | bytes 6291460
  121.3 10.3 %copy-start.15 = (f32[256,1024]{1,0:T(8,128)S(1)}, f32[256,1024]{1,0:T(8,128)}, u32[]{:S(2)}) copy-start(f32[256,1024]{1,0:T(8,128)} %param.26) | copy-start | bytes 3145732
  134.5 154.6 %copy-start.10 = (bf16[1024,1024]{1,0:T(8,128)(2,1)S(1)}, bf16[1024,1024]{1,0:T(8,128)(2,1)}, u32[]{:S(2)}) copy-start(bf16[1024,1024]{1,0:T(8,128)(2,1)} %param.21) | copy-start | bytes 6291460
  134.5 259.5 %all-reduce.12.cloned.1.call-start = ((), (), s32[]{:S(2)}) async-start(), calls=%async_computation.2 | async-start | bytes 4194304 | tf_op jit(solution)/shard_map/psum | solution.py:157
  308.4 180.6 %all-gather.5.cloned.1.call-start = ((), (), s32[]{:S(2)}) async-start(), calls=%async_computation.3 | async-start | bytes 1310720 | tf_op jit(solution)/shard_map/all_gather | solution.py:192
  405.6 9.0 %copy-start.30 = (f32[1024,4,64]{0,2,1:T(8,128)S(1)}, f32[1024,4,64]{0,2,1:T(8,128)}, u32[]{:S(2)}) copy-start(f32[1024,4,64]{0,2,1:T(8,128)} %get-tuple-element.74) | copy-start | bytes 3145732
  419.8 9.6 %copy-start.12 = (bf16[1024,4,16,16]{0,3,2,1:T(8,128)(2,1)S(1)}, bf16[1024,4,16,16]{0,3,2,1:T(8,128)(2,1)}, u32[]{:S(2)}) copy-start(bf16[1024,4,16,16]{0,3,2,1:T(8,128)(2,1)} %copy-done.11) | copy-start | bytes 6291460
  462.0 188.3 %all-reduce.16.cloned.1.call-start = ((), (), s32[]{:S(2)}) async-start(), calls=%async_computation.5 | async-start | bytes 8388608 | tf_op jit(solution)/shard_map/psum | solution.py:135
  462.0 10.3 %copy-start.2 = (f32[1024,1024]{0,1:T(8,128)S(1)}, f32[1024,1024]{0,1:T(8,128)}, u32[]{:S(2)}) copy-start(f32[1024,1024]{0,1:T(8,128)} %get-tuple-element.71) | copy-start | bytes 12582916
  482.2 10.9 %copy-start.14 = (f32[1024,256]{1,0:T(8,128)S(1)}, f32[1024,256]{1,0:T(8,128)}, u32[]{:S(2)}) copy-start(f32[1024,256]{1,0:T(8,128)} %param.25) | copy-start | bytes 3145732
  495.3 317.9 %all-reduce.14.cloned.1.call-start = ((), (), s32[]{:S(2)}) async-start(), calls=%async_computation.4 | async-start | bytes 22151168 | tf_op jit(solution)/shard_map/psum | solution.py:217
  514.5 135.9 %copy-start.51 = (f32[1024]{0:T(1024)S(1)}, f32[1024]{0:T(1024)}, u32[]{:S(2)}) copy-start(f32[1024]{0:T(1024)} %copy-done.50) | copy-start | bytes 12292
  514.5 135.9 %copy-start.53 = (f32[1,1024]{1,0:T(1,128)S(1)}, f32[1,1024]{1,0:T(1,128)}, u32[]{:S(2)}) copy-start(f32[1,1024]{1,0:T(1,128)} %copy-done.52) | copy-start | bytes 12292
  514.5 153.3 %copy-start.54 = (f32[2,1024]{1,0:T(2,128)S(1)}, f32[2,1024]{1,0:T(2,128)}, u32[]{:S(2)}) copy-start(f32[2,1024]{1,0:T(2,128)} %param.29) | copy-start | bytes 24580
  514.5 153.3 %copy-start.55 = (f32[2,1024]{1,0:T(2,128)S(1)}, f32[2,1024]{1,0:T(2,128)}, u32[]{:S(2)}) copy-start(f32[2,1024]{1,0:T(2,128)} %param.41) | copy-start | bytes 24580
  514.5 153.3 %copy-start.56 = (f32[2,1024]{1,0:T(2,128)S(1)}, f32[2,1024]{1,0:T(2,128)}, u32[]{:S(2)}) copy-start(f32[2,1024]{1,0:T(2,128)} %param.35) | copy-start | bytes 24580
  813.3 14.8 %copy-start.32 = (f32[688,1024]{1,0:T(8,128)S(1)}, f32[688,1024]{1,0:T(8,128)}, u32[]{:S(2)}) copy-start(f32[688,1024]{1,0:T(8,128)} %param.28) | copy-start | bytes 8454148
  813.3 14.8 %copy-start.33 = (f32[688,1024]{1,0:T(8,128)S(1)}, f32[688,1024]{1,0:T(8,128)}, u32[]{:S(2)}) copy-start(f32[688,1024]{1,0:T(8,128)} %param.40) | copy-start | bytes 8454148
  813.3 15.9 %copy-start.34 = (f32[688,1024]{1,0:T(8,128)S(1)}, f32[688,1024]{1,0:T(8,128)}, u32[]{:S(2)}) copy-start(f32[688,1024]{1,0:T(8,128)} %param.34) | copy-start | bytes 8454148
  813.3 16.7 %copy-start.35 = (f32[688,1024]{1,0:T(8,128)S(1)}, f32[688,1024]{1,0:T(8,128)}, u32[]{:S(2)}) copy-start(f32[688,1024]{1,0:T(8,128)} %get-tuple-element.38) | copy-start | bytes 8454148
  (46 other events, 159.8 us)
Sparse Core Ops, SparseCore 0:
  14.0 30.6 all-gather.2
  134.6 154.4 all-reduce.9
  308.5 85.4 all-reduce.11
  462.1 26.8 all-gather.4
  495.4 154.8 all-reduce.15
  656.4 156.7 all-reduce.13
where the time goes:
time: 859 us; the launch traced here: 849 us
  waiting for transfers between devices  530 us (62%)
  matrix products  190 us (22%)
  other arithmetic  79.2 us (9%)
  local copies, waits for them, and re-layouts  19.2 us (2%)
  between operations  15.1 us (2%)
  blocking collectives  14.4 us (2%)
    psum x1, waiting for transfers between devices, on_device(): lax.psum(jnp.dot(attn_low, out_low, preferred_element_type=jnp.float32),...  150 us
    psum x1, waiting for transfers between devices, on_device(): lax.psum((grad_pairs, grad_value, grad_out, grad_gate_up, grad_down, gain...  137 us
    psum x1, waiting for transfers between devices, on_device(): lax.psum(jnp.dot(hidden_low, down_low, preferred_element_type=jnp.float32...  136 us
    psum x1, waiting for transfers between devices, on_device(): lax.psum(normed_two_part.astype(jnp.bfloat16), 'feat').astype(jnp.float32)  76 us
    dot_general x4, matrix products, on_device(): jnp.einsum('thf,shf->hts', query_low[:, :, lower:lower + group_size], key...  48.9 us
    dot_general x4, matrix products, on_device(): jnp.einsum('hts,thc->shc', group_scores[group], numer_back, preferred_ele...  39.2 us
    dot_general x4, matrix products, on_device(): jnp.einsum('hts,shc->thc', scores_low, value_heads, preferred_element_typ...  34.9 us
    add x6, other arithmetic, update(): average_next = average + (weight_next - average) / STEP  26.5 us
  transfers between devices with their start and end apart: 6, of which 6 were waited for; matrix products, arithmetic and copies ran while one was open for 8% of the time, Pallas kernels for 0%

commit v1 on v0

v1 whole, which is shorter than its diff:
```python
import functools
import jax
import jax.numpy as jnp
from jax import lax
from jax.experimental import pallas as pl
from jax.experimental.pallas import tpu as pltpu
from jax.sharding import PartitionSpec as P

D = 1024
HEADS = 16
QK = 16
HV = 64
FF = 2752
STEP = 4
BT = 256
F32 = jnp.float32
BF16 = jnp.bfloat16

EPS = 1e-06
MOMENTUM = 0.9


def nt(a, b):
    return lax.dot_general(a, b, (((1,), (1,)), ((), ())), preferred_element_type=F32)


def nn(a, b):
    return lax.dot_general(a, b, (((1,), (0,)), ((), ())), preferred_element_type=F32)


def first_start(starts_ref, t):
    begin = jnp.int32(0)
    for n in range(starts_ref.shape[1]):
        begin = jnp.where(starts_ref[0, n] <= t, jnp.maximum(begin, starts_ref[0, n]), begin)
    return begin


def fill_mask(starts_ref, mask_ref, block, low_block):
    t = block * BT + lax.broadcasted_iota(jnp.int32, (BT, 1), 0)
    begin = jnp.zeros((BT, 1), jnp.int32)
    for n in range(starts_ref.shape[1]):
        begin = jnp.where(starts_ref[0, n] <= t, jnp.maximum(begin, starts_ref[0, n]), begin)

    def one(j, carry):
        s = j * BT + lax.broadcasted_iota(jnp.int32, (BT, BT), 1)
        keep = jnp.logical_and(s <= t, s >= begin)
        mask_ref[j] = keep.astype(F32).astype(BF16)
        return carry
    lax.fori_loop(low_block, block + 1, one, 0)


def attn_fwd_kernel(hb, starts_ref, q_ref, k_ref, v_ref, o_ref, rd_ref, mask_ref):
    block = pl.program_id(0)
    low_block = first_start(starts_ref, block * BT) // BT
    fill_mask(starts_ref, mask_ref, block, low_block)
    lane = lax.broadcasted_iota(jnp.int32, (1, 128), 1)

    def group(g, carry):
        qlanes = pl.ds(pl.multiple_of((g * hb) // 8 * 128, 128), 128)
        q = q_ref[:, qlanes]
        qms = []
        for n in range(hb):
            h8 = lax.rem(g * hb + n, 8)
            qms.append(jnp.where(lane // QK == h8, q, jnp.zeros_like(q)))

        def step(j, accs):
            rows = pl.ds(pl.multiple_of(j * BT, BT), BT)
            k = k_ref[rows, qlanes]
            mask = mask_ref[j]
            out = []
            for n in range(hb):
                vl = pl.ds(pl.multiple_of((g * hb + n) // 2 * 128, 128), 128)
                v = v_ref[rows, vl]
                v = jnp.where(lane // HV == n % 2, v, jnp.ones_like(v))
                t1 = nt(qms[n], k) + 1.0
                p = (t1 * t1 + 1.0).astype(BF16) * mask
                out.append(accs[n] + nn(p, v))
            return tuple(out)
        accs = lax.fori_loop(low_block, block + 1, step, tuple(jnp.zeros((BT, 128), F32) for _ in range(hb)))
        for m in range(hb // 2):
            vl = pl.ds(pl.multiple_of((g * hb + 2 * m) // 2 * 128, 128), 128)
            first, second = accs[2 * m], accs[2 * m + 1]
            numer = jnp.where(lane < HV, first, second)
            denom = pltpu.roll(jnp.where(lane < HV, second, first), HV, 1)
            recip = 1.0 / denom
            o_ref[:, vl] = (numer * recip).astype(BF16)
            rd_ref[:, vl] = recip
        return carry
    lax.fori_loop(0, HEADS // hb, group, 0)


def attn_fwd(starts, q, k, v, hb=4):
    length = q.shape[0]
    return pl.pallas_call(
        functools.partial(attn_fwd_kernel, hb),
        grid=(length // BT,),
        out_shape=(jax.ShapeDtypeStruct((length, HEADS * HV), BF16), jax.ShapeDtypeStruct((length, HEADS * HV), F32)),
        in_specs=[pl.BlockSpec(memory_space=pltpu.SMEM), pl.BlockSpec((BT, HEADS * QK), lambda i: (i, 0)),
                  pl.BlockSpec((length, HEADS * QK), lambda i: (0, 0)), pl.BlockSpec((length, HEADS * HV), lambda i: (0, 0))],
        out_specs=(pl.BlockSpec((BT, HEADS * HV), lambda i: (i, 0)), pl.BlockSpec((BT, HEADS * HV), lambda i: (i, 0))),
        scratch_shapes=[pltpu.VMEM((length // BT, BT, BT), BF16)],
        compiler_params=pltpu.CompilerParams(vmem_limit_bytes=40 * 2**20),
    )(starts, q, k, v)


def attn_bwd_kernel(
    hb, starts_ref, q_ref, k_ref, v_ref, attn_ref, rd_ref, ga_ref, out_w_ref,
    gq_ref, gk_ref, gv_ref, mask_ref, gn_ref, gd_ref, qt_ref, gnt_ref, gkt_ref, gvt_ref,
):
    block = pl.program_id(0)

    @pl.when(block == 0)
    def _():
        gkt_ref[...] = jnp.zeros_like(gkt_ref)
        gvt_ref[...] = jnp.zeros_like(gvt_ref)

    low_block = first_start(starts_ref, block * BT) // BT
    fill_mask(starts_ref, mask_ref, block, low_block)
    lane = lax.broadcasted_iota(jnp.int32, (1, 128), 1)
    qt_ref[...] = q_ref[...].T

    def prepare(m, carry):
        vl = pl.ds(pl.multiple_of(m * 128, 128), 128)
        grad_attn = nt(ga_ref[...], out_w_ref[vl, :])
        grad_numer = grad_attn * (2.0 * rd_ref[:, vl])
        both = grad_numer * attn_ref[:, vl].astype(F32)
        first = jnp.sum(jnp.where(lane < HV, both, 0.0), axis=1, keepdims=True)
        second = jnp.sum(jnp.where(lane < HV, 0.0, both), axis=1, keepdims=True)
        gd_ref[:, vl] = jnp.where(lane < HV, -second, -first).astype(BF16)
        low = grad_numer.astype(BF16)
        gn_ref[:, vl] = low
        gnt_ref[vl, :] = low.T
        return carry

    lax.fori_loop(0, HEADS // 2, prepare, 0)

    def group(g, carry):
        first = g * hb
        qlanes = pl.ds(pl.multiple_of(first // 8 * 128, 128), 128)
        q = q_ref[:, qlanes]
        qms, gns = [], []
        for n in range(hb):
            h8 = lax.rem(first + n, 8)
            qms.append(jnp.where(lane // QK == h8, q, jnp.zeros_like(q)))
            vl = pl.ds(pl.multiple_of((first + n) // 2 * 128, 128), 128)
            gn = gn_ref[:, vl]
            gn = jnp.where(lane // HV == n % 2, gn, jnp.zeros_like(gn))
            gns.append(jnp.where(lane == HV * (1 - n % 2), gd_ref[:, vl], gn))

        def step(j, gq):
            rows = pl.ds(pl.multiple_of(j * BT, BT), BT)
            k = k_ref[rows, qlanes]
            mask = mask_ref[j]
            for n in range(hb):
                h = first + n
                vl = pl.ds(pl.multiple_of(h // 2 * 128, 128), 128)
                v = v_ref[rows, vl]
                v = jnp.where(lane // HV == n % 2, v, jnp.ones_like(v))
                t1 = nt(qms[n], k) + 1.0
                p = (t1 * t1 + 1.0).astype(BF16) * mask
                dp = nt(gns[n], v).astype(BF16) * mask
                gs = (dp.astype(F32) * t1).astype(BF16)
                h8 = lax.rem(h, 8)
                km = jnp.where(lane // QK == h8, k, jnp.zeros_like(k))
                gq = gq + nn(gs, km)
                qrows = pl.ds(pl.multiple_of(h * QK, QK), QK)
                vrows = pl.ds(pl.multiple_of(h * HV, HV), HV)
                gkt_ref[qrows, rows] += nn(qt_ref[qrows, :], gs)
                gvt_ref[vrows, rows] += nn(gnt_ref[vrows, :], p)
            return gq

        gq = lax.fori_loop(low_block, block + 1, step, jnp.zeros((BT, 128), F32))
        gq_ref[:, qlanes] = (gq * 0.25).astype(BF16)
        return carry

    lax.fori_loop(0, HEADS // hb, group, 0)

    @pl.when(block == pl.num_programs(0) - 1)
    def _():
        gk_ref[...] = gkt_ref[...].T.astype(BF16)

        def turn(m, carry):
            vl = pl.ds(pl.multiple_of(m * 128, 128), 128)
            gv_ref[:, vl] = (gvt_ref[vl, :] * 0.5).T.astype(BF16)
            return carry

        lax.fori_loop(0, HEADS // 2, turn, 0)


def attn_bwd(starts, q, k, v, attn, rd, ga, out_w):
    hb = 8
    length = q.shape[0]
    nq, nv = HEADS * QK, HEADS * HV

    def whole(rows, cols):
        return pl.BlockSpec((rows, cols), lambda i: (0, 0))

    def rowblk(cols):
        return pl.BlockSpec((BT, cols), lambda i: (i, 0))

    return pl.pallas_call(
        functools.partial(attn_bwd_kernel, hb),
        grid=(length // BT,),
        out_shape=(
            jax.ShapeDtypeStruct((length, nq), BF16),
            jax.ShapeDtypeStruct((length, nq), BF16),
            jax.ShapeDtypeStruct((length, nv), BF16),
        ),
        in_specs=[
            pl.BlockSpec(memory_space=pltpu.SMEM),
            rowblk(nq), whole(length, nq), whole(length, nv), rowblk(nv), rowblk(nv), rowblk(nv), whole(nv, D),
        ],
        out_specs=(rowblk(nq), whole(length, nq), whole(length, nv)),
        scratch_shapes=[
            pltpu.VMEM((length // BT, BT, BT), BF16),
            pltpu.VMEM((BT, nv), BF16),
            pltpu.VMEM((BT, nv), BF16),
            pltpu.VMEM((nq, BT), BF16),
            pltpu.VMEM((nv, BT), BF16),
            pltpu.VMEM((nq, length), F32),
            pltpu.VMEM((nv, length), F32),
        ],
        compiler_params=pltpu.CompilerParams(vmem_limit_bytes=50 * 2**20),
        name="attn_bwd",
    )(starts, q, k, v, attn, rd, ga, out_w)


def update(weight, grad_total, moment, average, rate):
    moment_next = MOMENTUM * moment + grad_total
    weight_next = weight - rate * (grad_total + MOMENTUM * moment_next)
    average_next = average + (weight_next - average) / STEP
    return (moment_next, weight_next, average_next)


def on_device(
    tokens,
    cotangent,
    doc_starts,
    queries_keys,
    value_weight,
    out_weight,
    gate_up,
    down_weight,
    norm_gains,
    queries_moment,
    value_moment,
    out_moment,
    gate_moment,
    down_moment,
    gains_moment,
    queries_average,
    value_average,
    out_average,
    gate_average,
    down_average,
    gains_average,
):
    groups = lax.axis_size("feat")
    length = tokens.shape[0]
    total_tokens = float(length * lax.axis_size("dp"))
    half = HEADS * QK
    pair_cols = queries_keys.shape[1]
    value_cols = value_weight.shape[1]
    feat = lax.axis_index("feat")
    own_qkv = jnp.concatenate([queries_keys.astype(BF16), value_weight.astype(BF16)], axis=1)
    own_out = out_weight.astype(BF16)
    gate_low = gate_up.astype(BF16)
    down_low = down_weight.astype(BF16)
    all_qkv = lax.all_gather(own_qkv, "feat", axis=0)
    all_out = lax.all_gather(own_out, "feat", axis=0, tiled=True)
    pairs_full = all_qkv[:, :, :pair_cols].transpose(1, 0, 2).reshape(D, 2 * half)
    values_full = all_qkv[:, :, pair_cols:].transpose(1, 0, 2).reshape(D, HEADS * HV)
    inputs = tokens.astype(F32)
    scale_one = lax.rsqrt(jnp.mean(inputs * inputs, axis=1, keepdims=True) + EPS)
    unit_one = inputs * scale_one
    normed_one = (unit_one * norm_gains[0]).astype(BF16)
    pairs = jnp.dot(normed_one, pairs_full, preferred_element_type=F32).astype(BF16)
    values = jnp.dot(normed_one, values_full, preferred_element_type=F32).astype(BF16)
    queries = pairs[:, :half] * jnp.bfloat16(0.25)
    keys = pairs[:, half:]
    attn_low, recip = attn_fwd(doc_starts, queries, keys, values, 8)
    attended = jnp.dot(attn_low, all_out, preferred_element_type=F32)
    hidden_one = inputs + attended
    scale_two = lax.rsqrt(jnp.mean(hidden_one * hidden_one, axis=1, keepdims=True) + EPS)
    unit_two = hidden_one * scale_two
    normed_two = (unit_two * norm_gains[1]).astype(jnp.bfloat16)
    gate_value = jnp.dot(normed_two, gate_low[0], preferred_element_type=jnp.float32)
    up_value = jnp.dot(normed_two, gate_low[1], preferred_element_type=jnp.float32)
    activated = jax.nn.silu(gate_value)
    hidden_low = (activated * up_value).astype(jnp.bfloat16)
    ffn_out = lax.psum(
        jnp.dot(hidden_low, down_low, preferred_element_type=jnp.float32).astype(jnp.bfloat16),
        "feat",
    ).astype(jnp.float32)
    mixed = (hidden_one + ffn_out).astype(jnp.bfloat16)
    grad_down = jnp.einsum("tf,td->fd", hidden_low, cotangent, preferred_element_type=jnp.float32)
    grad_hidden_units = jnp.einsum(
        "td,fd->tf", cotangent, down_low, preferred_element_type=jnp.float32
    )
    sigmoid_gate = jax.nn.sigmoid(gate_value)
    slope = sigmoid_gate * (1.0 + gate_value * (1.0 - sigmoid_gate))
    grad_gate = (grad_hidden_units * up_value * slope).astype(jnp.bfloat16)
    grad_up = (grad_hidden_units * activated).astype(jnp.bfloat16)
    grad_gate_up = jnp.stack(
        [
            jnp.einsum("td,tf->df", normed_two, grad_gate, preferred_element_type=jnp.float32),
            jnp.einsum("td,tf->df", normed_two, grad_up, preferred_element_type=jnp.float32),
        ]
    )
    normed_two_part = jnp.einsum(
        "tf,df->td", grad_gate, gate_low[0], preferred_element_type=jnp.float32
    ) + jnp.einsum("tf,df->td", grad_up, gate_low[1], preferred_element_type=jnp.float32)
    grad_normed_two = lax.psum(normed_two_part.astype(jnp.bfloat16), "feat").astype(jnp.float32)
    gain_two = jnp.sum(grad_normed_two * unit_two, axis=0)
    grad_unit_two = grad_normed_two * norm_gains[1]
    grad_hidden = cotangent.astype(jnp.float32) + scale_two * (
        grad_unit_two - unit_two * jnp.mean(grad_unit_two * unit_two, axis=1, keepdims=True)
    )
    grad_attended = grad_hidden.astype(jnp.bfloat16)
    own_attn = lax.dynamic_slice_in_dim(attn_low, feat * value_cols, value_cols, 1)
    grad_out = jnp.einsum("tv,td->vd", own_attn, grad_attended, preferred_element_type=F32)
    grad_queries, grad_keys, grad_values = attn_bwd(
        doc_starts, queries, keys, values, attn_low, recip, grad_attended, all_out
    )
    grad_pairs_all = jnp.concatenate([grad_queries, grad_keys], axis=1)
    own_pairs = lax.dynamic_slice_in_dim(grad_pairs_all, feat * pair_cols, pair_cols, 1)
    own_values = lax.dynamic_slice_in_dim(grad_values, feat * value_cols, value_cols, 1)
    grad_pairs = jnp.einsum("td,tq->dq", normed_one, own_pairs, preferred_element_type=F32)
    grad_value = jnp.einsum("td,tv->dv", normed_one, own_values, preferred_element_type=F32)
    grad_normed_one = jnp.einsum(
        "tq,dq->td", grad_pairs_all, pairs_full, preferred_element_type=F32
    ) + jnp.einsum("tv,dv->td", grad_values, values_full, preferred_element_type=F32)
    gain_one = jnp.sum(grad_normed_one * unit_one, axis=0)
    grad_unit_one = grad_normed_one * norm_gains[0]
    input_gradient = grad_hidden + scale_one * (
        grad_unit_one - unit_one * jnp.mean(grad_unit_one * unit_one, axis=1, keepdims=True)
    )
    gain_one, gain_two = lax.psum((gain_one, gain_two), "dp")
    grad_gate_up, grad_down = lax.psum((grad_gate_up.astype(BF16), grad_down.astype(BF16)), "dp")
    grad_pairs, grad_value, grad_out = lax.psum(
        (grad_pairs.astype(BF16), grad_value.astype(BF16), grad_out.astype(BF16)), "dp"
    )
    grad_gains = jnp.stack([gain_one, gain_two])
    first = update(
        queries_keys, grad_pairs, queries_moment, queries_average, (D * total_tokens) ** (-0.5)
    )
    second = update(
        value_weight, grad_value, value_moment, value_average, (D * total_tokens) ** (-0.5)
    )
    third = update(
        out_weight, grad_out, out_moment, out_average, (HEADS * HV * total_tokens) ** (-0.5)
    )
    fourth = update(gate_up, grad_gate_up, gate_moment, gate_average, (D * total_tokens) ** (-0.5))
    fifth = update(down_weight, grad_down, down_moment, down_average, (FF * total_tokens) ** (-0.5))
    sixth = update(
        norm_gains, grad_gains, gains_moment, gains_average, 0.2 * total_tokens ** (-0.5)
    )
    return (
        mixed,
        input_gradient,
        first[0],
        first[1],
        first[2],
        second[0],
        second[1],
        second[2],
        third[0],
        third[1],
        third[2],
        fourth[0],
        fourth[1],
        fourth[2],
        fifth[0],
        fifth[1],
        fifth[2],
        sixth[0],
        sixth[1],
        sixth[2],
    )


def solution(mesh):
    in_specs = (
        P("dp", None),
        P("dp", None),
        P("dp", None),
        P(None, "feat"),
        P(None, "feat"),
        P("feat", None),
        P(None, None, "feat"),
        P("feat", None),
        P(),
        P(None, "feat"),
        P(None, "feat"),
        P("feat", None),
        P(None, None, "feat"),
        P("feat", None),
        P(),
        P(None, "feat"),
        P(None, "feat"),
        P("feat", None),
        P(None, None, "feat"),
        P("feat", None),
        P(),
    )
    out_specs = (
        P("dp", None),
        P("dp", None),
        P(None, "feat"),
        P(None, "feat"),
        P(None, "feat"),
        P(None, "feat"),
        P(None, "feat"),
        P(None, "feat"),
        P("feat", None),
        P("feat", None),
        P("feat", None),
        P(None, None, "feat"),
        P(None, None, "feat"),
        P(None, None, "feat"),
        P("feat", None),
        P("feat", None),
        P("feat", None),
        P(),
        P(),
        P(),
    )
    return jax.shard_map(
        on_device, mesh=mesh, in_specs=in_specs, out_specs=out_specs, check_vma=False
    )
```

time: 859 us -> 519 us (0.60)
  waiting for transfers between devices: 530 us -> 276 us
  matrix products: 190 us -> 47.7 us
  Pallas kernels: 0 us -> 81.6 us
  other arithmetic: 79.2 us -> 54.8 us
    psum x3 -> x1, waiting for transfers between devices: 363 us -> 65.8 us  [on_device(): lax.psum((grad_pairs.astype(BF16), grad_value.astype(BF16), grad_out.asty...]
    dot_general x24 -> x8, matrix products: 163 us -> 24.8 us  [the longest x1 5.32 us: on_device(): attended = jnp.dot(attn_low, all_out, preferred_element_type=F32)]
    pallas_call x0 -> x2, Pallas kernels: none -> 81.6 us  [the longest x1 59.7 us: attn_bwd(): pl.pallas_call(functools.partial(attn_bwd_kernel, hb), grid=(length // BT...]
    all_gather x2, waiting for transfers between devices: 32 us -> 65.7 us  [the longest x1 60.1 us: on_device(): all_qkv = lax.all_gather(own_qkv, 'feat', axis=0)]
    reduce_sum x6 -> x0, other arithmetic: 13.9 us -> none  [the longest x2 7.78 us: feature_map(): pairs[..., :, None] * pairs[..., None, :]]
    transpose x1 -> x4, local copies, waits for them, and re-layouts: 1.38 us -> 11.2 us  [the longest x2 7.44 us: on_device(): all_qkv[:, :, pair_cols:].transpose(1, 0, 2).reshape(D, HEADS * HV)]
  transfers between devices with their start and end apart: 6 -> 4, of which waited for: 6 -> 4; matrix products, arithmetic and copies ran while one was open for 8% -> 10% of each run, Pallas kernels for 0% -> 4%
where the time goes in v1:
time: 519 us; the launch traced here: 509 us
  waiting for transfers between devices  276 us (53%)
  Pallas kernels  81.6 us (16%)
  other arithmetic  54.8 us (11%)
  matrix products  47.7 us (9%)
  local copies, waits for them, and re-layouts  21.6 us (4%)
  between operations  14.8 us (3%)
  blocking collectives  13.1 us (3%)
    psum x1, waiting for transfers between devices, on_device(): lax.psum(jnp.dot(hidden_low, down_low, preferred_element_type=jnp.float32...  144 us
    psum x1, waiting for transfers between devices, on_device(): lax.psum((grad_pairs.astype(BF16), grad_value.astype(BF16), grad_out.asty...  65.8 us
    all_gather x1, waiting for transfers between devices, on_device(): all_qkv = lax.all_gather(own_qkv, 'feat', axis=0)  60.1 us
    pallas_call x1, Pallas kernels, attn_bwd(): pl.pallas_call(functools.partial(attn_bwd_kernel, hb), grid=(length // BT...  59.7 us
    add x6, other arithmetic, update(): average_next = average + (weight_next - average) / STEP  26.2 us
    pallas_call x1, Pallas kernels, attn_fwd(): pl.pallas_call(functools.partial(attn_fwd_kernel, hb), grid=(length // BT...  22 us
    psum x1, blocking collectives, on_device(): gain_one, gain_two = lax.psum((gain_one, gain_two), 'dp')  13.1 us
    unnamed x83, local copies, waits for them, and re-layouts  10.4 us
  transfers between devices with their start and end apart: 4, of which 4 were waited for; matrix products, arithmetic and copies ran while one was open for 10% of the time, Pallas kernels for 4%

profile of v1, /device:TPU:0, one launch (start us, length us, event | category | flops | bytes accessed | tf_op | source)
XLA Modules:
  0.0 509.3 jit_solution(4468665151994619355)
XLA Ops:
  11.7 4.7 convert_element_type.101
  17.0 60.1 %all-gather.6.cloned.1.call-done = bf16[4096,384]{1,0:T(8,128)(2,1)} async-done(((bf16[1024,384]{1,0:T(8,128)(2,1)}), bf16[4096,384]{1,0:T(8,128)(2,1)}) %all-gather.6.cloned.1.call-update) | async-done | bytes 3145744 | tf_op jit(solution)/shard_map/all_gather | solution.py:269
  80.8 3.4 slice_bitcast_fusion
  84.2 4.0 copy.44
  92.9 22.0 %shard_map.356 = (bf16[1024,1024]{1,0:T(8,128)(2,1)S(1)}, f32[1024,1024]{1,0:T(8,128)S(1)}) custom-call(s32[1,8]{1,0:T(1,128)S(1)} %copy-done.3, bf16[1024,256]{1,0:T(8,128)(2,1)S(1)} %get-tuple-element.67.q_ref, bf16[1024,256]{1,0:T(8,128)(2,1)S(1)} %get-tuple-element.66.k_ref, bf16[1024,1024]{1,0:T(8,128)(2,1)S(1)} %convolution_convert_fusion.v_ref), custom_call_target="tpu_custom_call" | custom-call | tf_op jit(solution)/shard_map/pallas_call | solution.py:94
  118.2 5.6 %all-gather.4.cloned.1.call-done.out_w_ref = bf16[1024,1024]{1,0:T(8,128)(2,1)} async-done(((bf16[256,1024]{1,0:T(8,128)(2,1)}), bf16[1024,1024]{1,0:T(8,128)(2,1)}) %all-gather.4.cloned.1.call-update) | async-done | bytes 2097168 | tf_op jit(solution)/shard_map/all_gather | solution.py:270
  123.8 5.3 %multiply_reduce_fusion = (f32[1024]{0:T(1024)S(1)}, f32[1024,1024]{1,0:T(8,128)S(1)}) fusion(bf16[1024,1024]{1,0:T(8,128)(2,1)} %copy-done.2, bf16[1024,1024]{1,0:T(8,128)(2,1)} %all-gather.4.cloned.1.call-done.out_w_ref, bf16[1024,1024]{1,0:T(8,128)(2,1)} %param.21), kind=kOutput, calls=%fused_computation.30 | convolution fusion | flops 2151676928 | bytes 10489856 | tf_op jit(solution)/shard_map/dot_general | solution.py:282
  136.6 3.0 multiply_convert_fusion.1
  139.7 3.2 convolution_convert_fusion.1
  144.7 3.3 add_convert_fusion
  148.1 3.8 fusion.23
  158.2 144.1 %all-reduce.8.cloned.1.call-done = (bf16[1024,1024]{1,0:T(8,128)(2,1)}, bf16[1024,1024]{1,0:T(8,128)(2,1)}) async-done(((bf16[1024,1024]{1,0:T(8,128)(2,1)}, bf16[1024,1024]{1,0:T(8,128)(2,1)}), (bf16[1024,1024]{1,0:T(8,128)(2,1)}, bf16[1024,1024]{1,0:T(8,128)(2,1)})) %all-reduce.8.cloned.1.call-update) | async-done | bytes 4194320 | tf_op jit(solution)/shard_map/psum | solution.py:291
  302.2 4.3 fusion.11
  306.9 3.9 fusion.42.ga_ref
  310.8 59.7 %attn_bwd.1 = (bf16[1024,256]{1,0:T(8,128)(2,1)S(1)}, bf16[1024,256]{1,0:T(8,128)(2,1)S(1)}, bf16[1024,1024]{1,0:T(8,128)(2,1)}) custom-call(s32[1,8]{1,0:T(1,128)S(1)} %copy-done.3, bf16[1024,256]{1,0:T(8,128)(2,1)S(1)} %get-tuple-element.67.q_ref, bf16[1024,256]{1,0:T(8,128)(2,1)S(1)} %get-tuple-element.66.k_ref, bf16[1024,1024]{1,0:T(8,128)(2,1)} %copy-done, ...), custom_call_target="tpu_custom_call" | custom-call | tf_op jit(solution)/shard_map/attn_bwd/pallas_call | solution.py:201
  373.2 2.8 convolution_convert_fusion.7
  377.9 4.7 fusion.54
  382.6 3.9 fusion.17
  386.5 13.1 %all-reduce = (f32[1,1024]{1,0:T(1,128)S(1)}, f32[1,1024]{1,0:T(1,128)S(1)}) all-reduce(f32[1,1024]{1,0:T(1,128)S(1)} %bitcast.60, f32[1,1024]{1,0:T(1,128)S(1)} %bitcast.61), channel_id=1, replica_groups=mesh['dp'=8,'feat'=4] {'dp'}, use_global_device_ids=true, to_apply=%region_14.15 | all-reduce | flops 2048 | bytes 16384 | tf_op jit(solution)/shard_map/psum | solution.py:338
  400.2 8.6 %fusion.16 = (f32[1024,1024]{1,0:T(8,128)}, bf16[1024,1024]{1,0:T(8,128)(2,1)}) fusion(bf16[1024,1024]{1,0:T(8,128)(2,1)} %param.21, f32[1024,1024]{1,0:T(8,128)} %get-tuple-element.72, f32[1024]{0:T(1024)S(1)} %broadcast_multiply_fusion, f32[1024]{0:T(1024)S(1)} %bitcast.59, f32[1024]{0:T(1024)S(1)} %add_rsqrt_fusion.1, ...), kind=kLoop, calls=%fused_computation.24 | loop fusion | flops 18874368 | bytes 23093248 | tf_op jit(solution)/shard_map/add | solution.py:335
  408.9 65.8 %all-reduce.6.cloned.1.call-done = (bf16[1024,128]{1,0:T(8,128)(2,1)}, bf16[1024,256]{1,0:T(8,128)(2,1)}, bf16[256,1024]{1,0:T(8,128)(2,1)}, bf16[2,1024,688]{1,2,0:T(8,128)(2,1)}, bf16[688,1024]{1,0:T(8,128)(2,1)}) async-done(((bf16[1024,128]{1,0:T(8,128)(2,1)}, bf16[1024,256]{1,0:T(8,128)(2,1)}, bf16[256,1024]{1,0:T(8,128)(2,1)}, bf16[2,1024,688]{1,2,0:T(8,128)(2,1)}, bf16[688,1024]{1,0:T(8,128)(2,1)}), ...) | async-done | bytes 5537808 | tf_op jit(solution)/shard_map/psum | solution.py:340
  477.4 3.1 multiply_add_fusion.3
  483.5 13.3 %multiply_add_fusion = (f32[2,1024,688]{1,2,0:T(8,128)}, f32[2,1024,688]{1,2,0:T(8,128)}, f32[2,1024,688]{1,2,0:T(8,128)}) fusion(f32[2,1024,688]{1,2,0:T(8,128)} %param.39, f32[2,1024,688]{1,2,0:T(8,128)} %param.27, bf16[2,1024,688]{1,2,0:T(8,128)(2,1)S(1)} %copy-done.23, f32[2,1024,688]{1,2,0:T(8,128)} %param.33), kind=kLoop, calls=%fused_computation.11 | loop fusion | flops 14090240 | bytes 36634624 | tf_op jit(solution)/shard_map/add | solution.py:231
  498.0 4.4 multiply_add_fusion.1
  (119 shorter events, 44.5 us)
Async XLA Ops:
  7.2 69.8 %all-gather.6.cloned.1.call-start = ((), (), s32[]{:S(2)}) async-start(), calls=%async_computation.1 | async-start | bytes 3932160 | tf_op jit(solution)/shard_map/all_gather | solution.py:269
  10.7 113.1 %all-gather.4.cloned.1.call-start = ((), (), s32[]{:S(2)}) async-start(), calls=%async_computation | async-start | bytes 2621440 | tf_op jit(solution)/shard_map/all_gather | solution.py:270
  11.6 4.8 copy-start.7
  11.7 5.3 %copy-start.33 = (f32[2,1024]{1,0:T(2,128)S(1)}, f32[2,1024]{1,0:T(2,128)}, u32[]{:S(2)}) copy-start(f32[2,1024]{1,0:T(2,128)} %param.29) | copy-start | bytes 24580
  11.7 290.6 %all-reduce.8.cloned.1.call-start = ((), (), s32[]{:S(2)}) async-start(), calls=%async_computation.3 | async-start | bytes 8388608 | tf_op jit(solution)/shard_map/psum | solution.py:291
  80.8 7.5 %copy-start.13 = (bf16[1024,4,128]{0,2,1:T(8,128)(2,1)}, bf16[1024,4,128]{0,2,1:T(8,128)(2,1)S(1)}, u32[]{:S(2)}) copy-start(bf16[1024,4,128]{0,2,1:T(8,128)(2,1)S(1)} %copy.43) | copy-start | bytes 3145732
  92.9 36.3 %copy-start = (bf16[1024,1024]{1,0:T(8,128)(2,1)}, bf16[1024,1024]{1,0:T(8,128)(2,1)S(1)}, u32[]{:S(2)}) copy-start(bf16[1024,1024]{1,0:T(8,128)(2,1)S(1)} %convolution_convert_fusion.v_ref) | copy-start | bytes 6291460
  139.7 5.1 copy-start.40
  148.0 326.6 %all-reduce.6.cloned.1.call-start = ((), (), s32[]{:S(2)}) async-start(), calls=%async_computation.2 | async-start | bytes 11075584 | tf_op jit(solution)/shard_map/psum | solution.py:340
  148.1 3.8 copy-start.26
  302.2 4.3 copy-start.5
  302.2 4.7 copy-start.6
  310.8 59.7 %copy-start.11 = (bf16[1024,1024]{1,0:T(8,128)(2,1)S(1)}, bf16[1024,1024]{1,0:T(8,128)(2,1)}, u32[]{:S(2)}) copy-start(bf16[1024,1024]{1,0:T(8,128)(2,1)} %fusion.42.ga_ref) | copy-start | bytes 6291460
  377.9 4.7 copy-start.10
  377.9 4.7 copy-start.14
  382.6 17.0 %copy-start.34 = (f32[2,1024]{1,0:T(2,128)S(1)}, f32[2,1024]{1,0:T(2,128)}, u32[]{:S(2)}) copy-start(f32[2,1024]{1,0:T(2,128)} %param.41) | copy-start | bytes 24580
  382.6 17.0 %copy-start.35 = (f32[2,1024]{1,0:T(2,128)S(1)}, f32[2,1024]{1,0:T(2,128)}, u32[]{:S(2)}) copy-start(f32[2,1024]{1,0:T(2,128)} %param.35) | copy-start | bytes 24580
  408.9 68.5 %copy-start.15 = (f32[1024,256]{1,0:T(8,128)S(1)}, f32[1024,256]{1,0:T(8,128)}, u32[]{:S(2)}) copy-start(f32[1024,256]{1,0:T(8,128)} %param.25) | copy-start | bytes 3145732
  408.9 68.5 %copy-start.28 = (f32[1024,256]{1,0:T(8,128)S(1)}, f32[1024,256]{1,0:T(8,128)}, u32[]{:S(2)}) copy-start(f32[1024,256]{1,0:T(8,128)} %param.37) | copy-start | bytes 3145732
  408.9 68.5 %copy-start.29 = (f32[1024,256]{1,0:T(8,128)S(1)}, f32[1024,256]{1,0:T(8,128)}, u32[]{:S(2)}) copy-start(f32[1024,256]{1,0:T(8,128)} %param.31) | copy-start | bytes 3145732
  483.5 13.4 %copy-start.19 = (f32[688,1024]{1,0:T(8,128)S(1)}, f32[688,1024]{1,0:T(8,128)}, u32[]{:S(2)}) copy-start(f32[688,1024]{1,0:T(8,128)} %param.28) | copy-start | bytes 8454148
  483.5 13.4 %copy-start.20 = (f32[688,1024]{1,0:T(8,128)S(1)}, f32[688,1024]{1,0:T(8,128)}, u32[]{:S(2)}) copy-start(f32[688,1024]{1,0:T(8,128)} %param.40) | copy-start | bytes 8454148
  483.5 13.6 %copy-start.21 = (f32[688,1024]{1,0:T(8,128)S(1)}, f32[688,1024]{1,0:T(8,128)}, u32[]{:S(2)}) copy-start(f32[688,1024]{1,0:T(8,128)} %param.34) | copy-start | bytes 8454148
  483.5 14.5 %copy-start.27 = (bf16[688,1024]{1,0:T(8,128)(2,1)S(1)}, bf16[688,1024]{1,0:T(8,128)(2,1)}, u32[]{:S(2)}) copy-start(bf16[688,1024]{1,0:T(8,128)(2,1)} %get-tuple-element.40) | copy-start | bytes 4227076
  (21 other events, 54.7 us)
Sparse Core Ops, SparseCore 0:
  10.8 66.1 all-gather.5
  79.2 44.5 all-gather.3
  148.2 154.0 all-reduce.7
  378.0 96.6 all-reduce.5

commit v2 on v1

--- a/solution.py
+++ b/solution.py
@@ -16,6 +16,7 @@
 F32 = jnp.float32
 BF16 = jnp.bfloat16
 
+MESH = pl.DeviceIdType.MESH
 EPS = 1e-06
 MOMENTUM = 0.9
 
@@ -103,6 +104,389 @@
     )(starts, q, k, v)
 
 
+def gather_kernel(bits, own_ref, all_ref, send_sem, recv_sem, own_sem):
+    dp = lax.axis_index("dp")
+    f = lax.axis_index("feat")
+    last = lax.axis_size("feat") - 1
+    pieces = 2 ** len(bits)
+    j = lax.rem(dp, pieces)
+    base = dp - j
+
+    def flip(k, bit):
+        return k + bit - 2 * bit * lax.rem(k // bit, 2)
+
+    barrier = pltpu.get_barrier_semaphore()
+    for bit in bits:
+        pl.semaphore_signal(barrier, inc=1, device_id=(base + flip(j, bit), f), device_id_type=MESH)
+
+    @pl.when(f > 0)
+    def _():
+        pl.semaphore_signal(barrier, inc=1, device_id=(dp, f - 1), device_id_type=MESH)
+
+    @pl.when(f < last)
+    def _():
+        pl.semaphore_signal(barrier, inc=1, device_id=(dp, f + 1), device_id_type=MESH)
+
+    pl.semaphore_wait(barrier, len(bits) + jnp.where(f > 0, 1, 0) + jnp.where(f < last, 1, 0))
+
+    def copy(z, colour, k, slot, device, own=False):
+        source = own_ref.at[k, colour] if own else all_ref.at[z, k, colour]
+        return pltpu.make_async_remote_copy(
+            src_ref=source, dst_ref=all_ref.at[z, k, colour], send_sem=send_sem.at[z, colour, slot],
+            recv_sem=recv_sem.at[z, colour, k], device_id=device, device_id_type=MESH)
+
+    here = (dp, f)
+    for colour in range(2):
+        @pl.when(f > 0)
+        def _():
+            copy(f, colour, j, 0, (dp, f - 1), True).start()
+
+        @pl.when(f < last)
+        def _():
+            copy(f, colour, j, 1, (dp, f + 1), True).start()
+    mine = pltpu.make_async_copy(own_ref, all_ref.at[f], own_sem)
+    mine.start()
+
+    order = [
+        jnp.where(f == 0, 1, f - 1),
+        jnp.where(f < 2, 2, jnp.where(f == 2, 3, 1)),
+        jnp.where(f < 2, 3, 0),
+    ]
+    colour_bits = [list(bits[1:]) + [bits[0]], list(bits[1:])[::-1] + [bits[0]]]
+
+    def held(colour, step):
+        out = [j]
+        for bit in colour_bits[colour][:step]:
+            out = out + [flip(k, bit) for k in out]
+        return out
+
+    def start_step(z, step):
+        for colour in range(2):
+            first = 2 + 2 ** step - 1
+            partner = (base + flip(j, colour_bits[colour][step]), f)
+            for n, k in enumerate(held(colour, step)):
+                copy(z, colour, k, first + n, partner).start()
+
+    def wait_step(z, step):
+        for colour in range(2):
+            for k in held(colour, step):
+                copy(z, colour, flip(k, colour_bits[colour][step]), 0, here).wait_recv()
+
+    def arrive(z):
+        ahead = jnp.where(z < f, f + 1, f - 1)
+        onward = jnp.logical_and(ahead >= 0, ahead <= last)
+        for colour in range(2):
+            copy(z, colour, j, 0, here).wait_recv()
+
+            @pl.when(onward)
+            def _():
+                copy(z, colour, j, jnp.where(z < f, 1, 0), (dp, ahead)).start()
+        start_step(z, 0)
+
+    steps = len(bits)
+    arrive(order[0])
+    for z, step in [(1, None), (0, 0), (2, None), (1, 0), (0, 1), (2, 0), (1, 1), (0, 2), (2, 1), (1, 2), (2, 2)]:
+        if step is None:
+            arrive(order[z])
+        else:
+            wait_step(order[z], step)
+            if step + 1 < steps:
+                start_step(order[z], step + 1)
+    for z in order:
+        ahead = jnp.where(z < f, f + 1, f - 1)
+        onward = jnp.logical_and(ahead >= 0, ahead <= last)
+        for colour in range(2):
+            @pl.when(onward)
+            def _():
+                copy(z, colour, j, jnp.where(z < f, 1, 0), here).wait_send()
+            for step in range(steps):
+                for n, k in enumerate(held(colour, step)):
+                    copy(z, colour, k, 2 + 2 ** step - 1 + n, here).wait_send()
+    for colour in range(2):
+        @pl.when(f > 0)
+        def _():
+            copy(f, colour, j, 0, here, True).wait_send()
+
+        @pl.when(f < last)
+        def _():
+            copy(f, colour, j, 1, here, True).wait_send()
+    mine.wait()
+
+
+def gather_all(own, cid):
+    rows, cols = own.shape
+    bits = (1, 2, 4)
+    shape = (8, 2, rows // 16, cols)
+    out = pl.pallas_call(
+        functools.partial(gather_kernel, bits),
+        out_shape=jax.ShapeDtypeStruct((4,) + shape, BF16),
+        in_specs=[pl.BlockSpec(memory_space=pltpu.VMEM)],
+        out_specs=pl.BlockSpec(memory_space=pltpu.VMEM),
+        scratch_shapes=[pltpu.SemaphoreType.DMA((4, 2, 9)), pltpu.SemaphoreType.DMA((4, 2, 8)), pltpu.SemaphoreType.DMA],
+        compiler_params=pltpu.CompilerParams(collective_id=cid, has_side_effects=True, vmem_limit_bytes=32 * 2**20),
+        name="gather_weights",
+    )(own.reshape(shape))
+    return out.reshape(4, rows, cols)
+
+
+class LineSum:
+    def __init__(self, part, leaf, mid, total, send, recv, rows, lags=(0, 2, 4)):
+        self.part, self.leaf, self.mid, self.total, self.send, self.recv = part, leaf, mid, total, send, recv
+        self.rows, self.lags = rows, lags
+        self.count = part.shape[0] // rows
+        self.dp, self.f = lax.axis_index("dp"), lax.axis_index("feat")
+
+    def barrier(self):
+        sem = pltpu.get_barrier_semaphore()
+        dp, f = self.dp, self.f
+
+        @pl.when(f > 0)
+        def _():
+            pl.semaphore_signal(sem, inc=1, device_id=(dp, f - 1), device_id_type=MESH)
+
+        @pl.when(f < 3)
+        def _():
+            pl.semaphore_signal(sem, inc=1, device_id=(dp, f + 1), device_id_type=MESH)
+        pl.semaphore_wait(sem, jnp.where(f > 0, 1, 0) + jnp.where(f < 3, 1, 0))
+
+    def place(self, c):
+        odd = lax.rem(c, 2)
+        return self.f + odd * (3 - 2 * self.f), 1 - 2 * odd
+
+    def copy(self, c, src, dst, kind, slot, to):
+        at = pl.ds(pl.multiple_of(c * self.rows, self.rows), self.rows)
+        return pltpu.make_async_remote_copy(
+            src_ref=src.at[at], dst_ref=dst.at[at], send_sem=self.send.at[slot, c], recv_sem=self.recv.at[kind, c],
+            device_id=(self.dp, to), device_id_type=MESH)
+
+    def leaves(self, c):
+        p, up = self.place(c)
+
+        @pl.when(p == 3)
+        def _():
+            self.copy(c, self.part, self.leaf, 0, 0, self.f - up).start()
+
+        @pl.when(p == 0)
+        def _():
+            self.copy(c, self.part, self.leaf, 0, 0, self.f + up).start()
+
+    def middle(self, c):
+        p, up = self.place(c)
+        at = pl.ds(pl.multiple_of(c * self.rows, self.rows), self.rows)
+
+        @pl.when(p == 2)
+        def _():
+            self.copy(c, self.part, self.leaf, 0, 0, self.f).wait_recv()
+            self.part[at, :] = (self.part[at, :].astype(F32) + self.leaf[at, :].astype(F32)).astype(BF16)
+            self.copy(c, self.part, self.mid, 1, 0, self.f - up).start()
+
+    def root(self, c):
+        p, up = self.place(c)
+        at = pl.ds(pl.multiple_of(c * self.rows, self.rows), self.rows)
+
+        @pl.when(p == 1)
+        def _():
+            self.copy(c, self.part, self.leaf, 0, 0, self.f).wait_recv()
+            self.copy(c, self.part, self.mid, 1, 0, self.f).wait_recv()
+            self.total[at, :] = (
+                self.part[at, :].astype(F32) + self.leaf[at, :].astype(F32) + self.mid[at, :].astype(F32)
+            ).astype(BF16)
+            self.copy(c, self.total, self.total, 2, 1, self.f + up).start()
+            self.copy(c, self.total, self.total, 2, 0, self.f - up).start()
+
+    def onward(self, c):
+        p, up = self.place(c)
+
+        @pl.when(p == 2)
+        def _():
+            self.copy(c, self.total, self.total, 2, 0, self.f).wait_recv()
+            self.copy(c, self.total, self.total, 2, 1, self.f + up).start()
+
+    def serve(self, i):
+        for lag, act in zip(self.lags, (self.middle, self.root, self.onward)):
+            c = i - lag
+
+            @pl.when(jnp.logical_and(c >= 0, c < self.count))
+            def _():
+                act(c)
+
+    def steps(self):
+        return self.count + self.lags[-1]
+
+    def arrived(self, c):
+        p, up = self.place(c)
+
+        @pl.when(jnp.logical_or(p == 0, p == 3))
+        def _():
+            self.copy(c, self.total, self.total, 2, 0, self.f).wait_recv()
+
+    def drain(self, c):
+        p, up = self.place(c)
+        self.copy(c, self.part, self.part, 0, 0, self.f).wait_send()
+
+        @pl.when(jnp.logical_or(p == 1, p == 2))
+        def _():
+            self.copy(c, self.part, self.part, 0, 1, self.f).wait_send()
+
+
+def line_sum_kernel(rows, lags, in_ref, total_ref, part, leaf, mid, send, recv):
+    line = LineSum(part, leaf, mid, total_ref, send, recv, rows, lags)
+    line.barrier()
+    part[...] = in_ref[...]
+
+    def each(act, n):
+        def body(c, carry):
+            act(c)
+            return carry
+        lax.fori_loop(0, n, body, 0)
+    each(line.leaves, line.count)
+    each(line.serve, line.steps())
+    each(line.arrived, line.count)
+    each(line.drain, line.count)
+
+
+def line_sum(x, cid, rows=32, lags=(0, 2, 4)):
+    length = x.shape[0]
+    count = length // rows
+    return pl.pallas_call(
+        functools.partial(line_sum_kernel, rows, lags),
+        out_shape=jax.ShapeDtypeStruct(x.shape, BF16),
+        in_specs=[pl.BlockSpec(memory_space=pltpu.VMEM)],
+        out_specs=pl.BlockSpec(memory_space=pltpu.VMEM),
+        scratch_shapes=[pltpu.VMEM(x.shape, BF16)] * 3 + [pltpu.SemaphoreType.DMA((2, count)), pltpu.SemaphoreType.DMA((3, count))],
+        compiler_params=pltpu.CompilerParams(collective_id=cid, has_side_effects=True, vmem_limit_bytes=32 * 2**20),
+        name="line_sum",
+    )(x)
+
+
+class CubeSum:
+    def __init__(self, work, recv, out, send_sem, recv_sem, pieces, bits):
+        self.work, self.recv, self.out, self.send_sem, self.recv_sem = work, recv, out, send_sem, recv_sem
+        self.pieces, self.nb = pieces, len(bits)
+        self.dp, self.f = lax.axis_index("dp"), lax.axis_index("feat")
+        self.orders = [list(bits), [bits[0]] + list(bits[1:])[::-1]]
+        self.bits = bits
+
+    def partner(self, bit):
+        return self.dp + bit - 2 * bit * lax.rem(self.dp // bit, 2)
+
+    def barrier(self):
+        sem = pltpu.get_barrier_semaphore()
+        for bit in self.bits:
+            pl.semaphore_signal(sem, inc=1, device_id=(self.partner(bit), self.f), device_id_type=MESH)
+        pl.semaphore_wait(sem, len(self.bits))
+
+    def lanes(self, colour):
+        half = self.work.shape[1] // 2
+        return pl.ds(colour * half, half)
+
+    def segment(self, piece, colour, k):
+        first, rows = self.pieces[piece]
+        start = first
+        for bit in self.orders[colour][:k]:
+            rows = rows // 2
+            start = start + rows * lax.rem(self.dp // bit, 2)
+        return start, rows
+
+    def at(self, start, rows):
+        return pl.ds(pl.multiple_of(start, 16), rows)
+
+    def halve(self, piece, colour, k):
+        start, rows = self.segment(piece, colour, k)
+        rows = rows // 2
+        bit = self.orders[colour][k]
+        own = lax.rem(self.dp // bit, 2)
+        first, whole = self.pieces[piece]
+        landing = first + whole - 2 * rows
+        return pltpu.make_async_remote_copy(
+            src_ref=self.work.at[self.at(start + rows * (1 - own), rows), self.lanes(colour)],
+            dst_ref=self.recv.at[self.at(landing, rows), self.lanes(colour)],
+            send_sem=self.send_sem.at[piece, colour, k], recv_sem=self.recv_sem.at[piece, colour, k],
+            device_id=(self.partner(bit), self.f), device_id_type=MESH)
+
+    def add(self, piece, colour, k):
+        start, rows = self.segment(piece, colour, k + 1)
+        first, whole = self.pieces[piece]
+        landing = first + whole - 2 * rows
+        target = self.out if k + 1 == self.nb else self.work
+        mine = self.work[self.at(start, rows), self.lanes(colour)].astype(F32)
+        target[self.at(start, rows), self.lanes(colour)] = (
+            mine + self.recv[self.at(landing, rows), self.lanes(colour)].astype(F32)
+        ).astype(BF16)
+
+    def double(self, piece, colour, k):
+        start, rows = self.segment(piece, colour, k + 1)
+        bit = self.orders[colour][k]
+        at = self.at(start, rows)
+        slot = 2 * self.nb - 1 - k
+        return pltpu.make_async_remote_copy(
+            src_ref=self.out.at[at, self.lanes(colour)], dst_ref=self.out.at[at, self.lanes(colour)],
+            send_sem=self.send_sem.at[piece, colour, slot], recv_sem=self.recv_sem.at[piece, colour, slot],
+            device_id=(self.partner(bit), self.f), device_id_type=MESH)
+
+    def launch(self, piece):
+        for colour in range(2):
+            self.halve(piece, colour, 0).start()
+
+    def advance(self, piece, t):
+        for colour in range(2):
+            if t < self.nb:
+                self.halve(piece, colour, t).wait_recv()
+                self.add(piece, colour, t)
+                if t + 1 < self.nb:
+                    self.halve(piece, colour, t + 1).start()
+                else:
+                    self.double(piece, colour, self.nb - 1).start()
+            else:
+                k = 2 * self.nb - 1 - t
+                self.double(piece, colour, k).wait_recv()
+                if k > 0:
+                    self.double(piece, colour, k - 1).start()
+
+    def drain(self, piece):
+        for colour in range(2):
+            for k in range(self.nb):
+                self.halve(piece, colour, k).wait_send()
+                self.double(piece, colour, k).wait_send()
+
+
+def cube_sum_kernel(pieces, bits, in_ref, out_ref, work, recv, send_sem, recv_sem):
+    cube = CubeSum(work, recv, out_ref, send_sem, recv_sem, pieces, bits)
+    work[...] = in_ref[...]
+    cube.barrier()
+    n = len(pieces)
+    for p in range(n):
+        cube.launch(p)
+    for t in range(2 * cube.nb):
+        for p in range(n):
+            cube.advance(p, t)
+    for p in range(n):
+        cube.drain(p)
+
+
+def split_rows(rows, unit, count):
+    units = rows // unit
+    out, first = [], 0
+    for n in range(count):
+        take = (units * (n + 1) // count - units * n // count) * unit
+        out.append((first, take))
+        first += take
+    return [p for p in out if p[1]]
+
+
+def cube_sum(x, dp_size, cid, count=3):
+    rows = x.shape[0]
+    bits = tuple(2**n for n in range(dp_size.bit_length() - 1))
+    pieces = split_rows(rows, 16 * dp_size, count)
+    return pl.pallas_call(
+        functools.partial(cube_sum_kernel, pieces, bits),
+        out_shape=jax.ShapeDtypeStruct(x.shape, BF16),
+        in_specs=[pl.BlockSpec(memory_space=pltpu.VMEM)],
+        out_specs=pl.BlockSpec(memory_space=pltpu.VMEM),
+        scratch_shapes=[pltpu.VMEM(x.shape, BF16)] * 2 + [pltpu.SemaphoreType.DMA((len(pieces), 2, 2 * len(bits)))] * 2,
+        compiler_params=pltpu.CompilerParams(collective_id=cid, has_side_effects=True, vmem_limit_bytes=40 * 2**20),
+        name="cube_sum",
+    )(x)
 def attn_bwd_kernel(
     hb, starts_ref, q_ref, k_ref, v_ref, attn_ref, rd_ref, ga_ref, out_w_ref,
     gq_ref, gk_ref, gv_ref, mask_ref, gn_ref, gd_ref, qt_ref, gnt_ref, gkt_ref, gvt_ref,
@@ -262,14 +646,15 @@
     pair_cols = queries_keys.shape[1]
     value_cols = value_weight.shape[1]
     feat = lax.axis_index("feat")
-    own_qkv = jnp.concatenate([queries_keys.astype(BF16), value_weight.astype(BF16)], axis=1)
-    own_out = out_weight.astype(BF16)
     gate_low = gate_up.astype(BF16)
     down_low = down_weight.astype(BF16)
-    all_qkv = lax.all_gather(own_qkv, "feat", axis=0)
-    all_out = lax.all_gather(own_out, "feat", axis=0, tiled=True)
-    pairs_full = all_qkv[:, :, :pair_cols].transpose(1, 0, 2).reshape(D, 2 * half)
-    values_full = all_qkv[:, :, pair_cols:].transpose(1, 0, 2).reshape(D, HEADS * HV)
+    own = jnp.concatenate(
+        [queries_keys.astype(BF16), value_weight.astype(BF16), out_weight.astype(BF16).T], axis=1
+    )
+    gathered = gather_all(own, 1)
+    pairs_full = gathered[:, :, :pair_cols].transpose(1, 0, 2).reshape(D, 2 * half)
+    values_full = gathered[:, :, pair_cols : pair_cols + value_cols].transpose(1, 0, 2).reshape(D, HEADS * HV)
+    all_out = gathered[:, :, pair_cols + value_cols :].transpose(0, 2, 1).reshape(HEADS * HV, D)
     inputs = tokens.astype(F32)
     scale_one = lax.rsqrt(jnp.mean(inputs * inputs, axis=1, keepdims=True) + EPS)
     unit_one = inputs * scale_one
@@ -288,10 +673,7 @@
     up_value = jnp.dot(normed_two, gate_low[1], preferred_element_type=jnp.float32)
     activated = jax.nn.silu(gate_value)
     hidden_low = (activated * up_value).astype(jnp.bfloat16)
-    ffn_out = lax.psum(
-        jnp.dot(hidden_low, down_low, preferred_element_type=jnp.float32).astype(jnp.bfloat16),
-        "feat",
-    ).astype(jnp.float32)
+    ffn_out = line_sum(jnp.dot(hidden_low, down_low, preferred_element_type=F32).astype(BF16), 2).astype(F32)
     mixed = (hidden_one + ffn_out).astype(jnp.bfloat16)
     grad_down = jnp.einsum("tf,td->fd", hidden_low, cotangent, preferred_element_type=jnp.float32)
     grad_hidden_units = jnp.einsum(
@@ -301,16 +683,12 @@
     slope = sigmoid_gate * (1.0 + gate_value * (1.0 - sigmoid_gate))
     grad_gate = (grad_hidden_units * up_value * slope).astype(jnp.bfloat16)
     grad_up = (grad_hidden_units * activated).astype(jnp.bfloat16)
-    grad_gate_up = jnp.stack(
-        [
-            jnp.einsum("td,tf->df", normed_two, grad_gate, preferred_element_type=jnp.float32),
-            jnp.einsum("td,tf->df", normed_two, grad_up, preferred_element_type=jnp.float32),
-        ]
-    )
+    grad_gate_turned = jnp.einsum("tf,td->fd", grad_gate, normed_two, preferred_element_type=F32)
+    grad_up_turned = jnp.einsum("tf,td->fd", grad_up, normed_two, preferred_element_type=F32)
     normed_two_part = jnp.einsum(
         "tf,df->td", grad_gate, gate_low[0], preferred_element_type=jnp.float32
     ) + jnp.einsum("tf,df->td", grad_up, gate_low[1], preferred_element_type=jnp.float32)
-    grad_normed_two = lax.psum(normed_two_part.astype(jnp.bfloat16), "feat").astype(jnp.float32)
+    grad_normed_two = line_sum(normed_two_part.astype(BF16), 2).astype(F32)
     gain_two = jnp.sum(grad_normed_two * unit_two, axis=0)
     grad_unit_two = grad_normed_two * norm_gains[1]
     grad_hidden = cotangent.astype(jnp.float32) + scale_two * (
@@ -325,8 +703,8 @@
     grad_pairs_all = jnp.concatenate([grad_queries, grad_keys], axis=1)
     own_pairs = lax.dynamic_slice_in_dim(grad_pairs_all, feat * pair_cols, pair_cols, 1)
     own_values = lax.dynamic_slice_in_dim(grad_values, feat * value_cols, value_cols, 1)
-    grad_pairs = jnp.einsum("td,tq->dq", normed_one, own_pairs, preferred_element_type=F32)
-    grad_value = jnp.einsum("td,tv->dv", normed_one, own_values, preferred_element_type=F32)
+    grad_pairs_turned = jnp.einsum("tq,td->qd", own_pairs, normed_one, preferred_element_type=F32)
+    grad_value_turned = jnp.einsum("tv,td->vd", own_values, normed_one, preferred_element_type=F32)
     grad_normed_one = jnp.einsum(
         "tq,dq->td", grad_pairs_all, pairs_full, preferred_element_type=F32
     ) + jnp.einsum("tv,dv->td", grad_values, values_full, preferred_element_type=F32)
@@ -335,12 +713,21 @@
     input_gradient = grad_hidden + scale_one * (
         grad_unit_one - unit_one * jnp.mean(grad_unit_one * unit_one, axis=1, keepdims=True)
     )
-    gain_one, gain_two = lax.psum((gain_one, gain_two), "dp")
-    grad_gate_up, grad_down = lax.psum((grad_gate_up.astype(BF16), grad_down.astype(BF16)), "dp")
-    grad_pairs, grad_value, grad_out = lax.psum(
-        (grad_pairs.astype(BF16), grad_value.astype(BF16), grad_out.astype(BF16)), "dp"
-    )
-    grad_gains = jnp.stack([gain_one, gain_two])
+    dp_size = lax.axis_size("dp")
+    units = [grad_down, grad_gate_turned, grad_up_turned, grad_out, grad_value_turned, grad_pairs_turned]
+    units = [u.astype(BF16) for u in units] + [jnp.stack([gain_one, gain_two]).astype(BF16)]
+    stacked = jnp.concatenate(units, axis=0)
+    rows = stacked.shape[0]
+    unit = 16 * dp_size
+    stacked = jnp.pad(stacked, ((0, (rows + unit - 1) // unit * unit - rows), (0, 0)))
+    summed = cube_sum(stacked, dp_size, 3, 4)
+    parts, at = [], 0
+    for u in units:
+        parts.append(summed[at : at + u.shape[0]].astype(F32))
+        at += u.shape[0]
+    grad_down, grad_out, grad_gains = parts[0], parts[3], parts[6]
+    grad_gate_up = jnp.stack([parts[1].T, parts[2].T])
+    grad_value, grad_pairs = parts[4].T, parts[5].T
     first = update(
         queries_keys, grad_pairs, queries_moment, queries_average, (D * total_tokens) ** (-0.5)
     )

time: 519 us -> 447 us (0.86); the launches traced: 509 us -> 443 us
  waiting for transfers between devices: 276 us -> 0 us
  Pallas kernels: 81.6 us -> 288 us
  local copies, waits for them, and re-layouts: 21.6 us -> 73 us
  between operations: 14.8 us -> 1.52 us
  blocking collectives: 13.1 us -> 0 us
  other arithmetic: 54.8 us -> 42.9 us
  matrix products: 47.7 us -> 37.5 us
    pallas_call x0 -> x4, Pallas kernels: none -> 213 us  [the longest x2 129 us: line_sum(): pl.pallas_call(functools.partial(line_sum_kernel, rows, lags), out_shape=...]
    psum x2 -> x0, waiting for transfers between devices: 210 us -> none  [the longest x1 144 us: on_device(): lax.psum(jnp.dot(hidden_low, down_low, preferred_element_type=jnp.float32...]
    all_gather x2 -> x0, waiting for transfers between devices: 65.7 us -> none  [the longest x1 60.1 us: on_device(): all_qkv = lax.all_gather(own_qkv, 'feat', axis=0)]
    unnamed x83 -> x98, local copies, waits for them, and re-layouts: 10.4 us -> 38.1 us
    concatenate x0 -> x2, local copies, waits for them, and re-layouts: none -> 25.1 us  [the longest x1 24.4 us: on_device(): stacked = jnp.concatenate(units, axis=0)]
    psum x1 -> x0, blocking collectives: 13.1 us -> none  [on_device(): gain_one, gain_two = lax.psum((gain_one, gain_two), 'dp')]
    transpose x4 -> x0, local copies, waits for them, and re-layouts: 11.2 us -> none  [the longest x2 7.44 us: on_device(): all_qkv[:, :, pair_cols:].transpose(1, 0, 2).reshape(D, HEADS * HV)]
  transfers between devices with their start and end apart: 4 -> 0, of which waited for: 4 -> 0; matrix products, arithmetic and copies ran while one was open for 10% -> 0% of each run, Pallas kernels for 4% -> 0%
where the time goes in v2:
time: 447 us; the launch traced here: 443 us
  Pallas kernels  288 us (64%)
  local copies, waits for them, and re-layouts  73 us (16%)
  other arithmetic  42.9 us (10%)
  matrix products  37.5 us (8%)
    pallas_call x2, Pallas kernels, line_sum(): pl.pallas_call(functools.partial(line_sum_kernel, rows, lags), out_shape=...  129 us
    pallas_call x1, Pallas kernels, attn_bwd(): pl.pallas_call(functools.partial(attn_bwd_kernel, hb), grid=(length // BT...  55.1 us
    pallas_call x1, Pallas kernels, cube_sum(): pl.pallas_call(functools.partial(cube_sum_kernel, pieces, bits), out_shap...  54.1 us
    unnamed x98, local copies, waits for them, and re-layouts  38.1 us
    pallas_call x1, Pallas kernels, gather_all(): pl.pallas_call(functools.partial(gather_kernel, bits), out_shape=jax.Shap...  30.3 us
    add x6, other arithmetic, update(): average_next = average + (weight_next - average) / STEP  26.7 us
    concatenate x1, local copies, waits for them, and re-layouts, on_device(): stacked = jnp.concatenate(units, axis=0)  24.4 us
    pallas_call x1, Pallas kernels, attn_fwd(): pl.pallas_call(functools.partial(attn_fwd_kernel, hb), grid=(length // BT...  19.9 us

profile of v2, /device:TPU:0, one launch (start us, length us, event | category | flops | bytes accessed | tf_op | source)
XLA Modules:
  0.0 443.4 jit_solution(9506743427555988133)
XLA Ops:
  14.2 4.6 %convert_element_type.102 = bf16[2,1024,688]{1,2,0:T(8,128)(2,1)} convert(f32[2,1024,688]{1,2,0:T(8,128)} %param.27) | non-fusion elementwise | flops 1409024 | bytes 8454144 | tf_op jit(solution)/shard_map/convert_element_type | solution.py:649
  18.8 30.3 %gather_weights.1 = bf16[4,8,2,64,640]{4,3,2,1,0:T(8,128)(2,1)S(1)} custom-call(bf16[8,2,64,640]{3,2,1,0:T(8,128)(2,1)S(1)} %bitcast.72), custom_call_target="tpu_custom_call" | custom-call | tf_op jit(solution)/shard_map/gather_weights/pallas_call | solution.py:220
  51.6 4.1 copy.84
  59.6 4.0 copy.83
  63.6 4.0 convolution_convert_fusion.v_ref
  67.6 19.9 %shard_map.356 = (bf16[1024,1024]{1,0:T(8,128)(2,1)S(1)}, f32[1024,1024]{1,0:T(8,128)S(1)}) custom-call(s32[1,8]{1,0:T(1,128)S(1)} %copy-done.4, bf16[1024,256]{1,0:T(8,128)(2,1)S(1)} %get-tuple-element.102.q_ref, bf16[1024,256]{1,0:T(8,128)(2,1)S(1)} %get-tuple-element.101.k_ref, bf16[1024,1024]{1,0:T(8,128)(2,1)S(1)} %convolution_convert_fusion.v_ref), custom_call_target="tpu_custom_call" | custom-call | tf_op jit(solution)/shard_map/pallas_call | solution.py:95
  90.6 2.9 copy-done.23
  97.6 3.3 multiply_convert_fusion.1
  100.9 2.8 convolution_convert_fusion.2
  103.7 2.7 convolution_convert_fusion.3
  106.4 2.8 convolution_convert_fusion.4
  111.1 66.3 %line_sum.2 = bf16[1024,1024]{1,0:T(8,128)(2,1)S(1)} custom-call(bf16[1024,1024]{1,0:T(8,128)(2,1)S(1)} %convolution_convert_fusion.1.in_ref), custom_call_target="tpu_custom_call" | custom-call | tf_op jit(solution)/shard_map/line_sum/pallas_call | solution.py:351
  181.2 62.8 %line_sum.3 = bf16[1024,1024]{1,0:T(8,128)(2,1)S(1)} custom-call(bf16[1024,1024]{1,0:T(8,128)(2,1)S(1)} %add_convert_fusion.in_ref), custom_call_target="tpu_custom_call" | custom-call | tf_op jit(solution)/shard_map/line_sum/pallas_call | solution.py:351
  247.9 55.1 %attn_bwd.1 = (bf16[1024,256]{1,0:T(8,128)(2,1)S(1)}, bf16[1024,256]{1,0:T(8,128)(2,1)S(1)}, bf16[1024,1024]{1,0:T(8,128)(2,1)}) custom-call(s32[1,8]{1,0:T(1,128)S(1)} %copy-done.4, bf16[1024,256]{1,0:T(8,128)(2,1)S(1)} %get-tuple-element.102.q_ref, bf16[1024,256]{1,0:T(8,128)(2,1)S(1)} %get-tuple-element.101.k_ref, bf16[1024,1024]{1,0:T(8,128)(2,1)} %copy-done.1, ...), custom_call_target="tpu_custom_call" | custom-call | tf_op jit(solution)/shard_map/attn_bwd/pallas_call | solution.py:585
  312.5 4.9 %fusion.16 = (f32[1024,1024]{1,0:T(8,128)}, bf16[1024,1024]{1,0:T(8,128)(2,1)}) fusion(bf16[1024,1024]{1,0:T(8,128)(2,1)S(1)} %copy-done.7, f32[1024,1024]{1,0:T(8,128)S(1)} %get-tuple-element.107, f32[1024]{0:T(1024)S(1)} %broadcast_multiply_fusion, f32[1024]{0:T(1024)S(1)} %bitcast.94, f32[1024]{0:T(1024)S(1)} %add_rsqrt_fusion.1, ...), kind=kLoop, calls=%fused_computation.24 | loop fusion | flops 18874368 | bytes 23093248 | tf_op jit(solution)/shard_map/add | solution.py:713
  317.4 24.4 %concatenate.12 = bf16[2706,1024]{1,0:T(8,128)(2,1)} concatenate(bf16[688,1024]{1,0:T(8,128)(2,1)} %convolution_convert_fusion.4, bf16[688,1024]{1,0:T(8,128)(2,1)} %convolution_convert_fusion.3, bf16[688,1024]{1,0:T(8,128)(2,1)} %convolution_convert_fusion.2, bf16[256,1024]{1,0:T(8,128)(2,1)S(1)} %convolution_convert_fusion.7, bf16[256,1024]{1,0:T(8,128)(2,1)S(1)} %convolution_convert_fusion.6, ...), dimensions={0} | concatenate | bytes 11083776 | tf_op jit(solution)/shard_map/concatenate | solution.py:719
  341.8 3.2 pad.4.in_ref
  345.0 54.1 %cube_sum.1 = bf16[2816,1024]{1,0:T(8,128)(2,1)S(1)} custom-call(bf16[2816,1024]{1,0:T(8,128)(2,1)S(1)} %pad.4.in_ref), custom_call_target="tpu_custom_call" | custom-call | tf_op jit(solution)/shard_map/cube_sum/pallas_call | solution.py:481
  405.0 3.5 multiply_add_fusion.3
  408.5 2.7 copy.80
  419.2 3.3 slice_bitcast_fusion.3
  422.5 3.2 multiply_add_fusion.2
  425.7 9.0 %multiply_add_fusion.1 = (f32[688,1024]{1,0:T(8,128)}, f32[688,1024]{1,0:T(8,128)}, f32[688,1024]{1,0:T(8,128)}) fusion(f32[688,1024]{1,0:T(8,128)} %param.40, f32[688,1024]{1,0:T(8,128)} %param.28, bf16[2816,1024]{1,0:T(8,128)(2,1)} %copy-done, f32[688,1024]{1,0:T(8,128)} %param.34), kind=kLoop, calls=%fused_computation.36 | loop fusion | flops 7045120 | bytes 18317312 | tf_op jit(solution)/shard_map/add | solution.py:615
  434.8 8.4 %multiply_add_fusion = (f32[2,1024,688]{1,2,0:T(8,128)}, f32[2,1024,688]{1,2,0:T(8,128)}, f32[2,1024,688]{1,2,0:T(8,128)}) fusion(f32[2,1024,688]{1,2,0:T(8,128)S(1)} %bitcast.78, f32[2,1024,688]{1,2,0:T(8,128)S(1)} %bitcast.74, bf16[1,1024,688]{1,2,0:T(8,128)(2,1)} %get-tuple-element.93, bf16[1,1024,688]{1,2,0:T(8,128)(2,1)S(1)} %get-tuple-element.92, ...), kind=kLoop, calls=%fused_computation.11 | loop fusion | flops 15499264 | bytes 36634624 | tf_op jit(solution)/shard_map/add | solution.py:615
  (131 shorter events, 59.8 us)
Async XLA Ops:
  0.7 4.3 copy-start.31
  0.7 7.4 %copy-start.16 = (f32[256,1024]{1,0:T(8,128)S(1)}, f32[256,1024]{1,0:T(8,128)}, u32[]{:S(2)}) copy-start(f32[256,1024]{1,0:T(8,128)} %param.26) | copy-start | bytes 3145732
  2.9 5.3 %copy-start.27 = (f32[1024,256]{1,0:T(8,128)S(1)}, f32[1024,256]{1,0:T(8,128)}, u32[]{:S(2)}) copy-start(f32[1024,256]{1,0:T(8,128)} %param.25) | copy-start | bytes 3145732
  51.6 5.4 %copy-start.7 = (bf16[1024,1024]{1,0:T(8,128)(2,1)S(1)}, bf16[1024,1024]{1,0:T(8,128)(2,1)}, u32[]{:S(2)}) copy-start(bf16[1024,1024]{1,0:T(8,128)(2,1)} %param.21) | copy-start | bytes 6291460
  63.6 4.0 copy-start.4
  67.6 22.4 %copy-start.1 = (bf16[1024,1024]{1,0:T(8,128)(2,1)}, bf16[1024,1024]{1,0:T(8,128)(2,1)S(1)}, u32[]{:S(2)}) copy-start(bf16[1024,1024]{1,0:T(8,128)(2,1)S(1)} %convolution_convert_fusion.v_ref) | copy-start | bytes 6291460
  67.6 19.9 %copy-start.13 = (bf16[4,1024,256]{1,2,0:T(8,128)(2,1)S(1)}, bf16[4,1024,256]{1,2,0:T(8,128)(2,1)}, u32[]{:S(2)}) copy-start(bf16[4,1024,256]{1,2,0:T(8,128)(2,1)} %copy.84) | copy-start | bytes 6291460
  90.2 155.2 %copy-start.5 = (f32[1024,1024]{1,0:T(8,128)}, f32[1024,1024]{1,0:T(8,128)S(1)}, u32[]{:S(2)}) copy-start(f32[1024,1024]{1,0:T(8,128)S(1)} %get-tuple-element.106) | copy-start | bytes 12582916
  247.9 55.1 %copy-start.8 = (bf16[1024,1024]{1,0:T(8,128)(2,1)S(1)}, bf16[1024,1024]{1,0:T(8,128)(2,1)}, u32[]{:S(2)}) copy-start(bf16[1024,1024]{1,0:T(8,128)(2,1)} %fusion.42.ga_ref) | copy-start | bytes 6291460
  345.0 56.6 %copy-start.15 = (f32[1024,128]{0,1:T(8,128)S(1)}, f32[1024,128]{0,1:T(8,128)}, u32[]{:S(2)}) copy-start(f32[1024,128]{0,1:T(8,128)} %copy-done.14) | copy-start | bytes 1572868
  345.0 56.6 %copy-start.25 = (f32[1024,128]{0,1:T(8,128)S(1)}, f32[1024,128]{0,1:T(8,128)}, u32[]{:S(2)}) copy-start(f32[1024,128]{0,1:T(8,128)} %copy.67) | copy-start | bytes 1572868
  345.0 56.6 %copy-start.26 = (f32[1024,128]{0,1:T(8,128)S(1)}, f32[1024,128]{0,1:T(8,128)}, u32[]{:S(2)}) copy-start(f32[1024,128]{0,1:T(8,128)} %copy.70) | copy-start | bytes 1572868
  401.6 3.4 copy-start.10
  401.6 3.4 copy-start.18
  405.0 6.2 %copy-start.32 = (f32[2,1024]{1,0:T(2,128)S(1)}, f32[2,1024]{1,0:T(2,128)}, u32[]{:S(2)}) copy-start(f32[2,1024]{1,0:T(2,128)} %param.29) | copy-start | bytes 24580
  405.0 6.2 %copy-start.33 = (f32[2,1024]{1,0:T(2,128)S(1)}, f32[2,1024]{1,0:T(2,128)}, u32[]{:S(2)}) copy-start(f32[2,1024]{1,0:T(2,128)} %param.41) | copy-start | bytes 24580
  405.0 29.7 %slice-start.4 = ((s8[5636096]{0:T(1024)(128)(4,1)}), s8[1441792]{0:T(1024)(128)(4,1)S(1)}, s32[]{:S(2)}) async-start(s8[5636096]{0:T(1024)(128)(4,1)} %bitcast.79), calls=%async_computation.4 | async-start | bytes 2883584
  408.5 8.1 %copy-start.20 = (f32[1024,256]{0,1:T(8,128)S(1)}, f32[1024,256]{0,1:T(8,128)}, u32[]{:S(2)}) copy-start(f32[1024,256]{0,1:T(8,128)} %get-tuple-element.87) | copy-start | bytes 3145732
  408.5 9.4 %copy-start.19 = (f32[1024,256]{0,1:T(8,128)S(1)}, f32[1024,256]{0,1:T(8,128)}, u32[]{:S(2)}) copy-start(f32[1024,256]{0,1:T(8,128)} %get-tuple-element.88) | copy-start | bytes 3145732
  422.5 12.2 %slice-start.5 = ((s8[5636096]{0:T(1024)(128)(4,1)}), s8[4194304]{0:T(1024)(128)(4,1)S(1)}, s32[]{:S(2)}) async-start(s8[5636096]{0:T(1024)(128)(4,1)} %bitcast.79), calls=%async_computation.5 | async-start | bytes 8388608
  425.7 9.0 %slice-start = ((s8[5636096]{0:T(1024)(128)(4,1)}), s8[4194304]{0:T(1024)(128)(4,1)S(1)}, s32[]{:S(2)}) async-start(s8[5636096]{0:T(1024)(128)(4,1)} %bitcast.73), calls=%async_computation | async-start | bytes 8388608
  425.7 9.0 %slice-start.2 = ((s8[5636096]{0:T(1024)(128)(4,1)}), s8[4194304]{0:T(1024)(128)(4,1)S(1)}, s32[]{:S(2)}) async-start(s8[5636096]{0:T(1024)(128)(4,1)} %bitcast.77), calls=%async_computation.2 | async-start | bytes 8388608
  425.7 9.0 %slice-start.1 = ((s8[5636096]{0:T(1024)(128)(4,1)}), s8[1441792]{0:T(1024)(128)(4,1)S(1)}, s32[]{:S(2)}) async-start(s8[5636096]{0:T(1024)(128)(4,1)} %bitcast.73), calls=%async_computation.1 | async-start | bytes 2883584
  425.7 9.0 %slice-start.3 = ((s8[5636096]{0:T(1024)(128)(4,1)}), s8[1441792]{0:T(1024)(128)(4,1)S(1)}, s32[]{:S(2)}) async-start(s8[5636096]{0:T(1024)(128)(4,1)} %bitcast.77), calls=%async_computation.3 | async-start | bytes 2883584
  (17 other events, 42.1 us)

commit v3 on v2

v3 whole, which is shorter than its diff:
```python
import functools
import jax
import jax.numpy as jnp
from jax import lax
from jax.experimental import pallas as pl
from jax.experimental.pallas import tpu as pltpu
from jax.sharding import PartitionSpec as P

D = 1024
HEADS = 16
QK = 16
HV = 64
FF = 2752
STEP = 4
BT = 256
F32 = jnp.float32
BF16 = jnp.bfloat16

MESH = pl.DeviceIdType.MESH
EPS = 1e-06
MOMENTUM = 0.9


def nt(a, b):
    return lax.dot_general(a, b, (((1,), (1,)), ((), ())), preferred_element_type=F32)


def nn(a, b):
    return lax.dot_general(a, b, (((1,), (0,)), ((), ())), preferred_element_type=F32)


def first_start(starts_ref, t):
    begin = jnp.int32(0)
    for n in range(starts_ref.shape[1]):
        begin = jnp.where(starts_ref[0, n] <= t, jnp.maximum(begin, starts_ref[0, n]), begin)
    return begin


def fill_mask(starts_ref, mask_ref, block, low_block):
    t = block * BT + lax.broadcasted_iota(jnp.int32, (BT, 1), 0)
    begin = jnp.zeros((BT, 1), jnp.int32)
    for n in range(starts_ref.shape[1]):
        begin = jnp.where(starts_ref[0, n] <= t, jnp.maximum(begin, starts_ref[0, n]), begin)

    def one(j, carry):
        s = j * BT + lax.broadcasted_iota(jnp.int32, (BT, BT), 1)
        keep = jnp.logical_and(s <= t, s >= begin)
        mask_ref[j] = keep.astype(F32).astype(BF16)
        return carry
    lax.fori_loop(low_block, block + 1, one, 0)


def attn_fwd_kernel(hb, starts_ref, q_ref, k_ref, v_ref, o_ref, rd_ref, mask_ref):
    block = pl.program_id(0)
    low_block = first_start(starts_ref, block * BT) // BT
    fill_mask(starts_ref, mask_ref, block, low_block)
    lane = lax.broadcasted_iota(jnp.int32, (1, 128), 1)

    def group(g, carry):
        qlanes = pl.ds(pl.multiple_of((g * hb) // 8 * 128, 128), 128)
        q = q_ref[:, qlanes]
        qms = []
        for n in range(hb):
            h8 = lax.rem(g * hb + n, 8)
            qms.append(jnp.where(lane // QK == h8, q, jnp.zeros_like(q)))

        def step(j, accs):
            rows = pl.ds(pl.multiple_of(j * BT, BT), BT)
            k = k_ref[rows, qlanes]
            mask = mask_ref[j]
            out = []
            for n in range(hb):
                vl = pl.ds(pl.multiple_of((g * hb + n) // 2 * 128, 128), 128)
                v = v_ref[rows, vl]
                v = jnp.where(lane // HV == n % 2, v, jnp.ones_like(v))
                t1 = nt(qms[n], k) + 1.0
                p = (t1 * t1 + 1.0).astype(BF16) * mask
                out.append(accs[n] + nn(p, v))
            return tuple(out)
        accs = lax.fori_loop(low_block, block + 1, step, tuple(jnp.zeros((BT, 128), F32) for _ in range(hb)))
        for m in range(hb // 2):
            vl = pl.ds(pl.multiple_of((g * hb + 2 * m) // 2 * 128, 128), 128)
            first, second = accs[2 * m], accs[2 * m + 1]
            numer = jnp.where(lane < HV, first, second)
            denom = pltpu.roll(jnp.where(lane < HV, second, first), HV, 1)
            recip = 1.0 / denom
            o_ref[:, vl] = (numer * recip).astype(BF16)
            rd_ref[:, vl] = recip
        return carry
    lax.fori_loop(0, HEADS // hb, group, 0)


def attn_fwd(starts, pairs, v, hb):
    length = pairs.shape[0]
    return pl.pallas_call(
        functools.partial(attn_fwd_kernel, hb),
        grid=(length // BT,),
        out_shape=(jax.ShapeDtypeStruct((length, HEADS * HV), BF16), jax.ShapeDtypeStruct((length, HEADS * HV), F32)),
        in_specs=[pl.BlockSpec(memory_space=pltpu.SMEM), pl.BlockSpec((BT, HEADS * QK), lambda i: (i, 0)),
                  pl.BlockSpec((length, HEADS * QK), lambda i: (0, 1)), pl.BlockSpec((length, HEADS * HV), lambda i: (0, 0))],
        out_specs=(pl.BlockSpec((BT, HEADS * HV), lambda i: (i, 0)), pl.BlockSpec((BT, HEADS * HV), lambda i: (i, 0))),
        scratch_shapes=[pltpu.VMEM((length // BT, BT, BT), BF16)],
        compiler_params=pltpu.CompilerParams(vmem_limit_bytes=40 * 2**20),
        name="mixer",
    )(starts, pairs, pairs, v)


class LineSum:
    def __init__(self, part, leaf, mid, total, send, recv, rows, lags=(0, 2, 4)):
        self.part, self.leaf, self.mid, self.total, self.send, self.recv = part, leaf, mid, total, send, recv
        self.rows, self.lags = rows, lags
        self.count = part.shape[0] // rows
        self.dp, self.f = lax.axis_index("dp"), lax.axis_index("feat")

    def barrier(self):
        sem = pltpu.get_barrier_semaphore()
        dp, f = self.dp, self.f

        @pl.when(f > 0)
        def _():
            pl.semaphore_signal(sem, inc=1, device_id=(dp, f - 1), device_id_type=MESH)

        @pl.when(f < 3)
        def _():
            pl.semaphore_signal(sem, inc=1, device_id=(dp, f + 1), device_id_type=MESH)
        pl.semaphore_wait(sem, jnp.where(f > 0, 1, 0) + jnp.where(f < 3, 1, 0))

    def place(self, c):
        odd = lax.rem(c, 2)
        return self.f + odd * (3 - 2 * self.f), 1 - 2 * odd

    def copy(self, c, src, dst, kind, slot, to):
        at = pl.ds(pl.multiple_of(c * self.rows, self.rows), self.rows)
        return pltpu.make_async_remote_copy(
            src_ref=src.at[at], dst_ref=dst.at[at], send_sem=self.send.at[slot, c], recv_sem=self.recv.at[kind, c],
            device_id=(self.dp, to), device_id_type=MESH)

    def leaves(self, c):
        p, up = self.place(c)

        @pl.when(p == 3)
        def _():
            self.copy(c, self.part, self.leaf, 0, 0, self.f - up).start()

        @pl.when(p == 0)
        def _():
            self.copy(c, self.part, self.leaf, 0, 0, self.f + up).start()

    def middle(self, c):
        p, up = self.place(c)
        at = pl.ds(pl.multiple_of(c * self.rows, self.rows), self.rows)

        @pl.when(p == 2)
        def _():
            self.copy(c, self.part, self.leaf, 0, 0, self.f).wait_recv()
            self.part[at, :] = (self.part[at, :].astype(F32) + self.leaf[at, :].astype(F32)).astype(BF16)
            self.copy(c, self.part, self.mid, 1, 0, self.f - up).start()

    def root(self, c):
        p, up = self.place(c)
        at = pl.ds(pl.multiple_of(c * self.rows, self.rows), self.rows)

        @pl.when(p == 1)
        def _():
            self.copy(c, self.part, self.leaf, 0, 0, self.f).wait_recv()
            self.copy(c, self.part, self.mid, 1, 0, self.f).wait_recv()
            self.total[at, :] = (
                self.part[at, :].astype(F32) + self.leaf[at, :].astype(F32) + self.mid[at, :].astype(F32)
            ).astype(BF16)
            self.copy(c, self.total, self.total, 2, 1, self.f + up).start()
            self.copy(c, self.total, self.total, 2, 0, self.f - up).start()

    def onward(self, c):
        p, up = self.place(c)

        @pl.when(p == 2)
        def _():
            self.copy(c, self.total, self.total, 2, 0, self.f).wait_recv()
            self.copy(c, self.total, self.total, 2, 1, self.f + up).start()

    def serve(self, i):
        for lag, act in zip(self.lags, (self.middle, self.root, self.onward)):
            c = i - lag

            @pl.when(jnp.logical_and(c >= 0, c < self.count))
            def _():
                act(c)

    def steps(self):
        return self.count + self.lags[-1]

    def arrived(self, c):
        p, up = self.place(c)

        @pl.when(jnp.logical_or(p == 0, p == 3))
        def _():
            self.copy(c, self.total, self.total, 2, 0, self.f).wait_recv()

    def drain(self, c):
        p, up = self.place(c)
        self.copy(c, self.part, self.part, 0, 0, self.f).wait_send()

        @pl.when(jnp.logical_or(p == 1, p == 2))
        def _():
            self.copy(c, self.part, self.part, 0, 1, self.f).wait_send()


class CubeSum:
    def __init__(self, work, recv, out, send_sem, recv_sem, pieces, bits):
        self.work, self.recv, self.out, self.send_sem, self.recv_sem = work, recv, out, send_sem, recv_sem
        self.pieces, self.nb = pieces, len(bits)
        self.dp, self.f = lax.axis_index("dp"), lax.axis_index("feat")
        self.orders = [list(bits), [bits[0]] + list(bits[1:])[::-1]]
        self.bits = bits

    def partner(self, bit):
        return self.dp + bit - 2 * bit * lax.rem(self.dp // bit, 2)

    def barrier(self):
        sem = pltpu.get_barrier_semaphore()
        for bit in self.bits:
            pl.semaphore_signal(sem, inc=1, device_id=(self.partner(bit), self.f), device_id_type=MESH)
        pl.semaphore_wait(sem, len(self.bits))

    def lanes(self, colour):
        half = self.work.shape[1] // 2
        return pl.ds(colour * half, half)

    def segment(self, piece, colour, k):
        first, rows = self.pieces[piece]
        start = first
        for bit in self.orders[colour][:k]:
            rows = rows // 2
            start = start + rows * lax.rem(self.dp // bit, 2)
        return start, rows

    def at(self, start, rows):
        return pl.ds(pl.multiple_of(start, 16), rows)

    def halve(self, piece, colour, k):
        start, rows = self.segment(piece, colour, k)
        rows = rows // 2
        bit = self.orders[colour][k]
        own = lax.rem(self.dp // bit, 2)
        first, whole = self.pieces[piece]
        landing = first + whole - 2 * rows
        return pltpu.make_async_remote_copy(
            src_ref=self.work.at[self.at(start + rows * (1 - own), rows), self.lanes(colour)],
            dst_ref=self.recv.at[self.at(landing, rows), self.lanes(colour)],
            send_sem=self.send_sem.at[piece, colour, k], recv_sem=self.recv_sem.at[piece, colour, k],
            device_id=(self.partner(bit), self.f), device_id_type=MESH)

    def add(self, piece, colour, k):
        start, rows = self.segment(piece, colour, k + 1)
        first, whole = self.pieces[piece]
        landing = first + whole - 2 * rows
        target = self.out if k + 1 == self.nb else self.work
        mine = self.work[self.at(start, rows), self.lanes(colour)].astype(F32)
        target[self.at(start, rows), self.lanes(colour)] = (
            mine + self.recv[self.at(landing, rows), self.lanes(colour)].astype(F32)
        ).astype(BF16)

    def double(self, piece, colour, k):
        start, rows = self.segment(piece, colour, k + 1)
        bit = self.orders[colour][k]
        at = self.at(start, rows)
        slot = 2 * self.nb - 1 - k
        return pltpu.make_async_remote_copy(
            src_ref=self.out.at[at, self.lanes(colour)], dst_ref=self.out.at[at, self.lanes(colour)],
            send_sem=self.send_sem.at[piece, colour, slot], recv_sem=self.recv_sem.at[piece, colour, slot],
            device_id=(self.partner(bit), self.f), device_id_type=MESH)

    def launch(self, piece):
        for colour in range(2):
            self.halve(piece, colour, 0).start()

    def advance(self, piece, t):
        for colour in range(2):
            if t < self.nb:
                self.halve(piece, colour, t).wait_recv()
                self.add(piece, colour, t)
                if t + 1 < self.nb:
                    self.halve(piece, colour, t + 1).start()
                else:
                    self.double(piece, colour, self.nb - 1).start()
            else:
                k = 2 * self.nb - 1 - t
                self.double(piece, colour, k).wait_recv()
                if k > 0:
                    self.double(piece, colour, k - 1).start()

    def drain(self, piece):
        for colour in range(2):
            for k in range(self.nb):
                self.halve(piece, colour, k).wait_send()
                self.double(piece, colour, k).wait_send()


def split_rows(rows, unit, count):
    units = rows // unit
    out, first = [], 0
    for n in range(count):
        take = (units * (n + 1) // count - units * n // count) * unit
        out.append((first, take))
        first += take
    return [p for p in out if p[1]]


def project_kernel(
    bits, tokens_in, gains_ref, pair_ref, value_ref, out_ref, gate_in, down_in,
    normed_ref, pairs_ref, values_ref, wide_ref, gate_ref, down_ref,
    all_ref, tokens_ref, gate_f32, down_f32, send_sem, recv_sem, load_sem,
):
    dp = lax.axis_index("dp")
    f = lax.axis_index("feat")
    last = lax.axis_size("feat") - 1
    slices = lax.axis_size("feat")
    pieces = 2 ** len(bits)
    j = lax.rem(dp, pieces)
    base = dp - j
    pair_cols, value_cols = pair_ref.shape[1], value_ref.shape[1]
    rows = pair_ref.shape[0] // pieces
    length = tokens_ref.shape[0]
    loads = [
        pltpu.make_async_copy(a, b, load_sem.at[n])
        for n, (a, b) in enumerate([(tokens_in, tokens_ref), (gate_in, gate_f32), (down_in, down_f32)])
    ]
    for load in loads:
        load.start()

    def flip(k, bit):
        return k + bit - 2 * bit * lax.rem(k // bit, 2)

    def cast(k):
        at = pl.ds(pl.multiple_of(k * rows, rows), rows)
        block = jnp.concatenate(
            [pair_ref[at, :].astype(BF16), value_ref[at, :].astype(BF16), out_ref[:, at].T.astype(BF16)], axis=1
        )
        all_ref[f, k, 0] = block[: rows // 2]
        all_ref[f, k, 1] = block[rows // 2 :]

    cast(j)
    barrier = pltpu.get_barrier_semaphore()
    for bit in bits:
        pl.semaphore_signal(barrier, inc=1, device_id=(base + flip(j, bit), f), device_id_type=MESH)

    @pl.when(f > 0)
    def _():
        pl.semaphore_signal(barrier, inc=1, device_id=(dp, f - 1), device_id_type=MESH)

    @pl.when(f < last)
    def _():
        pl.semaphore_signal(barrier, inc=1, device_id=(dp, f + 1), device_id_type=MESH)

    pl.semaphore_wait(barrier, len(bits) + jnp.where(f > 0, 1, 0) + jnp.where(f < last, 1, 0))

    def copy(z, colour, k, slot, device):
        return pltpu.make_async_remote_copy(
            src_ref=all_ref.at[z, k, colour], dst_ref=all_ref.at[z, k, colour], send_sem=send_sem.at[z, colour, slot],
            recv_sem=recv_sem.at[z, colour, k], device_id=device, device_id_type=MESH,
        )

    here = (dp, f)
    for colour in range(2):
        @pl.when(f > 0)
        def _():
            copy(f, colour, j, 0, (dp, f - 1)).start()

        @pl.when(f < last)
        def _():
            copy(f, colour, j, 1, (dp, f + 1)).start()

    order = [
        jnp.where(f == 0, 1, f - 1),
        jnp.where(f < 2, 2, jnp.where(f == 2, 3, 1)),
        jnp.where(f < 2, 3, 0),
    ]
    colour_bits = [list(bits[1:]) + [bits[0]], list(bits[1:])[::-1] + [bits[0]]]

    def held(colour, step):
        out = [j]
        for bit in colour_bits[colour][:step]:
            out = out + [flip(k, bit) for k in out]
        return out

    def start_step(z, step):
        for colour in range(2):
            first = 2 + 2**step - 1
            partner = (base + flip(j, colour_bits[colour][step]), f)
            for n, k in enumerate(held(colour, step)):
                copy(z, colour, k, first + n, partner).start()

    def wait_step(z, step):
        for colour in range(2):
            for k in held(colour, step):
                copy(z, colour, flip(k, colour_bits[colour][step]), 0, here).wait_recv()

    def arrive(z):
        ahead = jnp.where(z < f, f + 1, f - 1)
        onward = jnp.logical_and(ahead >= 0, ahead <= last)
        for colour in range(2):
            copy(z, colour, j, 0, here).wait_recv()

            @pl.when(onward)
            def _():
                copy(z, colour, j, jnp.where(z < f, 1, 0), (dp, ahead)).start()
        start_step(z, 0)

    half_pairs = slices * pair_cols // 2
    pairs_wide, values_wide = slices * pair_cols, slices * value_cols

    def use(z):
        weight = all_ref[z].reshape(pieces * rows, pair_cols + 2 * value_cols)
        pair_at = pl.ds(pl.multiple_of(z * pair_cols, pair_cols), pair_cols)
        value_at = pl.ds(pl.multiple_of(z * value_cols, value_cols), value_cols)
        wide_ref[:, pair_at] = weight[:, :pair_cols]
        wide_ref[:, pl.ds(pl.multiple_of(pairs_wide + z * value_cols, 128), value_cols)] = weight[
            :, pair_cols : pair_cols + value_cols
        ]
        wide_ref[:, pl.ds(pl.multiple_of(pairs_wide + values_wide + z * value_cols, 128), value_cols)] = weight[
            :, pair_cols + value_cols :
        ]
        factor = jnp.where(z * pair_cols < half_pairs, 0.25, 1.0).astype(F32)

        def some(n, carry):
            at = pl.ds(pl.multiple_of(n * BT, BT), BT)
            normed = normed_ref[at, :]
            pairs = nn(normed, wide_ref[:, pair_at])
            pairs_ref[at, pair_at] = (pairs.astype(BF16).astype(F32) * factor).astype(BF16)
            values_ref[at, value_at] = nn(
                normed, wide_ref[:, pl.ds(pl.multiple_of(pairs_wide + z * value_cols, 128), value_cols)]
            ).astype(BF16)
            return carry

        lax.fori_loop(0, length // BT, some, 0)

    def cast_rest(n, carry):
        cast(lax.rem(j + n, pieces))
        return carry

    lax.fori_loop(1, pieces, cast_rest, 0)
    loads[0].wait()

    def norm(n, carry):
        at = pl.ds(pl.multiple_of(n * BT, BT), BT)
        x = tokens_ref[at, :].astype(F32)
        scale = lax.rsqrt(jnp.mean(x * x, axis=1, keepdims=True) + EPS)
        normed_ref[at, :] = (x * scale * gains_ref[0:1, :]).astype(BF16)
        return carry

    lax.fori_loop(0, length // BT, norm, 0)

    steps = len(bits)
    arrive(order[0])
    use(f)
    loads[1].wait()
    loads[2].wait()

    def cast_gate(n):
        def go(m, carry):
            gate_ref[n, pl.ds(pl.multiple_of(m * 16, 16), 16), :] = gate_f32[
                n, pl.ds(pl.multiple_of(m * 16, 16), 16), :
            ].astype(BF16)
            return carry

        lax.fori_loop(0, gate_f32.shape[1] // 16, go, 0)

    def cast_down(m, carry):
        down_ref[pl.ds(pl.multiple_of(m * 16, 16), 16), :] = down_f32[pl.ds(pl.multiple_of(m * 16, 16), 16), :].astype(BF16)
        return carry

    plan = [(1, None), (0, 0), "gate", (2, None), (1, 0), (0, 1), "up", (2, 0), (1, 1), (0, 2), "down", (2, 1), (1, 2), (2, 2)]
    for item in plan:
        if item == "gate":
            cast_gate(0)
        elif item == "up":
            cast_gate(1)
        elif item == "down":
            lax.fori_loop(0, down_f32.shape[0] // 16, cast_down, 0)
        elif item[1] is None:
            arrive(order[item[0]])
        else:
            wait_step(order[item[0]], item[1])
            if item[1] + 1 < steps:
                start_step(order[item[0]], item[1] + 1)
            else:
                use(order[item[0]])
    for z in order:
        ahead = jnp.where(z < f, f + 1, f - 1)
        onward = jnp.logical_and(ahead >= 0, ahead <= last)
        for colour in range(2):
            @pl.when(onward)
            def _():
                copy(z, colour, j, jnp.where(z < f, 1, 0), here).wait_send()

            for step in range(steps):
                for n, k in enumerate(held(colour, step)):
                    copy(z, colour, k, 2 + 2**step - 1 + n, here).wait_send()
    for colour in range(2):
        @pl.when(f > 0)
        def _():
            copy(f, colour, j, 0, here).wait_send()

        @pl.when(f < last)
        def _():
            copy(f, colour, j, 1, here).wait_send()


def project(tokens, gains, pair_w, value_w, out_w, gate_turned, down):
    length = tokens.shape[0]
    ff = down.shape[0]
    slices = 4
    pair_cols, value_cols = pair_w.shape[1], value_w.shape[1]
    cols = pair_cols + 2 * value_cols
    bits = (1, 2, 4)
    hbm = pl.BlockSpec(memory_space=pl.ANY)
    vmem = pl.BlockSpec(memory_space=pltpu.VMEM)
    return pl.pallas_call(
        functools.partial(project_kernel, bits),
        out_shape=(
            jax.ShapeDtypeStruct((length, D), BF16),
            jax.ShapeDtypeStruct((length, slices * pair_cols), BF16),
            jax.ShapeDtypeStruct((length, slices * value_cols), BF16),
            jax.ShapeDtypeStruct((D, slices * cols), BF16),
            jax.ShapeDtypeStruct((2, ff, D), BF16),
            jax.ShapeDtypeStruct((ff, D), BF16),
        ),
        in_specs=[hbm] + [vmem] * 4 + [hbm] * 2,
        out_specs=(vmem,) * 6,
        scratch_shapes=[
            pltpu.VMEM((slices, 8, 2, D // 16, cols), BF16),
            pltpu.VMEM((length, D), BF16),
            pltpu.VMEM((2, ff, D), F32),
            pltpu.VMEM((ff, D), F32),
            pltpu.SemaphoreType.DMA((slices, 2, 9)),
            pltpu.SemaphoreType.DMA((slices, 2, 8)),
            pltpu.SemaphoreType.DMA((3,)),
        ],
        compiler_params=pltpu.CompilerParams(collective_id=1, has_side_effects=True, vmem_limit_bytes=56 * 2**20),
        name="project",
    )(tokens, gains, pair_w, value_w, out_w, gate_turned, down)


def feed_kernel(
    rows, tokens_in, cot_in, attn_in, wide_in, gate_in, down_in, gains_ref,
    hidden_out, grad_hidden_out, ga_ref, ffn_ref, grads_ref,
    tokens_ref, cot_ref, attn_ref, out_w, gate_ref, down_ref,
    hidden_ref, scale_ref, normed_ref, product_t, gate_t, up_t, own_t, gain_ref, gh_ref,
    part, leaf, mid, total, send, recv, load_sem, store_sem,
):
    f = lax.axis_index("feat")
    line = LineSum(part, leaf, mid, total, send, recv, rows, (0, 3, 6))
    length = tokens_ref.shape[0]
    ff = down_ref.shape[0]
    value_cols = own_t.shape[0]
    blocks = length // BT
    first_out = wide_in.shape[1] - attn_ref.shape[1]
    pairs = [(attn_in, attn_ref), (wide_in.at[:, pl.ds(first_out, attn_ref.shape[1])], out_w), (tokens_in, tokens_ref),
             (gate_in, gate_ref), (down_in, down_ref), (cot_in, cot_ref)]
    loads = [pltpu.make_async_copy(a, b, load_sem.at[n]) for n, (a, b) in enumerate(pairs)]
    for load in loads:
        load.start()
    greet(line, None)
    for load in loads:
        load.wait()

    def store(source, target, n, kind):
        at = pl.ds(pl.multiple_of(n * BT, BT), BT)
        return pltpu.make_async_copy(source.at[at], target.at[at], store_sem.at[kind, n])

    def block(b, carry):
        at = pl.ds(pl.multiple_of(b * BT, BT), BT)
        turn = 4 * (b - 1)
        hidden = tokens_ref[at, :].astype(F32) + nt(attn_ref[at, :], out_w[...])
        hidden_ref[at, :] = hidden
        store(hidden_ref, hidden_out, b, 0).start()
        scale = lax.rsqrt(jnp.mean(hidden * hidden, axis=1, keepdims=True) + EPS)
        scale_ref[at, :] = jnp.broadcast_to(scale, (BT, 128))
        normed = (hidden * scale * gains_ref[1:2, :]).astype(BF16)
        normed_ref[at, :] = normed
        line.serve(turn)
        gate = nt(normed, gate_ref[0])
        up = nt(normed, gate_ref[1])
        line.serve(turn + 1)
        back = nt(cot_ref[at, :], down_ref[...])
        sig = 1.0 / (1.0 + jnp.exp(-gate))
        active = gate * sig
        slope = sig * (1.0 + gate * (1.0 - sig))
        product = (active * up).astype(BF16)
        grad_gate = (back * up * slope).astype(BF16)
        grad_up = (back * active).astype(BF16)
        line.serve(turn + 2)
        part[at, :] = (nn(grad_gate, gate_ref[0]) + nn(grad_up, gate_ref[1])).astype(BF16)

        def out(c, carry):
            line.leaves(b * (BT // rows) + c)
            return carry

        lax.fori_loop(0, BT // rows, out, 0)
        ffn_ref[at, :] = nn(product, down_ref[...]).astype(BF16)
        product_t[:, at] = product.T
        gate_t[:, at] = grad_gate.T
        up_t[:, at] = grad_up.T
        line.serve(turn + 3)
        return carry

    lax.fori_loop(0, blocks, block, 0)
    served = 4 * (blocks - 1)
    gain_ref[...] = jnp.zeros_like(gain_ref)
    chunks = []
    at = 0
    while at < ff:
        chunks.append((at, min(176, ff - at)))
        at += chunks[-1][1]
    for n, (turned, right) in enumerate([(product_t, cot_ref), (gate_t, normed_ref), (up_t, normed_ref)]):
        for first, size in chunks:
            grads_ref[n * ff + first : n * ff + first + size, :] = nn(turned[first : first + size, :], right[...]).astype(BF16)
            line.serve(jnp.int32(served))
            served += 1
    own_t[...] = own_column(attn_ref, f, value_cols).T

    def back_rows(n):
        at = pl.ds(pl.multiple_of(n * BT, BT), BT)
        hidden, grad = hidden_ref[at, :], total[at, :].astype(F32)
        scale = scale_ref[at, 0:1]
        unit = hidden * scale
        u = grad * gains_ref[1:2, :]
        gh = cot_ref[at, :].astype(F32) + scale * (u - unit * jnp.mean(u * unit, axis=1, keepdims=True))
        gh_ref[at, :] = gh
        store(gh_ref, grad_hidden_out, n, 1).start()
        ga_ref[at, :] = gh.astype(BF16)
        gain_ref[0:1, :] += jnp.sum(grad * unit, axis=0, keepdims=True)

    per = BT // rows
    for n in range(blocks):
        until = min(per * (n + 1) + line.lags[-1], line.steps())

        def more(i, carry):
            line.serve(i)
            return carry

        lax.fori_loop(min(served, until), until, more, 0)
        served = max(served, until)
        lax.fori_loop(per * n, per * (n + 1), lambda c, carry: (line.arrived(c), carry)[1], 0)
        back_rows(jnp.int32(n))
    first = 3 * ff
    grads_ref[first : first + value_cols, :] = nn(own_t[...], ga_ref[...]).astype(BF16)
    first = first + value_cols
    rest = grads_ref.shape[0] - first
    grads_ref[first:, :] = jnp.zeros((rest, D), BF16)
    grads_ref[first : first + 16, :] = gain_ref[...].astype(BF16)
    each(line.drain, line.count)
    for n in range(blocks):
        store(hidden_ref, hidden_out, jnp.int32(n), 0).wait()
        store(gh_ref, grad_hidden_out, jnp.int32(n), 1).wait()


def feed(tokens, cotangent, attn, wide, gate_turned, down, gains, padded):
    length = tokens.shape[0]
    ff = down.shape[0]
    nv, rows = attn.shape[1], 32
    count = length // rows
    hbm = pl.BlockSpec(memory_space=pl.ANY)
    vmem = pl.BlockSpec(memory_space=pltpu.VMEM)
    return pl.pallas_call(
        functools.partial(feed_kernel, rows),
        out_shape=(
            jax.ShapeDtypeStruct((length, D), F32),
            jax.ShapeDtypeStruct((length, D), F32),
            jax.ShapeDtypeStruct((length, D), BF16),
            jax.ShapeDtypeStruct((length, D), BF16),
            jax.ShapeDtypeStruct((padded, D), BF16),
        ),
        in_specs=[hbm] * 6 + [vmem],
        out_specs=(hbm, hbm, vmem, vmem, vmem),
        scratch_shapes=[
            pltpu.VMEM((length, D), BF16), pltpu.VMEM((length, D), BF16), pltpu.VMEM((length, nv), BF16),
            pltpu.VMEM((D, nv), BF16), pltpu.VMEM((2, ff, D), BF16), pltpu.VMEM((ff, D), BF16),
            pltpu.VMEM((length, D), F32), pltpu.VMEM((length, 128), F32), pltpu.VMEM((length, D), BF16),
            pltpu.VMEM((ff, length), BF16), pltpu.VMEM((ff, length), BF16), pltpu.VMEM((ff, length), BF16),
            pltpu.VMEM((nv // 4, length), BF16), pltpu.VMEM((16, D), F32), pltpu.VMEM((length, D), F32),
            pltpu.VMEM((length, D), BF16), pltpu.VMEM((length, D), BF16), pltpu.VMEM((length, D), BF16),
            pltpu.VMEM((length, D), BF16),
            pltpu.SemaphoreType.DMA((2, count)), pltpu.SemaphoreType.DMA((3, count)),
            pltpu.SemaphoreType.DMA((6,)), pltpu.SemaphoreType.DMA((2, length // BT)),
        ],
        compiler_params=pltpu.CompilerParams(collective_id=2, has_side_effects=True, vmem_limit_bytes=60 * 2**20),
        name="feed",
    )(tokens, cotangent, attn, wide, gate_turned, down, gains)


def own_column(ref, f, width):
    return ref[:, pl.ds(pl.multiple_of(f * width, width), width)]


def mixer_back_kernel(
    pieces, bits, hb, rows,
    starts_ref, pairs_in, v_in, attn_in, rd_in, ga_in, wide_in, ffn_in, grads_in,
    gp_ref, gv_ref, total_ref, sums_ref,
    q_ref, k_ref, v_ref, attn_ref, rd_ref, ga_ref, out_ref,
    part, leaf, mid, work, landing,
    mask_ref, gn_ref, gd_ref, qt_ref, gnt_ref, gq_ref, gkt_ref, gvt_ref,
    line_send, line_recv, cube_send, cube_recv, load_sem,
):
    f = lax.axis_index("feat")
    line = LineSum(part, leaf, mid, total_ref, line_send, line_recv, rows, (0, 3, 6))
    cube = CubeSum(work, landing, sums_ref, cube_send, cube_recv, pieces, bits)
    pairs = [(grads_in, work), (ffn_in, part), (ga_in, ga_ref), (wide_in.at[:, pl.ds(wide_in.shape[1] - out_ref.shape[1], out_ref.shape[1])], out_ref), (rd_in, rd_ref), (attn_in, attn_ref),
             (pairs_in.at[:, pl.ds(0, HEADS * QK)], q_ref), (pairs_in.at[:, pl.ds(HEADS * QK, HEADS * QK)], k_ref), (v_in, v_ref)]
    loads = [pltpu.make_async_copy(a, b, load_sem.at[n]) for n, (a, b) in enumerate(pairs)]
    for load in loads:
        load.start()
    greet(line, cube)
    loads[0].wait()
    for p in range(len(pieces)):
        cube.launch(p)
    loads[1].wait()
    each(line.leaves, line.count)
    gkt_ref[...] = jnp.zeros_like(gkt_ref)
    gvt_ref[...] = jnp.zeros_like(gvt_ref)
    for load in loads[2:]:
        load.wait()

    lane = lax.broadcasted_iota(jnp.int32, (1, 128), 1)
    blocks = q_ref.shape[0] // BT
    groups = HEADS // hb

    def at_block(n):
        return pl.ds(pl.multiple_of(n * BT, BT), BT)

    def prepare(i):
        here = at_block(i)
        qt_ref[...] = q_ref[here, :].T
        gq_ref[...] = jnp.zeros_like(gq_ref)

        def one(m, carry):
            vl = pl.ds(pl.multiple_of(m * 128, 128), 128)
            grad_attn = nn(ga_ref[here, :], out_ref[:, vl])
            grad_numer = grad_attn * (2.0 * rd_ref[here, vl])
            both = grad_numer * attn_ref[here, vl].astype(F32)
            first = jnp.sum(jnp.where(lane < HV, both, 0.0), axis=1, keepdims=True)
            second = jnp.sum(jnp.where(lane < HV, 0.0, both), axis=1, keepdims=True)
            gd_ref[:, vl] = jnp.where(lane < HV, -second, -first).astype(BF16)
            low = grad_numer.astype(BF16)
            gn_ref[:, vl] = low
            gnt_ref[vl, :] = low.T
            return carry

        lax.fori_loop(0, HEADS // 2, one, 0)

    def make_mask(i, j):
        t = i * BT + lax.broadcasted_iota(jnp.int32, (BT, 1), 0)
        begin = jnp.zeros((BT, 1), jnp.int32)
        for n in range(starts_ref.shape[1]):
            begin = jnp.where(starts_ref[0, n] <= t, jnp.maximum(begin, starts_ref[0, n]), begin)
        s = j * BT + lax.broadcasted_iota(jnp.int32, (BT, BT), 1)
        mask_ref[...] = jnp.logical_and(s <= t, s >= begin).astype(F32).astype(BF16)

    steps = blocks * (blocks + 1) // 2 * groups
    sequence = [(p, t) for t in range(2 * cube.nb) for p in range(len(pieces))]
    slots = {}
    for n, item in enumerate(sequence):
        slots.setdefault(min(steps - 1, 2 + n * (steps - 4) // len(sequence)), []).append(item)

    def step(n, carry):
        m, g = n // groups, lax.rem(n, groups)
        i = jnp.int32(0)
        for b in range(1, blocks):
            i = i + jnp.where(m >= b * (b + 1) // 2, 1, 0)
        j = m - i * (i + 1) // 2

        @pl.when(jnp.logical_and(g == 0, j == 0))
        def _():
            prepare(i)

        @pl.when(g == 0)
        def _():
            make_mask(i, j)

        here, there = at_block(i), at_block(j)
        first = g * hb
        qlanes = pl.ds(pl.multiple_of(first // 8 * 128, 128), 128)
        q = q_ref[here, qlanes]
        k = k_ref[there, qlanes]
        mask = mask_ref[...]
        gq = jnp.zeros((BT, 128), F32)
        for a in range(hb):
            h = first + a
            own_lanes = lane // QK == lax.rem(h, 8)
            vl = pl.ds(pl.multiple_of(h // 2 * 128, 128), 128)
            gn = jnp.where(lane // HV == a % 2, gn_ref[:, vl], jnp.zeros((BT, 128), BF16))
            gn = jnp.where(lane == HV * (1 - a % 2), gd_ref[:, vl], gn)
            v = v_ref[there, vl]
            v = jnp.where(lane // HV == a % 2, v, jnp.ones_like(v))
            t1 = nt(jnp.where(own_lanes, q, jnp.zeros_like(q)), k) + 1.0
            p = (t1 * t1 + 1.0).astype(BF16) * mask
            dp = nt(gn, v).astype(BF16) * mask
            gs = (dp.astype(F32) * t1).astype(BF16)
            gq = gq + nn(gs, jnp.where(own_lanes, k, jnp.zeros_like(k)))
            qrows = pl.ds(pl.multiple_of(h * QK, QK), QK)
            vrows = pl.ds(pl.multiple_of(h * HV, HV), HV)
            gkt_ref[qrows, there] += nn(qt_ref[qrows, :], gs)
            gvt_ref[vrows, there] += nn(gnt_ref[vrows, :], p)
        gq_ref[:, qlanes] += gq

        @pl.when(jnp.logical_and(g == groups - 1, j == i))
        def _():
            gp_ref[here, : HEADS * QK] = (gq_ref[...] * 0.25).astype(BF16)

        line.serve(n)
        for slot, items in slots.items():
            @pl.when(n == slot)
            def _():
                for p, t in items:
                    cube.advance(p, t)
        return carry

    lax.fori_loop(0, steps, step, 0)
    gp_ref[:, HEADS * QK :] = gkt_ref[...].T.astype(BF16)

    def turn(m, carry):
        vl = pl.ds(pl.multiple_of(m * 128, 128), 128)
        gv_ref[:, vl] = (gvt_ref[vl, :] * 0.5).T.astype(BF16)
        return carry

    lax.fori_loop(0, HEADS // 2, turn, 0)
    for n in range(steps, line.steps()):
        line.serve(jnp.int32(n))
    each(line.arrived, line.count)
    each(line.drain, line.count)
    for p in range(len(pieces)):
        cube.drain(p)


def greet(line, cube):
    sem = pltpu.get_barrier_semaphore()
    f = lax.axis_index("feat")
    count = jnp.int32(0)
    if cube is not None:
        for bit in cube.bits:
            pl.semaphore_signal(sem, inc=1, device_id=(cube.partner(bit), f), device_id_type=MESH)
        count = count + len(cube.bits)
    if line is not None:
        @pl.when(f > 0)
        def _():
            pl.semaphore_signal(sem, inc=1, device_id=(line.dp, f - 1), device_id_type=MESH)

        @pl.when(f < 3)
        def _():
            pl.semaphore_signal(sem, inc=1, device_id=(line.dp, f + 1), device_id_type=MESH)
        count = count + jnp.where(f > 0, 1, 0) + jnp.where(f < 3, 1, 0)
    pl.semaphore_wait(sem, count)


def each(act, n):
    def body(c, carry):
        act(c)
        return carry

    lax.fori_loop(0, n, body, 0)


def cube_shape(rows, dp_size, count):
    unit = 16 * dp_size
    padded = (rows + unit - 1) // unit * unit
    bits = tuple(2**n for n in range(dp_size.bit_length() - 1))
    return padded, split_rows(padded, unit, count), bits


def mixer_back(starts, pairs, v, attn, rd, ga, wide, ffn, grads, pieces, bits):
    length = v.shape[0]
    nq, nv, hb, rows = HEADS * QK, HEADS * HV, 4, 32
    count = length // rows
    hbm = pl.BlockSpec(memory_space=pl.ANY)
    vmem = pl.BlockSpec(memory_space=pltpu.VMEM)
    return pl.pallas_call(
        functools.partial(mixer_back_kernel, pieces, bits, hb, rows),
        out_shape=(
            jax.ShapeDtypeStruct((length, 2 * nq), BF16),
            jax.ShapeDtypeStruct((length, nv), BF16),
            jax.ShapeDtypeStruct((length, D), BF16),
            jax.ShapeDtypeStruct(grads.shape, BF16),
        ),
        in_specs=[pl.BlockSpec(memory_space=pltpu.SMEM)] + [hbm] * 8,
        out_specs=(vmem,) * 4,
        scratch_shapes=[
            pltpu.VMEM((length, nq), BF16), pltpu.VMEM((length, nq), BF16), pltpu.VMEM((length, nv), BF16),
            pltpu.VMEM((length, nv), BF16), pltpu.VMEM((length, nv), F32), pltpu.VMEM((length, D), BF16),
            pltpu.VMEM((D, nv), BF16),
            pltpu.VMEM((length, D), BF16), pltpu.VMEM((length, D), BF16), pltpu.VMEM((length, D), BF16),
            pltpu.VMEM(grads.shape, BF16), pltpu.VMEM(grads.shape, BF16),
            pltpu.VMEM((BT, BT), BF16), pltpu.VMEM((BT, nv), BF16), pltpu.VMEM((BT, nv), BF16),
            pltpu.VMEM((nq, BT), BF16), pltpu.VMEM((nv, BT), BF16), pltpu.VMEM((BT, nq), F32),
            pltpu.VMEM((nq, length), F32), pltpu.VMEM((nv, length), F32),
            pltpu.SemaphoreType.DMA((2, count)), pltpu.SemaphoreType.DMA((3, count)),
            pltpu.SemaphoreType.DMA((len(pieces), 2, 2 * len(bits))), pltpu.SemaphoreType.DMA((len(pieces), 2, 2 * len(bits))),
            pltpu.SemaphoreType.DMA((9,)),
        ],
        compiler_params=pltpu.CompilerParams(collective_id=4, has_side_effects=True, vmem_limit_bytes=60 * 2**20),
        name="mixer_back",
    )(starts, pairs, v, attn, rd, ga, wide, ffn, grads)


def project_back_kernel(
    pieces, bits, gp_ref, gv_ref, normed_ref, wide_ref, tokens_ref,
    gn_ref, sums_ref, work, landing, gain_ref, send, recv,
):
    f = lax.axis_index("feat")
    cube = CubeSum(work, landing, sums_ref, send, recv, pieces, bits)
    length = gp_ref.shape[0]
    pair_cols, value_cols = 2 * HEADS * QK // 4, HEADS * HV // 4
    own_values = own_column(gv_ref, f, value_cols).T
    work[0:value_cols, :] = nn(own_values, normed_ref[...]).astype(BF16)
    greet(None, cube)
    cube.launch(0)
    own_pairs = own_column(gp_ref, f, pair_cols).T
    work[value_cols : value_cols + pair_cols, :] = nn(own_pairs, normed_ref[...]).astype(BF16)
    gain_ref[...] = jnp.zeros_like(gain_ref)

    def rows(n, carry):
        at = pl.ds(pl.multiple_of(n * BT, BT), BT)
        grad = nt(gp_ref[at, :], wide_ref[:, : gp_ref.shape[1]]) + nt(
            gv_ref[at, :], wide_ref[:, gp_ref.shape[1] : gp_ref.shape[1] + gv_ref.shape[1]]
        )
        gn_ref[at, :] = grad.astype(BF16)
        x = tokens_ref[at, :].astype(F32)
        scale = lax.rsqrt(jnp.mean(x * x, axis=1, keepdims=True) + EPS)
        gain_ref[0:1, :] += jnp.sum(grad * (x * scale), axis=0, keepdims=True)
        return carry

    lax.fori_loop(0, length // BT, rows, 0)
    rest = value_cols + pair_cols
    work[rest:, :] = jnp.zeros((work.shape[0] - rest, D), BF16)
    work[rest : rest + 16, :] = gain_ref[...].astype(BF16)
    for p in range(1, len(pieces)):
        cube.launch(p)
    for t in range(2 * cube.nb):
        for p in range(len(pieces)):
            cube.advance(p, t)
    for p in range(len(pieces)):
        cube.drain(p)


def project_back(gp, gv, normed, wide, tokens, dp_size):
    length = gp.shape[0]
    padded, _, bits = cube_shape(gv.shape[1] // 4 + gp.shape[1] // 4 + 16, dp_size, 1)
    unit = 16 * dp_size
    first = gv.shape[1] // 4 // unit * unit
    pieces = [(0, first), (first, padded - first)] if first else [(0, padded)]
    vmem = pl.BlockSpec(memory_space=pltpu.VMEM)
    return pl.pallas_call(
        functools.partial(project_back_kernel, pieces, bits),
        out_shape=(jax.ShapeDtypeStruct((length, D), BF16), jax.ShapeDtypeStruct((padded, D), BF16)),
        in_specs=[vmem] * 5,
        out_specs=(vmem,) * 2,
        scratch_shapes=[
            pltpu.VMEM((padded, D), BF16), pltpu.VMEM((padded, D), BF16), pltpu.VMEM((16, D), F32),
            pltpu.SemaphoreType.DMA((len(pieces), 2, 2 * len(bits))), pltpu.SemaphoreType.DMA((len(pieces), 2, 2 * len(bits))),
        ],
        compiler_params=pltpu.CompilerParams(collective_id=5, has_side_effects=True, vmem_limit_bytes=50 * 2**20),
        name="project_back",
    )(gp, gv, normed, wide, tokens)


def update_kernel(
    rates,
    down_w, down_m, down_a, gate_w, gate_m, gate_a, out_w, out_m, out_a, value_w, value_m, value_a,
    pair_w, pair_m, pair_a, gain_w, gain_m, gain_a, big, small, hidden, total, grad_hidden, grad_normed, tokens, gains,
    mixed_o, input_o, pair_mo, pair_wo, pair_ao, value_mo, value_wo, value_ao, out_mo, out_wo, out_ao,
    gate_mo, gate_wo, gate_ao, down_mo, down_wo, down_ao, gain_mo, gain_wo, gain_ao,
):
    ff = down_w.shape[0]
    narrow = value_w.shape[1]
    pair_cols = pair_w.shape[1]

    def put(index, outs, grad, w, m, a, rate):
        moment_next, weight_next, average_next = update(w[index], grad, m[index], a[index], rate)
        outs[0][index], outs[1][index], outs[2][index] = moment_next, weight_next, average_next

    put(..., (down_mo, down_wo, down_ao), big[:ff, :].astype(F32), down_w, down_m, down_a, rates[4])
    for n in range(2):
        first = (n + 1) * ff
        put(n, (gate_mo, gate_wo, gate_ao), big[first : first + ff, :].astype(F32), gate_w, gate_m, gate_a, rates[3])
    first = 3 * ff
    put(..., (out_mo, out_wo, out_ao), big[first : first + out_w.shape[0], :].astype(F32), out_w, out_m, out_a, rates[2])
    first = first + out_w.shape[0]
    put(..., (value_mo, value_wo, value_ao), small[:narrow, :].astype(F32).T, value_w, value_m, value_a, rates[1])
    put(..., (pair_mo, pair_wo, pair_ao), small[narrow : narrow + pair_cols, :].astype(F32).T, pair_w, pair_m, pair_a, rates[0])
    gain_one = small[narrow + pair_cols : narrow + pair_cols + 16, :].astype(F32)[0:1, :]
    gain_two = big[first : first + 16, :].astype(F32)[0:1, :]
    put(slice(0, 1), (gain_mo, gain_wo, gain_ao), gain_one, gain_w, gain_m, gain_a, rates[5])
    put(slice(1, 2), (gain_mo, gain_wo, gain_ao), gain_two, gain_w, gain_m, gain_a, rates[5])

    mixed_o[...] = (hidden[...] + total[...].astype(F32)).astype(BF16)
    x = tokens[...].astype(F32)
    scale = lax.rsqrt(jnp.mean(x * x, axis=1, keepdims=True) + EPS)
    unit = x * scale
    u = grad_normed[...].astype(F32) * gains[0:1, :]
    input_o[...] = grad_hidden[...] + scale * (u - unit * jnp.mean(u * unit, axis=1, keepdims=True))


def finish(rates, weights, big, small, hidden, total, grad_hidden, grad_normed, tokens, gains):
    length = tokens.shape[0]
    steps = D // 128
    rows = length // steps
    ff = weights[0][0].shape[0]
    narrow, pair_cols = weights[3][0].shape[1], weights[4][0].shape[1]

    def cols(n):
        return pl.BlockSpec((n, 128), lambda i: (0, i))

    def tall(n):
        return pl.BlockSpec((128, n), lambda i: (i, 0))

    token = pl.BlockSpec((rows, D), lambda i: (i, 0))
    specs = [cols(ff), pl.BlockSpec((2, ff, 128), lambda i: (0, 0, i)), cols(weights[2][0].shape[0]), tall(narrow), tall(pair_cols), cols(2)]
    order = [4, 3, 2, 1, 0, 5]
    flat = [a for group in weights for a in group]
    out_shape = [jax.ShapeDtypeStruct((length, D), BF16), jax.ShapeDtypeStruct((length, D), F32)]
    out_specs = [token, token]
    for n in order:
        out_shape += [jax.ShapeDtypeStruct(weights[n][0].shape, F32)] * 3
        out_specs += [specs[n]] * 3
    in_specs = [specs[n] for n in range(6) for _ in range(3)]
    in_specs += [cols(big.shape[0]), cols(small.shape[0])] + [token] * 5 + [pl.BlockSpec((2, D), lambda i: (0, 0))]
    return pl.pallas_call(
        functools.partial(update_kernel, rates),
        grid=(steps,),
        out_shape=out_shape,
        in_specs=in_specs,
        out_specs=out_specs,
        compiler_params=pltpu.CompilerParams(vmem_limit_bytes=50 * 2**20),
        name="finish",
    )(*flat, big, small, hidden, total, grad_hidden, grad_normed, tokens, gains)


def update(weight, grad_total, moment, average, rate):
    moment_next = MOMENTUM * moment + grad_total
    weight_next = weight - rate * (grad_total + MOMENTUM * moment_next)
    average_next = average + (weight_next - average) / STEP
    return (moment_next, weight_next, average_next)


def on_device(
    tokens,
    cotangent,
    doc_starts,
    queries_keys,
    value_weight,
    out_weight,
    gate_up,
    down_weight,
    norm_gains,
    queries_moment,
    value_moment,
    out_moment,
    gate_moment,
    down_moment,
    gains_moment,
    queries_average,
    value_average,
    out_average,
    gate_average,
    down_average,
    gains_average,
):
    total_tokens = float(tokens.shape[0] * lax.axis_size("dp"))
    dp_size = lax.axis_size("dp")
    ff = down_weight.shape[0]
    gate_turned = gate_up.transpose(0, 2, 1)
    normed_one, pairs, values, wide, gate_low, down_low = project(
        tokens, norm_gains, queries_keys, value_weight, out_weight, gate_turned, down_weight
    )
    attn_low, recip = attn_fwd(doc_starts, pairs, values, 8)
    padded, pieces, bits = cube_shape(3 * ff + out_weight.shape[0] + 16, dp_size, 4)
    hidden_one, grad_hidden, grad_attended, ffn_part, big = feed(
        tokens, cotangent, attn_low, wide, gate_low, down_low, norm_gains, padded
    )
    grad_pairs, grad_values, total, big = mixer_back(
        doc_starts, pairs, values, attn_low, recip, grad_attended, wide, ffn_part, big, pieces, bits
    )
    grad_normed_one, small = project_back(grad_pairs, grad_values, normed_one, wide, tokens, dp_size)
    rates = (
        (D * total_tokens) ** (-0.5),
        (D * total_tokens) ** (-0.5),
        (HEADS * HV * total_tokens) ** (-0.5),
        (D * total_tokens) ** (-0.5),
        (FF * total_tokens) ** (-0.5),
        0.2 * total_tokens ** (-0.5),
    )
    weights = (
        (down_weight, down_moment, down_average),
        (gate_turned, gate_moment.transpose(0, 2, 1), gate_average.transpose(0, 2, 1)),
        (out_weight, out_moment, out_average),
        (value_weight, value_moment, value_average),
        (queries_keys, queries_moment, queries_average),
        (norm_gains, gains_moment, gains_average),
    )
    outs = list(finish(rates, weights, big, small, hidden_one, total, grad_hidden, grad_normed_one, tokens, norm_gains))
    outs[11:14] = [o.transpose(0, 2, 1) for o in outs[11:14]]
    return tuple(outs)


def solution(mesh):
    in_specs = (
        P("dp", None),
        P("dp", None),
        P("dp", None),
        P(None, "feat"),
        P(None, "feat"),
        P("feat", None),
        P(None, None, "feat"),
        P("feat", None),
        P(),
        P(None, "feat"),
        P(None, "feat"),
        P("feat", None),
        P(None, None, "feat"),
        P("feat", None),
        P(),
        P(None, "feat"),
        P(None, "feat"),
        P("feat", None),
        P(None, None, "feat"),
        P("feat", None),
        P(),
    )
    out_specs = (
        P("dp", None),
        P("dp", None),
        P(None, "feat"),
        P(None, "feat"),
        P(None, "feat"),
        P(None, "feat"),
        P(None, "feat"),
        P(None, "feat"),
        P("feat", None),
        P("feat", None),
        P("feat", None),
        P(None, None, "feat"),
        P(None, None, "feat"),
        P(None, None, "feat"),
        P("feat", None),
        P("feat", None),
        P("feat", None),
        P(),
        P(),
        P(),
    )
    return jax.shard_map(
        on_device, mesh=mesh, in_specs=in_specs, out_specs=out_specs, check_vma=False
    )
```

time: 447 us -> 297 us (0.66)
  local copies, waits for them, and re-layouts: 73 us -> 8.36 us
  other arithmetic: 42.9 us -> 0 us
  matrix products: 37.5 us -> 0 us
    dot_general x17 -> x0, matrix products: 37.5 us -> none  [the longest x1 3.98 us: on_device(): jnp.dot(normed_one, values_full, preferred_element_type=F32).astype(BF16)]
    add x7 -> x0, other arithmetic: 31.6 us -> none  [the longest x6 26.7 us: update(): average_next = average + (weight_next - average) / STEP]
    unnamed x98 -> x30, local copies, waits for them, and re-layouts: 38.1 us -> 8.36 us
    concatenate x3 -> x0, local copies, waits for them, and re-layouts: 25.2 us -> none  [the longest x1 24.4 us: on_device(): stacked = jnp.concatenate(units, axis=0)]
    convert_element_type x5 -> x0, other arithmetic: 7.56 us -> none  [the longest x1 4.6 us: on_device(): gate_low = gate_up.astype(BF16)]
where the time goes in v3:
time: 297 us
  Pallas kernels  288 us (97%)
  local copies, waits for them, and re-layouts  8.36 us (3%)
    pallas_call x1, Pallas kernels, mixer_back(): pl.pallas_call(functools.partial(mixer_back_kernel, pieces, bits, hb, row...  92.3 us
    pallas_call x1, Pallas kernels, feed(): pl.pallas_call(functools.partial(feed_kernel, rows), out_shape=(jax.Shape...  73.9 us
    pallas_call x1, Pallas kernels, project(): pl.pallas_call(functools.partial(project_kernel, bits), out_shape=(jax.Sh...  41.8 us
    pallas_call x1, Pallas kernels, finish(): pl.pallas_call(functools.partial(update_kernel, rates), grid=(steps,), ou...  31.2 us
    pallas_call x1, Pallas kernels, project_back(): pl.pallas_call(functools.partial(project_back_kernel, pieces, bits), out_...  28.6 us
    pallas_call x1, Pallas kernels, attn_fwd(): pl.pallas_call(functools.partial(attn_fwd_kernel, hb), grid=(length // BT...  19.9 us
    unnamed x30, local copies, waits for them, and re-layouts  8.36 us

profile of v3, /device:TPU:0, one launch (start us, length us, event | category | flops | bytes accessed | tf_op | source)
XLA Modules:
  0.0 297.0 jit_solution(1989993615422158180)
XLA Ops:
  0.7 0.0 copy-start.14
  0.7 41.8 %project.1 = (bf16[1024,1024]{1,0:T(8,128)(2,1)}, bf16[1024,512]{1,0:T(8,128)(2,1)}, bf16[1024,1024]{1,0:T(8,128)(2,1)}, bf16[1024,2560]{1,0:T(8,128)(2,1)}, bf1...) custom-call(bf16[1024,1024]{1,0:T(8,128)(2,1)} %tokens.1, f32[2,1024]{1,0:T(2,128)} %gains.1, f32[1024,128]{1,0:T(8,128)} %pair_w.1, ...), custom_call_target="tpu_custom_call" | custom-call | tf_op jit(solution)/shard_map/project/pallas_call | solution.py:518
  42.5 0.0 copy-done.14
  42.5 0.0 copy-start
  42.5 1.2 copy-done
  43.7 1.6 copy-done.2
  45.3 19.9 %mixer.1 = (bf16[1024,1024]{1,0:T(8,128)(2,1)S(1)}, f32[1024,1024]{1,0:T(8,128)S(1)}) custom-call(s32[1,8]{1,0:T(1,128)S(1)} %copy-done.14, bf16[1024,512]{1,0:T(8,128)(2,1)S(1)} %copy-done, bf16[1024,512]{1,0:T(8,128)(2,1)S(1)} %copy-done, bf16[1024,1024]{1,0:T(8,128)(2,1)S(1)} %copy-done.2), custom_call_target="tpu_custom_call" | custom-call | tf_op jit(solution)/shard_map/mixer/pallas_call | solution.py:95
  65.2 0.0 copy-start.1
  65.2 1.3 copy-done.1
  66.5 2.0 copy-done.3
  68.5 73.9 %feed.1 = (f32[1024,1024]{1,0:T(8,128)}, f32[1024,1024]{1,0:T(8,128)}, bf16[1024,1024]{1,0:T(8,128)(2,1)}, bf16[1024,1024]{1,0:T(8,128)(2,1)}, bf16[2432,1024]{1,0:T(8,128)(2,1)}) custom-call(bf16[1024,1024]{1,0:T(8,128)(2,1)} %tokens.1, bf16[1024,1024]{1,0:T(8,128)(2,1)} %cot_in.1, bf16[1024,1024]{1,0:T(8,128)(2,1)} %copy-done.1, ...), custom_call_target="tpu_custom_call" | custom-call | tf_op jit(solution)/shard_map/feed/pallas_call | solution.py:665
  142.5 92.3 %mixer_back.1 = (bf16[1024,512]{1,0:T(8,128)(2,1)}, bf16[1024,1024]{1,0:T(8,128)(2,1)}, bf16[1024,1024]{1,0:T(8,128)(2,1)}, bf16[2432,1024]{1,0:T(8,128)(2,1)}) custom-call(s32[1,8]{1,0:T(1,128)} %starts_ref.3, bf16[1024,512]{1,0:T(8,128)(2,1)} %get-tuple-element.59.q_ref.k_ref.pairs_in, bf16[1024,1024]{1,0:T(8,128)(2,1)} %get-tuple-element.60.v_ref.v_in, ...), custom_call_target="tpu_custom_call" | custom-call | tf_op jit(solution)/shard_map/mixer_back/pallas_call | solution.py:876
  234.8 0.0 copy-start.8
  234.8 1.2 copy-done.8
  236.0 0.0 copy-start.10
  236.0 0.0 copy-start.11
  236.0 0.0 copy-start.12
  236.0 0.0 copy-start.13
  236.1 28.6 %project_back.1 = (bf16[1024,1024]{1,0:T(8,128)(2,1)}, bf16[512,1024]{1,0:T(8,128)(2,1)S(1)}) custom-call(bf16[1024,512]{1,0:T(8,128)(2,1)S(1)} %copy-done.8, bf16[1024,1024]{1,0:T(8,128)(2,1)} %get-tuple-element.71.gv_ref, bf16[1024,1024]{1,0:T(8,128)(2,1)} %get-tuple-element.72.normed_ref, bf16[1024,2560]{1,0:T(8,128)(2,1)} %get-tuple-element.63.wide_in.wide_ref, ...), custom_call_target="tpu_custom_call" | custom-call | tf_op jit(solution)/shard_map/project_back/pallas_call | solution.py:951
  264.6 0.0 copy-start.7
  264.7 1.0 copy-done.7
  265.6 0.0 copy-done.4
  265.6 0.0 copy-done.6
  265.7 31.2 %finish.1 = (bf16[1024,1024]{1,0:T(8,128)(2,1)}, f32[1024,1024]{1,0:T(8,128)}, f32[1024,128]{1,0:T(8,128)}, f32[1024,128]{1,0:T(8,128)}, f32[1024,128]{1,0:T(8,1...) custom-call(f32[688,1024]{1,0:T(8,128)} %down_w.1, ...), custom_call_target="tpu_custom_call" | custom-call | tf_op jit(solution)/shard_map/finish/pallas_call | solution.py:1026
  (12 shorter events, 0.0 us)
Async XLA Ops:
  0.7 41.8 %copy-start.14 = (s32[1,8]{1,0:T(1,128)S(1)}, s32[1,8]{1,0:T(1,128)}, u32[]{:S(2)}) copy-start(s32[1,8]{1,0:T(1,128)} %starts_ref.3) | copy-start | bytes 100
  42.5 1.2 copy-start
  43.7 1.6 copy-start.2
  65.2 1.3 copy-start.1
  66.5 2.0 copy-start.3
  234.8 1.2 copy-start.8
  236.0 29.6 %copy-start.4 = (f32[256,1024]{1,0:T(8,128)S(1)}, f32[256,1024]{1,0:T(8,128)}, u32[]{:S(2)}) copy-start(f32[256,1024]{1,0:T(8,128)} %out_w.1) | copy-start | bytes 3145732
  236.0 29.6 %copy-start.5 = (f32[1024,128]{1,0:T(8,128)S(1)}, f32[1024,128]{1,0:T(8,128)}, u32[]{:S(2)}) copy-start(f32[1024,128]{1,0:T(8,128)} %pair_w.1) | copy-start | bytes 1572868
  236.0 29.6 %copy-start.6 = (f32[256,1024]{1,0:T(8,128)S(1)}, f32[256,1024]{1,0:T(8,128)}, u32[]{:S(2)}) copy-start(f32[256,1024]{1,0:T(8,128)} %out_m.1) | copy-start | bytes 3145732
  236.0 29.6 %copy-start.9 = (f32[1024,128]{1,0:T(8,128)S(1)}, f32[1024,128]{1,0:T(8,128)}, u32[]{:S(2)}) copy-start(f32[1024,128]{1,0:T(8,128)} %pair_m.1) | copy-start | bytes 1572868
  236.0 29.6 %copy-start.10 = (f32[1024,128]{1,0:T(8,128)S(1)}, f32[1024,128]{1,0:T(8,128)}, u32[]{:S(2)}) copy-start(f32[1024,128]{1,0:T(8,128)} %pair_a.1) | copy-start | bytes 1572868
  236.0 29.6 %copy-start.11 = (f32[2,1024]{1,0:T(2,128)S(1)}, f32[2,1024]{1,0:T(2,128)}, u32[]{:S(2)}) copy-start(f32[2,1024]{1,0:T(2,128)} %gains.1) | copy-start | bytes 24580
  236.0 29.6 %copy-start.12 = (f32[2,1024]{1,0:T(2,128)S(1)}, f32[2,1024]{1,0:T(2,128)}, u32[]{:S(2)}) copy-start(f32[2,1024]{1,0:T(2,128)} %gain_m.1) | copy-start | bytes 24580
  236.0 29.6 %copy-start.13 = (f32[2,1024]{1,0:T(2,128)S(1)}, f32[2,1024]{1,0:T(2,128)}, u32[]{:S(2)}) copy-start(f32[2,1024]{1,0:T(2,128)} %gain_a.1) | copy-start | bytes 24580
  264.6 1.0 copy-start.7

commit v4 on v3

v4 whole, which is shorter than its diff:
```python
import functools
import jax
import jax.numpy as jnp
from jax import lax
from jax.experimental import pallas as pl
from jax.experimental.pallas import tpu as pltpu
from jax.sharding import PartitionSpec as P

D = 1024
HEADS = 16
QK = 16
HV = 64
FF = 2752
STEP = 4
BT = 256
F32 = jnp.float32
BF16 = jnp.bfloat16

MESH = pl.DeviceIdType.MESH
EPS = 1e-06
MOMENTUM = 0.9


def nt(a, b):
    return lax.dot_general(a, b, (((1,), (1,)), ((), ())), preferred_element_type=F32)


def nn(a, b):
    return lax.dot_general(a, b, (((1,), (0,)), ((), ())), preferred_element_type=F32)


class LineSum:
    def __init__(self, part, leaf, mid, total, send, recv, rows, lags=(0, 2, 4)):
        self.part, self.leaf, self.mid, self.total, self.send, self.recv = part, leaf, mid, total, send, recv
        self.rows, self.lags = rows, lags
        self.count = part.shape[0] // rows
        self.dp, self.f = lax.axis_index("dp"), lax.axis_index("feat")

    def barrier(self):
        sem = pltpu.get_barrier_semaphore()
        dp, f = self.dp, self.f

        @pl.when(f > 0)
        def _():
            pl.semaphore_signal(sem, inc=1, device_id=(dp, f - 1), device_id_type=MESH)

        @pl.when(f < 3)
        def _():
            pl.semaphore_signal(sem, inc=1, device_id=(dp, f + 1), device_id_type=MESH)
        pl.semaphore_wait(sem, jnp.where(f > 0, 1, 0) + jnp.where(f < 3, 1, 0))

    def place(self, c):
        odd = lax.rem(c, 2)
        return self.f + odd * (3 - 2 * self.f), 1 - 2 * odd

    def copy(self, c, src, dst, kind, slot, to):
        at = pl.ds(pl.multiple_of(c * self.rows, self.rows), self.rows)
        return pltpu.make_async_remote_copy(
            src_ref=src.at[at], dst_ref=dst.at[at], send_sem=self.send.at[slot, c], recv_sem=self.recv.at[kind, c],
            device_id=(self.dp, to), device_id_type=MESH)

    def leaves(self, c):
        p, up = self.place(c)

        @pl.when(p == 3)
        def _():
            self.copy(c, self.part, self.leaf, 0, 0, self.f - up).start()

        @pl.when(p == 0)
        def _():
            self.copy(c, self.part, self.leaf, 0, 0, self.f + up).start()

    def middle(self, c):
        p, up = self.place(c)
        at = pl.ds(pl.multiple_of(c * self.rows, self.rows), self.rows)

        @pl.when(p == 2)
        def _():
            self.copy(c, self.part, self.leaf, 0, 0, self.f).wait_recv()
            self.part[at, :] = (self.part[at, :].astype(F32) + self.leaf[at, :].astype(F32)).astype(BF16)
            self.copy(c, self.part, self.mid, 1, 0, self.f - up).start()

    def root(self, c):
        p, up = self.place(c)
        at = pl.ds(pl.multiple_of(c * self.rows, self.rows), self.rows)

        @pl.when(p == 1)
        def _():
            self.copy(c, self.part, self.leaf, 0, 0, self.f).wait_recv()
            self.copy(c, self.part, self.mid, 1, 0, self.f).wait_recv()
            self.total[at, :] = (
                self.part[at, :].astype(F32) + self.leaf[at, :].astype(F32) + self.mid[at, :].astype(F32)
            ).astype(BF16)
            self.copy(c, self.total, self.total, 2, 1, self.f + up).start()
            self.copy(c, self.total, self.total, 2, 0, self.f - up).start()

    def onward(self, c):
        p, up = self.place(c)

        @pl.when(p == 2)
        def _():
            self.copy(c, self.total, self.total, 2, 0, self.f).wait_recv()
            self.copy(c, self.total, self.total, 2, 1, self.f + up).start()

    def serve(self, i):
        for lag, act in zip(self.lags, (self.middle, self.root, self.onward)):
            c = i - lag

            @pl.when(jnp.logical_and(c >= 0, c < self.count))
            def _():
                act(c)

    def steps(self):
        return self.count + self.lags[-1]

    def arrived(self, c):
        p, up = self.place(c)

        @pl.when(jnp.logical_or(p == 0, p == 3))
        def _():
            self.copy(c, self.total, self.total, 2, 0, self.f).wait_recv()

    def drain(self, c):
        p, up = self.place(c)
        self.copy(c, self.part, self.part, 0, 0, self.f).wait_send()

        @pl.when(jnp.logical_or(p == 1, p == 2))
        def _():
            self.copy(c, self.part, self.part, 0, 1, self.f).wait_send()


class CubeSum:
    def __init__(self, work, recv, out, send_sem, recv_sem, pieces, bits):
        self.work, self.recv, self.out, self.send_sem, self.recv_sem = work, recv, out, send_sem, recv_sem
        self.pieces, self.nb = pieces, len(bits)
        self.dp, self.f = lax.axis_index("dp"), lax.axis_index("feat")
        self.orders = [list(bits), [bits[0]] + list(bits[1:])[::-1]]
        self.bits = bits

    def partner(self, bit):
        return self.dp + bit - 2 * bit * lax.rem(self.dp // bit, 2)

    def barrier(self):
        sem = pltpu.get_barrier_semaphore()
        for bit in self.bits:
            pl.semaphore_signal(sem, inc=1, device_id=(self.partner(bit), self.f), device_id_type=MESH)
        pl.semaphore_wait(sem, len(self.bits))

    def lanes(self, colour):
        half = self.work.shape[1] // 2
        return pl.ds(colour * half, half)

    def segment(self, piece, colour, k):
        first, rows = self.pieces[piece]
        start = first
        for bit in self.orders[colour][:k]:
            rows = rows // 2
            start = start + rows * lax.rem(self.dp // bit, 2)
        return start, rows

    def at(self, start, rows):
        return pl.ds(pl.multiple_of(start, 16), rows)

    def halve(self, piece, colour, k):
        start, rows = self.segment(piece, colour, k)
        rows = rows // 2
        bit = self.orders[colour][k]
        own = lax.rem(self.dp // bit, 2)
        first, whole = self.pieces[piece]
        landing = first + whole - 2 * rows
        return pltpu.make_async_remote_copy(
            src_ref=self.work.at[self.at(start + rows * (1 - own), rows), self.lanes(colour)],
            dst_ref=self.recv.at[self.at(landing, rows), self.lanes(colour)],
            send_sem=self.send_sem.at[piece, colour, k], recv_sem=self.recv_sem.at[piece, colour, k],
            device_id=(self.partner(bit), self.f), device_id_type=MESH)

    def add(self, piece, colour, k):
        start, rows = self.segment(piece, colour, k + 1)
        first, whole = self.pieces[piece]
        landing = first + whole - 2 * rows
        target = self.out if k + 1 == self.nb else self.work
        mine = self.work[self.at(start, rows), self.lanes(colour)].astype(F32)
        target[self.at(start, rows), self.lanes(colour)] = (
            mine + self.recv[self.at(landing, rows), self.lanes(colour)].astype(F32)
        ).astype(BF16)

    def double(self, piece, colour, k):
        start, rows = self.segment(piece, colour, k + 1)
        bit = self.orders[colour][k]
        at = self.at(start, rows)
        slot = 2 * self.nb - 1 - k
        return pltpu.make_async_remote_copy(
            src_ref=self.out.at[at, self.lanes(colour)], dst_ref=self.out.at[at, self.lanes(colour)],
            send_sem=self.send_sem.at[piece, colour, slot], recv_sem=self.recv_sem.at[piece, colour, slot],
            device_id=(self.partner(bit), self.f), device_id_type=MESH)

    def launch(self, piece):
        for colour in range(2):
            self.halve(piece, colour, 0).start()

    def advance(self, piece, t):
        for colour in range(2):
            if t < self.nb:
                self.halve(piece, colour, t).wait_recv()
                self.add(piece, colour, t)
                if t + 1 < self.nb:
                    self.halve(piece, colour, t + 1).start()
                else:
                    self.double(piece, colour, self.nb - 1).start()
            else:
                k = 2 * self.nb - 1 - t
                self.double(piece, colour, k).wait_recv()
                if k > 0:
                    self.double(piece, colour, k - 1).start()

    def drain(self, piece):
        for colour in range(2):
            for k in range(self.nb):
                self.halve(piece, colour, k).wait_send()
                self.double(piece, colour, k).wait_send()


def split_rows(rows, unit, count):
    units = rows // unit
    out, first = [], 0
    for n in range(count):
        take = (units * (n + 1) // count - units * n // count) * unit
        out.append((first, take))
        first += take
    return [p for p in out if p[1]]


def own_column(ref, f, width):
    return ref[:, pl.ds(pl.multiple_of(f * width, width), width)]


def greet(line, cube):
    sem = pltpu.get_barrier_semaphore()
    f = lax.axis_index("feat")
    count = jnp.int32(0)
    if cube is not None:
        for bit in cube.bits:
            pl.semaphore_signal(sem, inc=1, device_id=(cube.partner(bit), f), device_id_type=MESH)
        count = count + len(cube.bits)
    if line is not None:
        @pl.when(f > 0)
        def _():
            pl.semaphore_signal(sem, inc=1, device_id=(line.dp, f - 1), device_id_type=MESH)

        @pl.when(f < 3)
        def _():
            pl.semaphore_signal(sem, inc=1, device_id=(line.dp, f + 1), device_id_type=MESH)
        count = count + jnp.where(f > 0, 1, 0) + jnp.where(f < 3, 1, 0)
    pl.semaphore_wait(sem, count)


def each(act, n):
    def body(c, carry):
        act(c)
        return carry

    lax.fori_loop(0, n, body, 0)


def cube_shape(rows, dp_size, count):
    unit = 16 * dp_size
    padded = (rows + unit - 1) // unit * unit
    bits = tuple(2**n for n in range(dp_size.bit_length() - 1))
    return padded, split_rows(padded, unit, count), bits


def front_kernel(
    bits, starts_ref, tokens_in, gains_ref, pair_ref, value_ref, out_ref, gate_in, down_in,
    normed_out, pairs_out, values_out, wide_out, gate_out, down_out, attn_out, recip_out, mask_out,
    thin_ref, thick_ref, tokens_ref, gate_f32, down_f32,
    normed_ref, pairs_ref, values_ref, wide_ref, gate_ref, down_ref, attn_ref, recip_ref, mask_ref, acc_ref,
    send_sem, recv_sem, load_sem, store_sem,
):
    dp = lax.axis_index("dp")
    f = lax.axis_index("feat")
    slices = lax.axis_size("feat")
    last = slices - 1
    pieces = 2 ** len(bits)
    j = lax.rem(dp, pieces)
    base = dp - j
    pair_cols, value_cols = pair_ref.shape[1], value_ref.shape[1]
    pairs_wide, values_wide = slices * pair_cols, slices * value_cols
    rows = pair_ref.shape[0] // pieces
    length = tokens_ref.shape[0]
    blocks = length // BT
    loads = [
        pltpu.make_async_copy(a, b, load_sem.at[n])
        for n, (a, b) in enumerate([(tokens_in, tokens_ref), (gate_in, gate_f32), (down_in, down_f32)])
    ]
    for load in loads:
        load.start()

    def flip(k, bit):
        return k + bit - 2 * bit * lax.rem(k // bit, 2)

    def cast(k):
        at = pl.ds(pl.multiple_of(k * rows, rows), rows)
        pair = pair_ref[at, :].astype(BF16)
        thick = jnp.concatenate([value_ref[at, :].astype(BF16), out_ref[:, at].T.astype(BF16)], axis=1)
        for colour in range(2):
            part = slice(colour * rows // 2, (colour + 1) * rows // 2)
            thin_ref[f, k, colour] = pair[part]
            thick_ref[f, k, colour] = thick[part]

    cast(j)
    barrier = pltpu.get_barrier_semaphore()
    for bit in bits:
        pl.semaphore_signal(barrier, inc=1, device_id=(base + flip(j, bit), f), device_id_type=MESH)

    @pl.when(f > 0)
    def _():
        pl.semaphore_signal(barrier, inc=1, device_id=(dp, f - 1), device_id_type=MESH)

    @pl.when(f < last)
    def _():
        pl.semaphore_signal(barrier, inc=1, device_id=(dp, f + 1), device_id_type=MESH)

    pl.semaphore_wait(barrier, len(bits) + jnp.where(f > 0, 1, 0) + jnp.where(f < last, 1, 0))

    def copy(wave, z, colour, k, slot, device):
        ref = (thin_ref, thick_ref)[wave]
        return pltpu.make_async_remote_copy(
            src_ref=ref.at[z, k, colour], dst_ref=ref.at[z, k, colour], send_sem=send_sem.at[wave, z, colour, slot],
            recv_sem=recv_sem.at[wave, z, colour, k], device_id=device, device_id_type=MESH,
        )

    here = (dp, f)
    for wave in range(2):
        for colour in range(2):
            @pl.when(f > 0)
            def _():
                copy(wave, f, colour, j, 0, (dp, f - 1)).start()

            @pl.when(f < last)
            def _():
                copy(wave, f, colour, j, 1, (dp, f + 1)).start()

    order = [
        jnp.where(f == 0, 1, f - 1),
        jnp.where(f < 2, 2, jnp.where(f == 2, 3, 1)),
        jnp.where(f < 2, 3, 0),
    ]
    colour_bits = [list(bits[1:]) + [bits[0]], list(bits[1:])[::-1] + [bits[0]]]

    def held(colour, step):
        out = [j]
        for bit in colour_bits[colour][:step]:
            out = out + [flip(k, bit) for k in out]
        return out

    def start_step(wave, z, step):
        for colour in range(2):
            first = 2 + 2**step - 1
            partner = (base + flip(j, colour_bits[colour][step]), f)
            for n, k in enumerate(held(colour, step)):
                copy(wave, z, colour, k, first + n, partner).start()

    def step(wave, a, n):
        z = order[a]
        for colour in range(2):
            for k in held(colour, n):
                copy(wave, z, colour, flip(k, colour_bits[colour][n]), 0, here).wait_recv()
        if n + 1 < len(bits):
            start_step(wave, z, n + 1)

    def arrive(wave, a):
        z = order[a]
        ahead = jnp.where(z < f, f + 1, f - 1)
        onward = jnp.logical_and(ahead >= 0, ahead <= last)
        for colour in range(2):
            copy(wave, z, colour, j, 0, here).wait_recv()

            @pl.when(onward)
            def _():
                copy(wave, z, colour, j, jnp.where(z < f, 1, 0), (dp, ahead)).start()
        start_step(wave, z, 0)

    def put_thin(z):
        at = pl.ds(pl.multiple_of(z * pair_cols, pair_cols), pair_cols)
        wide_ref[:, at] = thin_ref[z].reshape(pieces * rows, pair_cols)

    def lanes(first, z):
        return pl.ds(pl.multiple_of(first + z * value_cols, 128), value_cols)

    def store(n, source, target, at=None):
        if at is not None:
            source, target = source.at[:, at], target.at[:, at]
        return pltpu.make_async_copy(source, target, store_sem.at[n])

    def use(a, z):
        weight = thick_ref[z].reshape(pieces * rows, 2 * value_cols)
        wide_ref[:, lanes(pairs_wide, z)] = weight[:, :value_cols]
        wide_ref[:, lanes(pairs_wide + values_wide, z)] = weight[:, value_cols:]

        def some(n, carry):
            at = pl.ds(pl.multiple_of(n * BT, BT), BT)
            values_ref[at, lanes(0, z)] = nn(normed_ref[at, :], wide_ref[:, lanes(pairs_wide, z)]).astype(BF16)
            return carry

        lax.fori_loop(0, blocks, some, 0)
        store(6 + a, wide_ref, wide_out, lanes(pairs_wide, z)).start()
        store(10 + a, wide_ref, wide_out, lanes(pairs_wide + values_wide, z)).start()
        store(14 + a, values_ref, values_out, lanes(0, z)).start()

    def cast_rest(n, carry):
        cast(lax.rem(j + n, pieces))
        return carry

    lax.fori_loop(1, pieces, cast_rest, 0)
    loads[0].wait()

    def norm(n, carry):
        at = pl.ds(pl.multiple_of(n * BT, BT), BT)
        x = tokens_ref[at, :].astype(F32)
        scale = lax.rsqrt(jnp.mean(x * x, axis=1, keepdims=True) + EPS)
        normed_ref[at, :] = (x * scale * gains_ref[0:1, :]).astype(BF16)
        return carry

    lax.fori_loop(0, blocks, norm, 0)
    store(0, normed_ref, normed_out).start()
    arrive(0, 0)
    put_thin(f)
    use(0, f)
    arrive(0, 1)
    step(0, 0, 0)
    arrive(0, 2)
    step(0, 1, 0)

    begin = jnp.zeros((length, 1), jnp.int32)
    position = lax.broadcasted_iota(jnp.int32, (length, 1), 0)
    for n in range(starts_ref.shape[1]):
        begin = jnp.where(starts_ref[0, n] <= position, jnp.maximum(begin, starts_ref[0, n]), begin)
    for n in range(blocks):
        rest = length - n * BT
        s = n * BT + lax.broadcasted_iota(jnp.int32, (rest, BT), 1)
        keep = jnp.logical_and(s <= position[n * BT :], s >= begin[n * BT :])
        mask_ref[n, :rest, :] = keep.astype(F32).astype(BF16)
        if n:
            mask_ref[n, rest:, :] = jnp.zeros((n * BT, BT), BF16)
    store(1, mask_ref, mask_out).start()
    step(0, 0, 1)
    step(0, 2, 0)
    step(0, 1, 1)
    arrive(1, 0)
    step(0, 0, 2)
    put_thin(order[0])
    step(0, 2, 1)

    def cast_all(source, target):
        def go(m, carry):
            at = pl.ds(pl.multiple_of(m * 16, 16), 16)
            target[at, :] = source[at, :].astype(BF16)
            return carry

        lax.fori_loop(0, source.shape[0] // 16, go, 0)

    loads[1].wait()
    loads[2].wait()
    cast_all(gate_f32.at[0], gate_ref.at[0])
    arrive(1, 1)
    step(1, 0, 0)
    cast_all(gate_f32.at[1], gate_ref.at[1])
    step(0, 1, 2)
    put_thin(order[1])
    step(0, 2, 2)
    put_thin(order[2])
    step(1, 0, 1)
    arrive(1, 2)
    step(1, 1, 0)
    cast_all(down_f32, down_ref)
    store(2, gate_ref, gate_out).start()
    store(3, down_ref, down_out).start()

    half = pairs_wide // 2

    def project_pairs(n, carry):
        at = pl.ds(pl.multiple_of(n * BT, BT), BT)
        pairs = nn(normed_ref[at, :], wide_ref[:, :pairs_wide]).astype(BF16)
        pairs_ref[at, :half] = pairs[:, :half] * jnp.bfloat16(0.25)
        pairs_ref[at, half:] = pairs[:, half:]
        return carry

    lax.fori_loop(0, blocks, project_pairs, 0)
    store(4, pairs_ref, pairs_out).start()
    store(5, wide_ref, wide_out, pl.ds(0, pairs_wide)).start()

    lane = lax.broadcasted_iota(jnp.int32, (1, 128), 1)
    events = {
        1: [(step, 1, 2, 0), (step, 1, 1, 1)],
        2: [(step, 1, 0, 2), (use, 1, order[0])],
        3: [(step, 1, 2, 1)],
        4: [(step, 1, 1, 2), (use, 2, order[1])],
        6: [(step, 1, 2, 2), (use, 3, order[2])],
    }

    def unit(n, carry):
        for at, acts in events.items():
            @pl.when(n == at)
            def _():
                for act in acts:
                    act[0](*act[1:])
        a = n // 2
        z = jnp.where(a == 0, f, jnp.where(a == 1, order[0], jnp.where(a == 2, order[1], order[2])))
        pair = 2 * z + lax.rem(n, 2)
        vl = pl.ds(pl.multiple_of(pair * 128, 128), 128)
        ql = pl.ds(pl.multiple_of(pair // 4 * 128, 128), 128)
        kl = pl.ds(pl.multiple_of(half + pair // 4 * 128, 128), 128)
        for block in range(blocks):
            first = block * BT
            below, there = pl.ds(first, length - first), pl.ds(first, BT)
            q, k, v = pairs_ref[below, ql], pairs_ref[there, kl], values_ref[there, vl]
            mask = mask_ref[block, : length - first, :]
            for m in range(2):
                own = lane // QK == lax.rem(2 * pair + m, 8)
                t1 = nt(q, jnp.where(own, k, jnp.zeros_like(k))) + 1.0
                p = (t1 * t1 + 1.0).astype(BF16) * mask
                out = nn(p, jnp.where(lane // HV == m, v, jnp.ones_like(v)))
                if block:
                    acc_ref[m, below, :] += out
                else:
                    acc_ref[m] = out
        one, two = acc_ref[0], acc_ref[1]
        numer = jnp.where(lane < HV, one, two)
        recip = 1.0 / pltpu.roll(jnp.where(lane < HV, two, one), HV, 1)
        attn_ref[:, vl] = (numer * recip).astype(BF16)
        recip_ref[:, vl] = recip
        store(18 + n, attn_ref, attn_out, vl).start()
        store(26 + n, recip_ref, recip_out, vl).start()
        return carry

    lax.fori_loop(0, 2 * slices, unit, 0)
    for wave in range(2):
        for z in order:
            ahead = jnp.where(z < f, f + 1, f - 1)
            onward = jnp.logical_and(ahead >= 0, ahead <= last)
            for colour in range(2):
                @pl.when(onward)
                def _():
                    copy(wave, z, colour, j, jnp.where(z < f, 1, 0), here).wait_send()

                for n in range(len(bits)):
                    for m, k in enumerate(held(colour, n)):
                        copy(wave, z, colour, k, 2 + 2**n - 1 + m, here).wait_send()
        for colour in range(2):
            @pl.when(f > 0)
            def _():
                copy(wave, f, colour, j, 0, here).wait_send()

            @pl.when(f < last)
            def _():
                copy(wave, f, colour, j, 1, here).wait_send()
    for n, (source, target) in enumerate([
        (normed_ref, normed_out), (mask_ref, mask_out), (gate_ref, gate_out), (down_ref, down_out), (pairs_ref, pairs_out),
    ]):
        store(n, source, target).wait()
    store(5, wide_ref, wide_out, pl.ds(0, pairs_wide)).wait()
    for a in range(slices):
        store(6 + a, wide_ref, wide_out, pl.ds(0, value_cols)).wait()
        store(10 + a, wide_ref, wide_out, pl.ds(0, value_cols)).wait()
        store(14 + a, values_ref, values_out, pl.ds(0, value_cols)).wait()
    for n in range(2 * slices):
        store(18 + n, attn_ref, attn_out, pl.ds(0, 128)).wait()
        store(26 + n, recip_ref, recip_out, pl.ds(0, 128)).wait()


def front(starts, tokens, gains, pair_w, value_w, out_w, gate_turned, down):
    length = tokens.shape[0]
    ff = down.shape[0]
    slices = 4
    pair_cols, value_cols = pair_w.shape[1], value_w.shape[1]
    bits = (1, 2, 4)
    hbm = pl.BlockSpec(memory_space=pl.ANY)
    vmem = pl.BlockSpec(memory_space=pltpu.VMEM)
    shapes = [
        ((length, D), BF16),
        ((length, slices * pair_cols), BF16),
        ((length, slices * value_cols), BF16),
        ((D, slices * (pair_cols + 2 * value_cols)), BF16),
        ((2, ff, D), BF16),
        ((ff, D), BF16),
        ((length, slices * value_cols), BF16),
        ((length, slices * value_cols), F32),
        ((length // BT, length, BT), BF16),
    ]
    return pl.pallas_call(
        functools.partial(front_kernel, bits),
        out_shape=tuple(jax.ShapeDtypeStruct(*s) for s in shapes),
        in_specs=[pl.BlockSpec(memory_space=pltpu.SMEM), hbm] + [vmem] * 4 + [hbm] * 2,
        out_specs=(hbm,) * 9,
        scratch_shapes=[
            pltpu.VMEM((slices, 8, 2, D // 16, pair_cols), BF16),
            pltpu.VMEM((slices, 8, 2, D // 16, 2 * value_cols), BF16),
            pltpu.VMEM((length, D), BF16),
            pltpu.VMEM((2, ff, D), F32),
            pltpu.VMEM((ff, D), F32),
        ]
        + [pltpu.VMEM(*s) for s in shapes]
        + [
            pltpu.VMEM((2, length, 128), F32),
            pltpu.SemaphoreType.DMA((2, slices, 2, 9)),
            pltpu.SemaphoreType.DMA((2, slices, 2, 8)),
            pltpu.SemaphoreType.DMA((3,)),
            pltpu.SemaphoreType.DMA((18 + 4 * slices,)),
        ],
        compiler_params=pltpu.CompilerParams(collective_id=1, has_side_effects=True, vmem_limit_bytes=60 * 2**20),
        name="front",
    )(starts, tokens, gains, pair_w, value_w, out_w, gate_turned, down)


def feed_kernel(
    rows, tokens_in, cot_in, attn_in, recip_in, wide_in, gate_in, down_in, gains_ref,
    hidden_out, grad_hidden_out, gn_out, gnt_out, gd_out, ffn_out, grads_out,
    tokens_ref, cot_ref, attn_ref, out_w, gate_ref, down_ref, recip_ref,
    hidden_ref, scale_ref, normed_ref, product_t, gate_t, up_t, own_t, gain_ref, ga_ref, gn_ref, gnt_ref, gd_ref, ffn_ref, grads_ref,
    part, leaf, mid, total, send, recv, load_sem, store_sem,
):
    f = lax.axis_index("feat")
    line = LineSum(part, leaf, mid, total, send, recv, rows, (0, 3, 6))
    length = tokens_ref.shape[0]
    ff = down_ref.shape[0]
    value_cols = own_t.shape[0]
    blocks = length // BT
    first_out = wide_in.shape[1] - attn_ref.shape[1]
    pairs = [(attn_in, attn_ref), (wide_in.at[:, pl.ds(first_out, attn_ref.shape[1])], out_w), (tokens_in, tokens_ref),
             (gate_in, gate_ref), (down_in, down_ref), (cot_in, cot_ref), (recip_in, recip_ref)]
    loads = [pltpu.make_async_copy(a, b, load_sem.at[n]) for n, (a, b) in enumerate(pairs)]
    for load in loads:
        load.start()
    greet(line, None)
    for load in loads[:-1]:
        load.wait()

    def store(source, target, n, kind):
        at = pl.ds(pl.multiple_of(n * BT, BT), BT)
        return pltpu.make_async_copy(source.at[at], target.at[at], store_sem.at[kind, n])

    def block(b, carry):
        at = pl.ds(pl.multiple_of(b * BT, BT), BT)
        turn = 4 * (b - 1)
        hidden = tokens_ref[at, :].astype(F32) + nt(attn_ref[at, :], out_w[...])
        hidden_ref[at, :] = hidden
        store(hidden_ref, hidden_out, b, 0).start()
        scale = lax.rsqrt(jnp.mean(hidden * hidden, axis=1, keepdims=True) + EPS)
        scale_ref[at, :] = jnp.broadcast_to(scale, (BT, 128))
        normed = (hidden * scale * gains_ref[1:2, :]).astype(BF16)
        normed_ref[at, :] = normed
        line.serve(turn)
        gate = nt(normed, gate_ref[0])
        up = nt(normed, gate_ref[1])
        line.serve(turn + 1)
        back = nt(cot_ref[at, :], down_ref[...])
        sig = 1.0 / (1.0 + jnp.exp(-gate))
        active = gate * sig
        slope = sig * (1.0 + gate * (1.0 - sig))
        product = (active * up).astype(BF16)
        grad_gate = (back * up * slope).astype(BF16)
        grad_up = (back * active).astype(BF16)
        line.serve(turn + 2)
        part[at, :] = (nn(grad_gate, gate_ref[0]) + nn(grad_up, gate_ref[1])).astype(BF16)

        def out(c, carry):
            line.leaves(b * (BT // rows) + c)
            return carry

        lax.fori_loop(0, BT // rows, out, 0)
        ffn_ref[at, :] = nn(product, down_ref[...]).astype(BF16)
        product_t[:, at] = product.T
        gate_t[:, at] = grad_gate.T
        up_t[:, at] = grad_up.T
        line.serve(turn + 3)
        return carry

    lax.fori_loop(0, blocks, block, 0)
    served = 4 * (blocks - 1)
    gain_ref[...] = jnp.zeros_like(gain_ref)
    chunks = []
    at = 0
    while at < ff:
        chunks.append((at, min(176, ff - at)))
        at += chunks[-1][1]
    for n, (turned, right) in enumerate([(product_t, cot_ref), (gate_t, normed_ref), (up_t, normed_ref)]):
        for first, size in chunks:
            at = slice(n * ff + first, n * ff + first + size)
            grads_ref[at, :] = nn(turned[first : first + size, :], right[...]).astype(BF16)
            line.serve(jnp.int32(served))
            served += 1
    ffn_store = pltpu.make_async_copy(ffn_ref, ffn_out, store_sem.at[0, blocks])
    ffn_store.start()
    grads_store = pltpu.make_async_copy(
        grads_ref.at[pl.ds(0, 3 * ff)], grads_out.at[pl.ds(0, 3 * ff)], store_sem.at[1, blocks]
    )
    grads_store.start()
    own_t[...] = own_column(attn_ref, f, value_cols).T
    loads[-1].wait()
    same = lax.broadcasted_iota(jnp.int32, (128, 128), 0) // HV == lax.broadcasted_iota(jnp.int32, (128, 128), 1) // HV
    negate = jnp.where(same, -1.0, 0.0).astype(BF16)

    def back_rows(n):
        at = pl.ds(pl.multiple_of(n * BT, BT), BT)
        hidden, grad = hidden_ref[at, :], total[at, :].astype(F32)
        scale = scale_ref[at, 0:1]
        unit = hidden * scale
        u = grad * gains_ref[1:2, :]
        gh = cot_ref[at, :].astype(F32) + scale * (u - unit * jnp.mean(u * unit, axis=1, keepdims=True))
        store(hidden_ref, hidden_out, n, 0).wait()
        hidden_ref[at, :] = gh
        store(hidden_ref, grad_hidden_out, n, 1).start()
        ga = gh.astype(BF16)
        ga_ref[at, :] = ga
        gain_ref[0:1, :] += jnp.sum(grad * unit, axis=0, keepdims=True)

        def pair(m, carry):
            wide = pl.ds(pl.multiple_of(m * 256, 256), 256)
            numer = nn(ga, out_w[:, wide]) * (2.0 * recip_ref[at, wide])
            low = numer.astype(BF16)
            both = (numer * attn_ref[at, wide].astype(F32)).astype(BF16)
            gn_ref[at, wide] = low
            gnt_ref[wide, at] = low.T
            gd_ref[at, wide] = jnp.concatenate([nn(both[:, :128], negate), nn(both[:, 128:], negate)], axis=1).astype(BF16)
            return carry

        lax.fori_loop(0, attn_ref.shape[1] // 256, pair, 0)
        store(gn_ref, gn_out, n, 2).start()
        store(gd_ref, gd_out, n, 3).start()
        turned_store(n).start()

    def turned_store(n):
        at = pl.ds(pl.multiple_of(n * BT, BT), BT)
        return pltpu.make_async_copy(gnt_ref.at[:, at], gnt_out.at[:, at], store_sem.at[4, n])

    per = BT // rows
    for n in range(blocks):
        until = min(per * (n + 1) + line.lags[-1], line.steps())

        def more(i, carry):
            line.serve(i)
            return carry

        lax.fori_loop(min(served, until), until, more, 0)
        served = max(served, until)
        lax.fori_loop(per * n, per * (n + 1), lambda c, carry: (line.arrived(c), carry)[1], 0)
        back_rows(jnp.int32(n))
    first = 3 * ff
    grads_ref[first : first + value_cols, :] = nn(own_t[...], ga_ref[...]).astype(BF16)
    first = first + value_cols
    rest = grads_ref.shape[0] - first
    grads_ref[first:, :] = jnp.zeros((rest, D), BF16)
    grads_ref[first : first + 16, :] = gain_ref[...].astype(BF16)
    each(line.drain, line.count)
    last = pl.ds(3 * ff, grads_ref.shape[0] - 3 * ff)
    last_store = pltpu.make_async_copy(grads_ref.at[last], grads_out.at[last], store_sem.at[2, blocks])
    last_store.start()
    for n in range(blocks):
        n = jnp.int32(n)
        store(hidden_ref, grad_hidden_out, n, 1).wait()
        store(gn_ref, gn_out, n, 2).wait()
        store(gd_ref, gd_out, n, 3).wait()
        turned_store(n).wait()
    ffn_store.wait()
    grads_store.wait()
    last_store.wait()


def feed(tokens, cotangent, attn, recip, wide, gate_turned, down, gains, padded):
    length = tokens.shape[0]
    ff = down.shape[0]
    nv, rows = attn.shape[1], 32
    count = length // rows
    hbm = pl.BlockSpec(memory_space=pl.ANY)
    vmem = pl.BlockSpec(memory_space=pltpu.VMEM)
    return pl.pallas_call(
        functools.partial(feed_kernel, rows),
        out_shape=(
            jax.ShapeDtypeStruct((length, D), F32),
            jax.ShapeDtypeStruct((length, D), F32),
            jax.ShapeDtypeStruct((length, nv), BF16),
            jax.ShapeDtypeStruct((nv, length), BF16),
            jax.ShapeDtypeStruct((length, nv), BF16),
            jax.ShapeDtypeStruct((length, D), BF16),
            jax.ShapeDtypeStruct((padded, D), BF16),
        ),
        in_specs=[hbm] * 7 + [vmem],
        out_specs=(hbm,) * 7,
        scratch_shapes=[
            pltpu.VMEM((length, D), BF16), pltpu.VMEM((length, D), BF16), pltpu.VMEM((length, nv), BF16),
            pltpu.VMEM((D, nv), BF16), pltpu.VMEM((2, ff, D), BF16), pltpu.VMEM((ff, D), BF16), pltpu.VMEM((length, nv), F32),
            pltpu.VMEM((length, D), F32), pltpu.VMEM((length, 128), F32), pltpu.VMEM((length, D), BF16),
            pltpu.VMEM((ff, length), BF16), pltpu.VMEM((ff, length), BF16), pltpu.VMEM((ff, length), BF16),
            pltpu.VMEM((nv // 4, length), BF16), pltpu.VMEM((16, D), F32), pltpu.VMEM((length, D), BF16),
            pltpu.VMEM((length, nv), BF16), pltpu.VMEM((nv, length), BF16), pltpu.VMEM((length, nv), BF16),
            pltpu.VMEM((length, D), BF16), pltpu.VMEM((padded, D), BF16),
            pltpu.VMEM((length, D), BF16), pltpu.VMEM((length, D), BF16), pltpu.VMEM((length, D), BF16),
            pltpu.VMEM((length, D), BF16),
            pltpu.SemaphoreType.DMA((2, count)), pltpu.SemaphoreType.DMA((3, count)),
            pltpu.SemaphoreType.DMA((7,)), pltpu.SemaphoreType.DMA((5, length // BT + 1)),
        ],
        compiler_params=pltpu.CompilerParams(collective_id=2, has_side_effects=True, vmem_limit_bytes=60 * 2**20),
        name="feed",
    )(tokens, cotangent, attn, recip, wide, gate_turned, down, gains)


def back_kernel(
    pieces, small_pieces, bits, rows,
    pairs_in, values_in, gn_in, gnt_in, gd_in, mask_in, ffn_in, grads_in, normed_in, wide_in, tokens_in,
    total_out, sums_out, grad_out, small_out,
    q_ref, k_ref, v_ref, gn_ref, gnt_ref, gd_ref, mask_ref, normed_ref, wide_ref, tokens_ref,
    part, leaf, mid, total, work, landing, sums, small_work, small_landing, small_sums,
    qt_ref, gq_ref, gkt_ref, gvt_ref, gp_ref, gv_ref, grad_ref, gain_ref,
    line_send, line_recv, cube_send, cube_recv, small_send, small_recv, load_sem, store_sem,
):
    f = lax.axis_index("feat")
    line = LineSum(part, leaf, mid, total, line_send, line_recv, rows, (0, 3, 6))
    cube = CubeSum(work, landing, sums, cube_send, cube_recv, pieces, bits)
    small = CubeSum(small_work, small_landing, small_sums, small_send, small_recv, small_pieces, bits)
    half = HEADS * QK
    first_loads = [
        pltpu.make_async_copy(grads_in.at[pl.ds(a, n)], work.at[pl.ds(a, n)], load_sem.at[m]) for m, (a, n) in enumerate(pieces)
    ] + [pltpu.make_async_copy(ffn_in, part, load_sem.at[len(pieces)])]
    sources = [
        (pairs_in.at[:, pl.ds(0, half)], q_ref), (pairs_in.at[:, pl.ds(half, half)], k_ref), (values_in, v_ref),
        (mask_in, mask_ref), (gn_in, gn_ref), (gd_in, gd_ref), (gnt_in, gnt_ref), (normed_in, normed_ref),
        (wide_in.at[:, pl.ds(0, wide_ref.shape[1])], wide_ref), (tokens_in, tokens_ref),
    ]
    loads = [pltpu.make_async_copy(a, b, load_sem.at[len(pieces) + 1 + n]) for n, (a, b) in enumerate(sources)]
    for load in first_loads:
        load.start()
    greet(line, cube)
    for p in range(len(pieces)):
        first_loads[p].wait()
        cube.launch(p)
    for load in loads:
        load.start()
    first_loads[-1].wait()
    each(line.leaves, line.count)
    gq_ref[...] = jnp.zeros_like(gq_ref)
    for load in loads[:7]:
        load.wait()
    qt_ref[...] = q_ref[...].T

    lane = lax.broadcasted_iota(jnp.int32, (1, 128), 1)
    length = q_ref.shape[0]
    blocks = length // BT
    hb = 2
    groups = HEADS // hb
    lengths = [(blocks - n // groups) + 0.3 for n in range(blocks * groups)]
    whole = sum(lengths)
    sequence = [(p, t) for t in range(2 * cube.nb) for p in range(len(pieces))]
    line_share, cube_share = PASS_LINE, PASS_CUBE

    def due(n, count, share):
        return int(sum(lengths[:n]) / whole * count * share)

    for block in range(blocks):
        lo = block * BT
        below, there = pl.ds(lo, length - lo), pl.ds(lo, BT)

        def group(g, carry):
            h = g * hb
            ql = pl.ds(pl.multiple_of(h // 8 * 128, 128), 128)
            vl = pl.ds(pl.multiple_of(g * 128, 128), 128)
            q, k, v = q_ref[below, ql], k_ref[there, ql], v_ref[there, vl]
            both = jnp.concatenate([gn_ref[below, vl], gd_ref[below, vl]], axis=1)
            mask = mask_ref[block, : length - lo, :]
            gq, turned = None, []
            for a in range(hb):
                km = jnp.where(lane // QK == lax.rem(h + a, 8), k, jnp.zeros_like(k))
                vm = jnp.where(lane // HV == a, v, jnp.zeros_like(v))
                pick = jnp.where(lane == HV * a, jnp.ones_like(v), jnp.zeros_like(v))
                t1 = nt(q, km) + 1.0
                p = (t1 * t1 + 1.0).astype(BF16) * mask
                dp = nt(both, jnp.concatenate([vm, pick], axis=1)).astype(BF16) * mask
                gs = (dp.astype(F32) * t1).astype(BF16)
                out = nn(gs, km)
                gq = out if gq is None else gq + out
                qrows = pl.ds(pl.multiple_of((h + a) * QK, QK), QK)
                vrows = pl.ds(pl.multiple_of((h + a) * HV, HV), HV)
                gkt_ref[qrows, there] = nn(qt_ref[qrows, below], gs)
                turned.append(nn(gnt_ref[vrows, below], p) * 0.5)
            gq_ref[below, ql] += gq
            gvt = jnp.concatenate(turned, axis=0)
            gvt_ref[vl, there] = gvt.astype(BF16)
            gv_ref[there, vl] = gvt.T.astype(BF16)
            for n in range(groups):
                m = block * groups + n
                steps = list(range(due(m, line.steps(), line_share), due(m + 1, line.steps(), line_share)))
                items = sequence[due(m, len(sequence), cube_share) : due(m + 1, len(sequence), cube_share)]
                if steps or items:
                    @pl.when(g == n)
                    def _():
                        for i in range(max(len(steps), len(items))):
                            if i < len(steps):
                                line.serve(jnp.int32(steps[i]))
                            if i < len(items):
                                cube.advance(*items[i])
            return carry

        lax.fori_loop(0, groups, group, 0)
    served, advanced = due(blocks * groups, line.steps(), line_share), due(blocks * groups, len(sequence), cube_share)
    gp_ref[:, :half] = (gq_ref[...] * 0.25).astype(BF16)
    gp_ref[:, half:] = gkt_ref[...].T.astype(BF16)
    for load in loads[7:]:
        load.wait()

    pair_cols, value_cols = 2 * half // 4, HEADS * HV // 4
    small_work[0:value_cols, :] = nn(
        gvt_ref[pl.ds(pl.multiple_of(f * value_cols, value_cols), value_cols), :], normed_ref[...]
    ).astype(BF16)
    small.launch(0)
    small_work[value_cols : value_cols + pair_cols, :] = nn(own_column(gp_ref, f, pair_cols).T, normed_ref[...]).astype(BF16)
    gain_ref[...] = jnp.zeros_like(gain_ref)

    def more(count):
        nonlocal served, advanced
        for _ in range(count):
            if served < line.steps():
                line.serve(jnp.int32(served))
                served += 1
            if advanced < len(sequence) and (len(sequence) - advanced) * 3 >= (line.steps() - served) * 2:
                cube.advance(*sequence[advanced])
                advanced += 1

    def back(n, carry):
        at = pl.ds(pl.multiple_of(n * BT, BT), BT)
        grad = nt(gp_ref[at, :], wide_ref[:, : 2 * half]) + nt(gv_ref[at, :], wide_ref[:, 2 * half :])
        grad_ref[at, :] = grad.astype(BF16)
        x = tokens_ref[at, :].astype(F32)
        scale = lax.rsqrt(jnp.mean(x * x, axis=1, keepdims=True) + EPS)
        gain_ref[0:1, :] += jnp.sum(grad * (x * scale), axis=0, keepdims=True)
        return carry

    lax.fori_loop(0, blocks, back, 0)
    grad_store = pltpu.make_async_copy(grad_ref, grad_out, store_sem.at[0])
    grad_store.start()
    rest = value_cols + pair_cols
    small_work[rest:, :] = jnp.zeros((small_work.shape[0] - rest, D), BF16)
    small_work[rest : rest + 16, :] = gain_ref[...].astype(BF16)
    for p in range(1, len(small_pieces)):
        small.launch(p)
    while advanced < len(sequence):
        more(1)
    stores = []
    for m, (a, n) in enumerate(pieces):
        stores.append(pltpu.make_async_copy(sums.at[pl.ds(a, n)], sums_out.at[pl.ds(a, n)], store_sem.at[2 + m]))
        stores[-1].start()
    for t in range(2 * small.nb):
        for p in range(len(small_pieces)):
            more(1)
            small.advance(p, t)
    small_store = pltpu.make_async_copy(small_sums, small_out, store_sem.at[1])
    small_store.start()
    while served < line.steps():
        more(1)
    each(line.arrived, line.count)
    total_store = pltpu.make_async_copy(total, total_out, store_sem.at[2 + len(pieces)])
    total_store.start()
    each(line.drain, line.count)
    for p in range(len(pieces)):
        cube.drain(p)
    for p in range(len(small_pieces)):
        small.drain(p)
    for s in stores + [grad_store, small_store, total_store]:
        s.wait()


PASS_LINE, PASS_CUBE = 0.7, 0.8


def back(pairs, values, gn, gnt, gd, mask, ffn, grads, normed, wide, tokens, pieces, bits, dp_size):
    length = tokens.shape[0]
    nq, nv, rows = HEADS * QK, HEADS * HV, 32
    count = length // rows
    unit = 16 * dp_size
    small_rows, small_pieces = 0, []
    for n in (nv // 4, nq // 2 + 16):
        n = (n + unit - 1) // unit * unit if small_pieces else n // unit * unit
        if n:
            small_pieces.append((small_rows, n))
            small_rows += n
    need = nv // 4 + nq // 2 + 16
    if small_rows < need:
        small_rows = (need + unit - 1) // unit * unit
        small_pieces = [(0, small_rows)]
    hbm = pl.BlockSpec(memory_space=pl.ANY)

    def buf(*shape, dtype=BF16):
        return pltpu.VMEM(shape, dtype)

    sems = [pltpu.SemaphoreType.DMA((len(p), 2, 2 * len(bits))) for p in (pieces, pieces, small_pieces, small_pieces)]
    return pl.pallas_call(
        functools.partial(back_kernel, pieces, small_pieces, bits, rows),
        out_shape=(
            jax.ShapeDtypeStruct((length, D), BF16),
            jax.ShapeDtypeStruct(grads.shape, BF16),
            jax.ShapeDtypeStruct((length, D), BF16),
            jax.ShapeDtypeStruct((small_rows, D), BF16),
        ),
        in_specs=[hbm] * 11,
        out_specs=(hbm,) * 4,
        scratch_shapes=[
            buf(length, nq), buf(length, nq), buf(length, nv), buf(length, nv), buf(nv, length), buf(length, nv),
            buf(*mask.shape), buf(length, D), buf(D, 2 * nq + nv), buf(length, D),
            buf(length, D), buf(length, D), buf(length, D), buf(length, D),
            buf(*grads.shape), buf(*grads.shape), buf(*grads.shape),
            buf(small_rows, D), buf(small_rows, D), buf(small_rows, D),
            buf(nq, length), buf(length, nq, dtype=F32), buf(nq, length, dtype=F32), buf(nv, length), buf(length, 2 * nq), buf(length, nv),
            buf(length, D), buf(16, D, dtype=F32),
            pltpu.SemaphoreType.DMA((2, count)), pltpu.SemaphoreType.DMA((3, count)), *sems,
            pltpu.SemaphoreType.DMA((len(pieces) + 11,)), pltpu.SemaphoreType.DMA((3 + len(pieces),)),
        ],
        compiler_params=pltpu.CompilerParams(collective_id=4, has_side_effects=True, vmem_limit_bytes=62 * 2**20),
        name="back",
    )(pairs, values, gn, gnt, gd, mask, ffn, grads, normed, wide, tokens)


def update_kernel(
    rates,
    down_w, down_m, down_a, gate_w, gate_m, gate_a, out_w, out_m, out_a, value_w, value_m, value_a,
    pair_w, pair_m, pair_a, gain_w, gain_m, gain_a, big, small, hidden, total, grad_hidden, grad_normed, tokens, gains,
    mixed_o, input_o, pair_mo, pair_wo, pair_ao, value_mo, value_wo, value_ao, out_mo, out_wo, out_ao,
    gate_mo, gate_wo, gate_ao, down_mo, down_wo, down_ao, gain_mo, gain_wo, gain_ao,
):
    ff = down_w.shape[0]
    narrow = value_w.shape[1]
    pair_cols = pair_w.shape[1]

    def put(index, outs, grad, w, m, a, rate):
        moment_next, weight_next, average_next = update(w[index], grad, m[index], a[index], rate)
        outs[0][index], outs[1][index], outs[2][index] = moment_next, weight_next, average_next

    put(..., (down_mo, down_wo, down_ao), big[:ff, :].astype(F32), down_w, down_m, down_a, rates[4])
    for n in range(2):
        first = (n + 1) * ff
        put(n, (gate_mo, gate_wo, gate_ao), big[first : first + ff, :].astype(F32), gate_w, gate_m, gate_a, rates[3])
    first = 3 * ff
    put(..., (out_mo, out_wo, out_ao), big[first : first + out_w.shape[0], :].astype(F32), out_w, out_m, out_a, rates[2])
    first = first + out_w.shape[0]
    put(..., (value_mo, value_wo, value_ao), small[:narrow, :].astype(F32).T, value_w, value_m, value_a, rates[1])
    put(..., (pair_mo, pair_wo, pair_ao), small[narrow : narrow + pair_cols, :].astype(F32).T, pair_w, pair_m, pair_a, rates[0])
    gain_one = small[narrow + pair_cols : narrow + pair_cols + 16, :].astype(F32)[0:1, :]
    gain_two = big[first : first + 16, :].astype(F32)[0:1, :]
    put(slice(0, 1), (gain_mo, gain_wo, gain_ao), gain_one, gain_w, gain_m, gain_a, rates[5])
    put(slice(1, 2), (gain_mo, gain_wo, gain_ao), gain_two, gain_w, gain_m, gain_a, rates[5])

    mixed_o[...] = (hidden[...] + total[...].astype(F32)).astype(BF16)
    x = tokens[...].astype(F32)
    scale = lax.rsqrt(jnp.mean(x * x, axis=1, keepdims=True) + EPS)
    unit = x * scale
    u = grad_normed[...].astype(F32) * gains[0:1, :]
    input_o[...] = grad_hidden[...] + scale * (u - unit * jnp.mean(u * unit, axis=1, keepdims=True))


def finish(rates, weights, big, small, hidden, total, grad_hidden, grad_normed, tokens, gains):
    length = tokens.shape[0]
    steps = D // 128
    rows = length // steps
    ff = weights[0][0].shape[0]
    narrow, pair_cols = weights[3][0].shape[1], weights[4][0].shape[1]

    def cols(n):
        return pl.BlockSpec((n, 128), lambda i: (0, i))

    def tall(n):
        return pl.BlockSpec((128, n), lambda i: (i, 0))

    token = pl.BlockSpec((rows, D), lambda i: (i, 0))
    specs = [cols(ff), pl.BlockSpec((2, ff, 128), lambda i: (0, 0, i)), cols(weights[2][0].shape[0]), tall(narrow), tall(pair_cols), cols(2)]
    order = [4, 3, 2, 1, 0, 5]
    flat = [a for group in weights for a in group]
    out_shape = [jax.ShapeDtypeStruct((length, D), BF16), jax.ShapeDtypeStruct((length, D), F32)]
    out_specs = [token, token]
    for n in order:
        out_shape += [jax.ShapeDtypeStruct(weights[n][0].shape, F32)] * 3
        out_specs += [specs[n]] * 3
    in_specs = [specs[n] for n in range(6) for _ in range(3)]
    in_specs += [cols(big.shape[0]), cols(small.shape[0])] + [token] * 5 + [pl.BlockSpec((2, D), lambda i: (0, 0))]
    return pl.pallas_call(
        functools.partial(update_kernel, rates),
        grid=(steps,),
        out_shape=out_shape,
        in_specs=in_specs,
        out_specs=out_specs,
        compiler_params=pltpu.CompilerParams(vmem_limit_bytes=50 * 2**20),
        name="finish",
    )(*flat, big, small, hidden, total, grad_hidden, grad_normed, tokens, gains)


def update(weight, grad_total, moment, average, rate):
    moment_next = MOMENTUM * moment + grad_total
    weight_next = weight - rate * (grad_total + MOMENTUM * moment_next)
    average_next = average + (weight_next - average) / STEP
    return (moment_next, weight_next, average_next)


def on_device(
    tokens,
    cotangent,
    doc_starts,
    queries_keys,
    value_weight,
    out_weight,
    gate_up,
    down_weight,
    norm_gains,
    queries_moment,
    value_moment,
    out_moment,
    gate_moment,
    down_moment,
    gains_moment,
    queries_average,
    value_average,
    out_average,
    gate_average,
    down_average,
    gains_average,
):
    total_tokens = float(tokens.shape[0] * lax.axis_size("dp"))
    dp_size = lax.axis_size("dp")
    ff = down_weight.shape[0]
    gate_turned = gate_up.transpose(0, 2, 1)
    normed_one, pairs, values, wide, gate_low, down_low, attn_low, recip, mask = front(
        doc_starts, tokens, norm_gains, queries_keys, value_weight, out_weight, gate_turned, down_weight
    )
    padded, pieces, bits = cube_shape(3 * ff + out_weight.shape[0] + 16, dp_size, 4)
    hidden_one, grad_hidden, grad_numer, grad_numer_turned, grad_denom, ffn_part, big = feed(
        tokens, cotangent, attn_low, recip, wide, gate_low, down_low, norm_gains, padded
    )
    total, big, grad_normed_one, small = back(
        pairs, values, grad_numer, grad_numer_turned, grad_denom, mask, ffn_part, big, normed_one, wide, tokens,
        pieces, bits, dp_size,
    )
    rates = (
        (D * total_tokens) ** (-0.5),
        (D * total_tokens) ** (-0.5),
        (HEADS * HV * total_tokens) ** (-0.5),
        (D * total_tokens) ** (-0.5),
        (FF * total_tokens) ** (-0.5),
        0.2 * total_tokens ** (-0.5),
    )
    weights = (
        (down_weight, down_moment, down_average),
        (gate_turned, gate_moment.transpose(0, 2, 1), gate_average.transpose(0, 2, 1)),
        (out_weight, out_moment, out_average),
        (value_weight, value_moment, value_average),
        (queries_keys, queries_moment, queries_average),
        (norm_gains, gains_moment, gains_average),
    )
    outs = list(finish(rates, weights, big, small, hidden_one, total, grad_hidden, grad_normed_one, tokens, norm_gains))
    outs[11:14] = [o.transpose(0, 2, 1) for o in outs[11:14]]
    return tuple(outs)


def solution(mesh):
    in_specs = (
        P("dp", None),
        P("dp", None),
        P("dp", None),
        P(None, "feat"),
        P(None, "feat"),
        P("feat", None),
        P(None, None, "feat"),
        P("feat", None),
        P(),
        P(None, "feat"),
        P(None, "feat"),
        P("feat", None),
        P(None, None, "feat"),
        P("feat", None),
        P(),
        P(None, "feat"),
        P(None, "feat"),
        P("feat", None),
        P(None, None, "feat"),
        P("feat", None),
        P(),
    )
    out_specs = (
        P("dp", None),
        P("dp", None),
        P(None, "feat"),
        P(None, "feat"),
        P(None, "feat"),
        P(None, "feat"),
        P(None, "feat"),
        P(None, "feat"),
        P("feat", None),
        P("feat", None),
        P("feat", None),
        P(None, None, "feat"),
        P(None, None, "feat"),
        P(None, None, "feat"),
        P("feat", None),
        P("feat", None),
        P("feat", None),
        P(),
        P(),
        P(),
    )
    return jax.shard_map(
        on_device, mesh=mesh, in_specs=in_specs, out_specs=out_specs, check_vma=False
    )
```

time: 297 us -> 254 us (0.86)
  the two profiles are of different devices: /device:TPU:0 before, /device:TPU:11 now
where the time goes in v4:
time: 254 us; the launch traced here: 253 us
  Pallas kernels  249 us (98%)
  local copies, waits for them, and re-layouts  3.33 us (1%)
    pallas_call x1, Pallas kernels, back(): pl.pallas_call(functools.partial(back_kernel, pieces, small_pieces, bits,...  98.1 us
    pallas_call x1, Pallas kernels, feed(): pl.pallas_call(functools.partial(feed_kernel, rows), out_shape=(jax.Shape...  74.9 us
    pallas_call x1, Pallas kernels, front(): pl.pallas_call(functools.partial(front_kernel, bits), out_shape=tuple((ja...  45 us
    pallas_call x1, Pallas kernels, finish(): pl.pallas_call(functools.partial(update_kernel, rates), grid=(steps,), ou...  31 us

profile of v4, /device:TPU:11, one launch (start us, length us, event | category | flops | bytes accessed | tf_op | source)
XLA Modules:
  0.0 253.3 jit_solution(18410728874412628616)
XLA Ops:
  0.7 45.0 %front.1 = (bf16[1024,1024]{1,0:T(8,128)(2,1)}, bf16[1024,512]{1,0:T(8,128)(2,1)}, bf16[1024,1024]{1,0:T(8,128)(2,1)}, bf16[1024,2560]{1,0:T(8,128)(2,1)}, bf16[...) custom-call(s32[1,8]{1,0:T(1,128)} %starts_ref.1, ...), custom_call_target="tpu_custom_call" | custom-call | tf_op jit(solution)/shard_map/front/pallas_call | solution.py:590
  45.7 74.9 %feed.1 = (f32[1024,1024]{1,0:T(8,128)}, f32[1024,1024]{1,0:T(8,128)}, bf16[1024,1024]{1,0:T(8,128)(2,1)}, bf16[1024,1024]{1,0:T(8,128)(2,1)}, bf16[1024,1024]{1...) custom-call(bf16[1024,1024]{1,0:T(8,128)(2,1)} %tokens.1, bf16[1024,1024]{1,0:T(8,128)(2,1)} %cot_in.1, ...), custom_call_target="tpu_custom_call" | custom-call | tf_op jit(solution)/shard_map/feed/pallas_call | solution.py:776
  120.6 0.0 copy-start
  120.6 0.0 copy-start.1
  120.6 0.0 copy-start.5
  120.6 0.0 copy-start.6
  120.6 0.0 copy-start.7
  120.6 98.1 %back.1 = (bf16[1024,1024]{1,0:T(8,128)(2,1)}, bf16[2432,1024]{1,0:T(8,128)(2,1)}, bf16[1024,1024]{1,0:T(8,128)(2,1)}, bf16[512,1024]{1,0:T(8,128)(2,1)}) custom-call(bf16[1024,512]{1,0:T(8,128)(2,1)} %get-tuple-element.60.pairs_in, bf16[1024,1024]{1,0:T(8,128)(2,1)} %get-tuple-element.61.values_in, bf16[1024,1024]{1,0:T(8,128)(2,1)} %get-tuple-element.67.gn_in, ...), custom_call_target="tpu_custom_call" | custom-call | tf_op jit(solution)/shard_map/back/pallas_call | solution.py:994
  218.8 0.0 copy-done
  218.8 0.0 copy-done.1
  218.8 0.0 copy-done.5
  218.8 0.0 copy-done.6
  218.8 0.0 copy-done.7
  218.8 0.0 copy-start.2
  218.8 1.2 copy-done.2
  220.1 0.0 copy-start.3
  220.1 1.0 copy-done.3
  221.1 0.0 copy-start.4
  221.1 1.0 copy-done.4
  222.1 31.0 %finish.1 = (bf16[1024,1024]{1,0:T(8,128)(2,1)}, f32[1024,1024]{1,0:T(8,128)}, f32[1024,128]{1,0:T(8,128)}, f32[1024,128]{1,0:T(8,128)}, f32[1024,128]{1,0:T(8,1...) custom-call(f32[688,1024]{1,0:T(8,128)} %down_w.1, ...), custom_call_target="tpu_custom_call" | custom-call | tf_op jit(solution)/shard_map/finish/pallas_call | solution.py:1081
Async XLA Ops:
  120.6 98.2 %copy-start = (f32[256,1024]{1,0:T(8,128)S(1)}, f32[256,1024]{1,0:T(8,128)}, u32[]{:S(2)}) copy-start(f32[256,1024]{1,0:T(8,128)} %out_w.1) | copy-start | bytes 3145732
  120.6 98.2 %copy-start.1 = (f32[1024,128]{1,0:T(8,128)S(1)}, f32[1024,128]{1,0:T(8,128)}, u32[]{:S(2)}) copy-start(f32[1024,128]{1,0:T(8,128)} %pair_w.1) | copy-start | bytes 1572868
  120.6 98.2 %copy-start.5 = (f32[2,1024]{1,0:T(2,128)S(1)}, f32[2,1024]{1,0:T(2,128)}, u32[]{:S(2)}) copy-start(f32[2,1024]{1,0:T(2,128)} %gains.1) | copy-start | bytes 24580
  120.6 98.2 %copy-start.6 = (f32[2,1024]{1,0:T(2,128)S(1)}, f32[2,1024]{1,0:T(2,128)}, u32[]{:S(2)}) copy-start(f32[2,1024]{1,0:T(2,128)} %gain_m.1) | copy-start | bytes 24580
  120.6 98.2 %copy-start.7 = (f32[2,1024]{1,0:T(2,128)S(1)}, f32[2,1024]{1,0:T(2,128)}, u32[]{:S(2)}) copy-start(f32[2,1024]{1,0:T(2,128)} %gain_a.1) | copy-start | bytes 24580
  218.8 1.2 copy-start.2
  220.1 1.0 copy-start.3
  221.1 1.0 copy-start.4
